TPU v7x, 256 devices: a whole 4x4x8 slice. The times are simulated.
256 devices in a mesh: group: 4 (over x_hi, core), fsdp: 64 (over z, y, x_lo).
Axes of the slice: x: 4 (x_hi: 2, x_lo: 2; x = x_hi * 2 + x_lo), y: 4, z: 8, core: 2. Of those that a mesh axis runs over, the one named last changes fastest.
Arguments:
- tokens: bfloat16 [4, 16384, 2048], P('group', 'fsdp'), may hold values from -16 to 16
- targets: bfloat16 [4, 16384, 1024], P('group', 'fsdp'), may hold values from -6 to 6
- lengths: int32 [4, 64], P('group'), may hold values from 128 to 256, as said below
- outer_param: float32 [2048, 1024], P('fsdp', 'group'), may hold values from -6 to 6
- outer_mom: float32 [2048, 1024], P('fsdp', 'group'), may hold values from -0.75 to 0.75
- first_mom: float32 [4, 2048, 1024], P('group', 'fsdp'), may hold values from -0.0014648438 to 0.0014648438
- second_mom: float32 [4, 2048, 1024], P('group', 'fsdp'), may hold values from 5e-09 to 5e-08
Outputs:
- new_param: float32 [2048, 1024], P('fsdp', 'group')
- new_mom: float32 [2048, 1024], P('fsdp', 'group')
- new_first: float32 [4, 2048, 1024], P('group', 'fsdp')
- new_second: float32 [4, 2048, 1024], P('group', 'fsdp')
Inputs may be any that keep to these rules, and one draw needn't show every extreme that they name: `lengths`: every entry is a multiple of 128, and some entry equals 256.
All inputs are finite; a program needn't handle non-finite values.
Results may differ from a plain program's by a relative error of at most 0.0075.
Values may be sent and summed in bfloat16 or wider, within the bound.
No kernel may reach another device: no remote copies, remote signals or barrier semaphores. Data moves between devices by JAX's collectives and lax.ppermute only.
A program may use at most 64 MiB of HBM per device.

v0:
```python
import jax
import jax.numpy as jnp
from jax import lax
from jax.sharding import PartitionSpec as P

D = 2048
STEPS = 2
PRIOR = 1000


def adam_update(param, first, second, grad, step):
    first = 0.9 * first + 0.1 * grad
    second = 0.95 * second + 0.05 * grad * grad
    upd = first / (1.0 - 0.9**step) / (jnp.sqrt(second / (1.0 - 0.95**step)) + 1e-08)
    return (param - 0.1 * (upd + 0.1 * param), first, second)


def transpose_product(left, right):
    return lax.dot_general(
        left, right, (((0,), (0,)), ((), ())), preferred_element_type=jnp.float32
    )


def gradient(inputs, goal, length, count, shard_bf):
    factor = D ** (-0.5)
    coef = factor / count
    width = shard_bf.shape[1]
    empty = jnp.zeros((inputs.shape[0], width), jnp.float32)
    piece = lax.all_gather(shard_bf, "fsdp", axis=0, tiled=True)
    columns = lax.slice_in_dim(inputs, 0, piece.shape[0], axis=1)
    outputs = (empty + jnp.dot(columns, piece, preferred_element_type=jnp.float32)) * factor
    valid = (lax.iota(jnp.int32, inputs.shape[0]) < length).astype(jnp.float32)[:, None]
    resid = (valid * (outputs - goal.astype(jnp.float32))).astype(jnp.bfloat16)
    columns = lax.slice_in_dim(inputs, 0, shard_bf.shape[0] * lax.axis_size("fsdp"), axis=1)
    return lax.psum_scatter(
        transpose_product(columns, resid) * coef, "fsdp", scatter_dimension=0, tiled=True
    )


def per_device(tokens, targets, lengths, outer_param, outer_mom, first_mom, second_mom):
    inputs = tokens[0]
    goal = targets[0]
    own_lengths = lengths[0]
    length = lax.dynamic_index_in_dim(own_lengths, lax.axis_index("fsdp"), 0, keepdims=False)
    count = jnp.sum(own_lengths).astype(jnp.float32)
    start_param = lax.all_gather(outer_param, "group", axis=1, tiled=True)
    param = start_param
    first = first_mom[0]
    second = second_mom[0]
    for step in range(STEPS):
        grad = gradient(inputs, goal, length, count, param.astype(jnp.bfloat16))
        param, first, second = adam_update(param, first, second, grad, PRIOR + step + 1)
    change = start_param - param
    groups = lax.axis_size("group")
    pseudo = (
        lax.psum_scatter(
            change.astype(jnp.bfloat16), "group", scatter_dimension=1, tiled=True
        ).astype(jnp.float32)
        / groups
    )
    new_mom = 0.9 * outer_mom + pseudo
    new_param = outer_param - 0.7 * (pseudo + 0.9 * new_mom)
    return (new_param, new_mom, first[None], second[None])


def solution(mesh):
    in_specs = (
        P("group", "fsdp", None),
        P("group", "fsdp", None),
        P("group", None),
        P("fsdp", "group"),
        P("fsdp", "group"),
        P("group", "fsdp", None),
        P("group", "fsdp", None),
    )
    out_specs = (
        P("fsdp", "group"),
        P("fsdp", "group"),
        P("group", "fsdp", None),
        P("group", "fsdp", None),
    )
    return jax.shard_map(
        per_device, mesh=mesh, in_specs=in_specs, out_specs=out_specs, check_vma=False
    )
```

profile of v0, /device:TPU:1, one launch (start us, length us, event | category | flops | bytes accessed | tf_op | source)
XLA Modules:
  0.0 1359.3 jit_solution(13857486780279179594)
XLA Ops:
  7.2 0.0 copy-start
  7.2 0.0 all-gather.3.cloned.1.call-start
  7.2 10.3 all_gather.9
  17.6 0.6 convert_element_type.37
  18.2 0.0 all-gather.3.cloned.1.call-update
  18.2 0.0 reduce-scatter.10.cloned.1.call-start
  18.3 1.3 reduce_sum.9
  20.2 1.2 constant_dynamic-slice_fusion
  21.5 0.7 compare_convert_fusion
  22.2 259.4 %all-gather.3.cloned.1.call-done = bf16[2048,1024]{1,0:T(8,128)(2,1)} async-done(((bf16[32,1024]{1,0:T(8,128)(2,1)}), bf16[2048,1024]{1,0:T(8,128)(2,1)}) %all-gather.3.cloned.1.call-update) | async-done | bytes 4194320 | tf_op jit(solution)/shard_map/all_gather | solution.py:29
  281.5 0.0 copy-done
  281.5 7.9 multiply_bitcast_fusion.1
  289.5 9.2 copy.26
  298.7 0.0 copy-start.2
  298.7 0.0 copy-start.3
  298.7 0.0 copy-start.1
  298.7 0.0 reduce-scatter.10.cloned.1.call-update
  298.7 0.0 all-gather.5.cloned.1.call-start
  298.8 326.1 %reduce-scatter.10.cloned.1.call-done = f32[32,1024]{1,0:T(8,128)} async-done(((f32[2048,1024]{1,0:T(8,128)}), f32[32,1024]{1,0:T(8,128)}) %reduce-scatter.10.cloned.1.call-update) | async-done | bytes 131088 | tf_op jit(solution)/shard_map/reduce_scatter | solution.py:35
  624.9 0.0 copy-done.2
  624.9 0.0 copy-done.3
  624.9 1.6 fusion.19
  626.5 0.0 all-gather.5.cloned.1.call-update
  626.6 0.0 reduce-scatter.12.cloned.1.call-start
  626.6 305.4 %all-gather.5.cloned.1.call-done = bf16[2048,1024]{1,0:T(8,128)(2,1)} async-done(((bf16[32,1024]{1,0:T(8,128)(2,1)}), bf16[2048,1024]{1,0:T(8,128)(2,1)}) %all-gather.5.cloned.1.call-update) | async-done | bytes 4194320 | tf_op jit(solution)/shard_map/all_gather | solution.py:29
  932.0 0.0 copy-done.1
  932.0 7.8 multiply_bitcast_fusion
  939.9 9.2 copy.28
  949.1 0.0 copy-start.4
  949.1 0.0 copy-start.5
  949.1 0.0 copy-start.6
  949.1 0.0 reduce-scatter.12.cloned.1.call-update
  949.1 0.0 reduce-scatter.8.cloned.1.call-start
  949.2 325.7 %reduce-scatter.12.cloned.1.call-done = f32[32,1024]{1,0:T(8,128)} async-done(((f32[2048,1024]{1,0:T(8,128)}), f32[32,1024]{1,0:T(8,128)}) %reduce-scatter.12.cloned.1.call-update) | async-done | bytes 131088 | tf_op jit(solution)/shard_map/reduce_scatter | solution.py:35
  1274.9 0.0 copy-done.4
  1274.9 1.8 fusion.18
  1276.7 0.0 reduce-scatter.8.cloned.1.call-update
  1276.7 74.8 %reduce-scatter.8.cloned.1.call-done = bf16[32,256]{1,0:T(8,128)(2,1)} async-done(((bf16[32,1024]{1,0:T(8,128)(2,1)}), bf16[32,256]{1,0:T(8,128)(2,1)}) %reduce-scatter.8.cloned.1.call-update) | async-done | bytes 16400 | tf_op jit(solution)/shard_map/reduce_scatter | solution.py:56
  1351.5 0.0 copy-done.5
  1351.5 0.0 copy-done.6
  1351.5 1.4 multiply_subtract_fusion.1
Async XLA Ops:
  7.2 274.4 %copy-start = (bf16[1,256,2048]{2,1,0:T(8,128)(2,1)S(1)}, bf16[1,256,2048]{2,1,0:T(8,128)(2,1)}, u32[]{:S(2)}) copy-start(bf16[1,256,2048]{2,1,0:T(8,128)(2,1)} %param.7) | copy-start | bytes 3145732
  7.2 274.4 %all-gather.3.cloned.1.call-start = ((), (), s32[]{:S(2)}) async-start(), calls=%async_computation.3 | async-start | bytes 4259840 | tf_op jit(solution)/shard_map/all_gather | solution.py:29
  18.2 606.7 %reduce-scatter.10.cloned.1.call-start = ((), (), s32[]{:S(2)}) async-start(), calls=%async_computation.6 | async-start | bytes 8519680 | tf_op jit(solution)/shard_map/reduce_scatter | solution.py:35
  298.7 326.2 %copy-start.2 = (f32[1,32,1024]{2,1,0:T(8,128)S(1)}, f32[1,32,1024]{2,1,0:T(8,128)}, u32[]{:S(2)}) copy-start(f32[1,32,1024]{2,1,0:T(8,128)} %param.12) | copy-start | bytes 393220
  298.7 326.2 %copy-start.3 = (f32[1,32,1024]{2,1,0:T(8,128)S(1)}, f32[1,32,1024]{2,1,0:T(8,128)}, u32[]{:S(2)}) copy-start(f32[1,32,1024]{2,1,0:T(8,128)} %param.13) | copy-start | bytes 393220
  298.7 633.3 %copy-start.1 = (bf16[1,256,1024]{2,1,0:T(8,128)(2,1)S(1)}, bf16[1,256,1024]{2,1,0:T(8,128)(2,1)}, u32[]{:S(2)}) copy-start(bf16[1,256,1024]{2,1,0:T(8,128)(2,1)} %param.8) | copy-start | bytes 1572868
  298.7 633.3 %all-gather.5.cloned.1.call-start = ((), (), s32[]{:S(2)}) async-start(), calls=%async_computation.4 | async-start | bytes 4259840 | tf_op jit(solution)/shard_map/all_gather | solution.py:29
  626.6 648.3 %reduce-scatter.12.cloned.1.call-start = ((), (), s32[]{:S(2)}) async-start(), calls=%async_computation.7 | async-start | bytes 8519680 | tf_op jit(solution)/shard_map/reduce_scatter | solution.py:35
  949.1 325.8 %copy-start.4 = (f32[32,1024]{1,0:T(8,128)S(1)}, f32[32,1024]{1,0:T(8,128)}, u32[]{:S(2)}) copy-start(f32[32,1024]{1,0:T(8,128)} %reduce-scatter.10.cloned.1.call-done) | copy-start | bytes 393220
  949.1 402.4 %copy-start.5 = (f32[32,256]{1,0:T(8,128)S(1)}, f32[32,256]{1,0:T(8,128)}, u32[]{:S(2)}) copy-start(f32[32,256]{1,0:T(8,128)} %param.10) | copy-start | bytes 98308
  949.1 402.4 %copy-start.6 = (f32[32,256]{1,0:T(8,128)S(1)}, f32[32,256]{1,0:T(8,128)}, u32[]{:S(2)}) copy-start(f32[32,256]{1,0:T(8,128)} %param.11) | copy-start | bytes 98308
  949.1 402.3 %reduce-scatter.8.cloned.1.call-start = ((), (), s32[]{:S(2)}) async-start(), calls=%async_computation.5 | async-start | bytes 81920 | tf_op jit(solution)/shard_map/reduce_scatter | solution.py:56
Sparse Core Ops, SparseCore 0:
  18.4 263.1 all-gather.2
  298.9 325.9 reduce-scatter.9
  627.3 304.7 all-gather.4
  949.2 325.5 reduce-scatter.11
  1277.4 74.0 reduce-scatter.7
where the time goes:
time: 1360 us
  waiting for transfers between devices  1290 us (95%)
  local copies, waits for them, and re-layouts  19.7 us (1%)
  matrix products  15.8 us (1%)
  between operations  14.5 us (1%)
    reduce_scatter x2, waiting for transfers between devices, gradient(): lax.psum_scatter(transpose_product(columns, resid) * coef, 'fsdp', scatte...  652 us
    all_gather x2, waiting for transfers between devices, gradient(): piece = lax.all_gather(shard_bf, 'fsdp', axis=0, tiled=True)  565 us
    reduce_scatter x1, waiting for transfers between devices, per_device(): lax.psum_scatter(change.astype(jnp.bfloat16), 'group', scatter_dimension=...  74.8 us
  transfers between devices with their start and end apart: 5, of which 5 were waited for; matrix products, arithmetic and copies ran while one was open for 0% of the time, Pallas kernels for 0%

commit v1 on v0

v1 whole, which is shorter than its diff:
```python
import jax
import jax.numpy as jnp
from jax import lax
from jax.sharding import Mesh
from jax.sharding import PartitionSpec as P

D = 2048
STEPS = 2
PRIOR = 1000
BLOCK = 128
TURN = [(0, 0), (1, 2), (2, 1), (3, 3)]


def adam_moments(first, second, grad):
    return 0.9 * first + 0.1 * grad, 0.95 * second + 0.05 * grad * grad


def adam_update(param, first, second, step):
    upd = first / (1.0 - 0.9**step) / (jnp.sqrt(second / (1.0 - 0.95**step)) + 1e-08)
    return param - 0.1 * (upd + 0.1 * param)


def shift(x, axis, by):
    size = lax.axis_size(axis)
    return lax.ppermute(x, axis, [(i, (i + by) % size) for i in range(size)])


def other_core(x):
    return shift(x, "c", 1)


def exchange(x, axes):
    return lax.all_to_all(x, axes, 0, 0, tiled=True)


def pick(x, index, axis):
    return lax.dynamic_index_in_dim(x, index, axis, keepdims=False)


def turned(x):
    return lax.ppermute(x, ("c", "x"), TURN)


def spread_rows(x):
    own = turned(x)
    half = own.shape[0] // 2
    above = shift(own, ("yh", "yl"), -1)
    below = shift(own, ("yh", "yl"), 1)
    far = jnp.concatenate(
        [shift(above[:half], ("yh", "yl"), -1), shift(below[half:], ("yh", "yl"), 1)], 0
    )
    return [(0, own), (1, above), (3, below), (2, far)]


def per_device(tokens, targets, lengths, outer_param, outer_mom, first_mom, second_mom):
    c, x = lax.axis_index("c"), lax.axis_index("x")
    z, h = lax.axis_index("z"), lax.axis_index("h")
    y, yh = lax.axis_index(("yh", "yl")), lax.axis_index("yh")
    rows = tokens.shape[1]
    factor = D ** (-0.5)

    sizes = turned(lengths[0])
    coef = factor / jnp.sum(sizes).astype(jnp.float32)
    goals = lax.all_to_all(turned(targets[0]), ("yh", "c", "yl"), 1, 0, tiled=True)
    goals = goals.reshape(2, 2, 2, rows, BLOCK)
    blocks, wanted, valid = [], [], []
    for away, block in spread_rows(tokens[0]):
        for core, part in ((c, block), (1 - c, other_core(block))):
            at = (y + away) % 4
            blocks.append(part)
            goal = pick(pick(pick(goals, at // 2, 0), core, 0), at % 2, 0)
            wanted.append(goal)
            limit = pick(sizes, (z * 4 + at) * 2 + core, 0)
            valid.append((lax.iota(jnp.int32, rows) < limit).astype(jnp.float32))
    inputs = jnp.concatenate(blocks, 0)
    goal = jnp.concatenate(wanted, 0)
    valid = jnp.concatenate(valid, 0)[:, None]

    param = jnp.moveaxis(outer_param.reshape(32, 2, BLOCK), 1, 0)
    param = jnp.broadcast_to(param[None, None, :, None], (2, 2, 2, 2, 32, BLOCK))
    param = exchange(param.reshape(16, 32, BLOCK), ("h", "yh", "yl", "x"))
    param = pick(param.reshape(2, 256, BLOCK), yh, 0)
    moments = jnp.stack([first_mom[0], second_mom[0]]).reshape(2, 32, 2, 2, 2, BLOCK)
    moments = moments.transpose(3, 2, 4, 0, 1, 5)[:, :, :, None]
    moments = jnp.broadcast_to(moments, (2, 2, 2, 2, 2, 32, BLOCK))
    moments = exchange(moments.reshape(16, 2, 32, BLOCK), ("c", "yh", "yl", "x"))
    moments = pick(moments.reshape(2, 8, 2, 32, BLOCK), x, 0)
    first = moments[:, 0].reshape(256, BLOCK)
    second = moments[:, 1].reshape(256, BLOCK)

    start = param
    home_first, home_second = first_mom[0], second_mom[0]
    for step in range(STEPS):
        weights = jnp.broadcast_to(param.astype(jnp.bfloat16)[None], (8, 256, BLOCK))
        weights = exchange(weights, "z").reshape(D, BLOCK)
        outputs = jnp.dot(inputs, weights, preferred_element_type=jnp.float32) * factor
        resid = (valid * (outputs - goal.astype(jnp.float32))).astype(jnp.bfloat16)
        grad = lax.dot_general(
            inputs, resid, (((0,), (0,)), ((), ())), preferred_element_type=jnp.float32
        )
        grad = exchange(grad.astype(jnp.bfloat16).reshape(8, 256, BLOCK), "z")
        grad = jnp.sum(grad.astype(jnp.float32), 0) * coef
        first, second = adam_moments(first, second, grad)
        param = adam_update(param, first, second, PRIOR + step + 1)

        home = grad.astype(jnp.bfloat16).reshape(1, 8, 32, BLOCK)
        home = jnp.broadcast_to(home, (2, 8, 32, BLOCK)).reshape(16, 32, BLOCK)
        home = exchange(home, ("c", "yh", "yl", "x"))
        home = pick(home.reshape(2, 2, 2, 2, 32, BLOCK), c, 3)
        home = home.transpose(3, 1, 0, 2, 4).reshape(32, 8 * BLOCK)
        home_first, home_second = adam_moments(
            home_first, home_second, home.astype(jnp.float32)
        )

    change = (start - param).astype(jnp.bfloat16).reshape(1, 8, 32, BLOCK)
    change = jnp.broadcast_to(change, (2, 8, 32, BLOCK)).reshape(16, 32, BLOCK)
    change = exchange(change, ("h", "yh", "yl", "x")).reshape(2, 2, 2, 2, 32, BLOCK)
    change = jnp.sum(pick(change, h, 1).astype(jnp.float32), (0, 2))
    pseudo = jnp.moveaxis(change, 0, 1).reshape(32, 2 * BLOCK) / 4
    new_mom = 0.9 * outer_mom + pseudo
    new_param = outer_param - 0.7 * (pseudo + 0.9 * new_mom)
    return (new_param, new_mom, home_first[None], home_second[None])


def solution(mesh):
    fine = Mesh(
        mesh.devices.reshape(2, 2, 8, 2, 2, 2), ("h", "c", "z", "yh", "yl", "x")
    )
    group, fsdp = ("h", "c"), ("z", "yh", "yl", "x")
    in_specs = (
        P(group, fsdp, None),
        P(group, fsdp, None),
        P(group, None),
        P(fsdp, group),
        P(fsdp, group),
        P(group, fsdp, None),
        P(group, fsdp, None),
    )
    out_specs = (
        P(fsdp, group),
        P(fsdp, group),
        P(group, fsdp, None),
        P(group, fsdp, None),
    )
    return jax.shard_map(
        per_device, mesh=fine, in_specs=in_specs, out_specs=out_specs, check_vma=False
    )
```

time: 1360 us -> 232 us (0.17)
  waiting for transfers between devices: 1290 us -> 80.4 us
  starting transfers between devices: 0.21 us -> 68 us
    reduce_scatter x3 -> x0, waiting for transfers between devices: 727 us -> none  [the longest x2 652 us: gradient(): lax.psum_scatter(transpose_product(columns, resid) * coef, 'fsdp', scatte...]
    all_gather x2 -> x0, waiting for transfers between devices: 565 us -> none  [gradient(): piece = lax.all_gather(shard_bf, 'fsdp', axis=0, tiled=True)]
    all_to_all x0 -> x9, waiting for transfers between devices: none -> 53.7 us  [the longest x8 52 us: exchange(): return lax.all_to_all(x, axes, 0, 0, tiled=True)]
    all_to_all x0 -> x9, starting transfers between devices: none -> 50.3 us  [the longest x8 46 us: exchange(): return lax.all_to_all(x, axes, 0, 0, tiled=True)]
    ppermute x0 -> x11, waiting for transfers between devices: none -> 26.7 us  [the longest x8 15.6 us: shift(): return lax.ppermute(x, axis, [(i, (i + by) % size) for i in range(size)])]
    all_to_all x0 -> x1, blocking collectives: none -> 20.2 us  [exchange(): return lax.all_to_all(x, axes, 0, 0, tiled=True)]
    ppermute x0 -> x11, starting transfers between devices: none -> 17.7 us  [the longest x3 9.95 us: turned(): return lax.ppermute(x, ('c', 'x'), TURN)]
  transfers between devices with their start and end apart: 5 -> 20, of which waited for: 5 -> 10; matrix products, arithmetic and copies ran while one was open for 0% -> 18% of each run, Pallas kernels for 0% -> 0%
where the time goes in v1:
time: 232 us; the launch traced here: 231 us
  waiting for transfers between devices  80.4 us (35%)
  starting transfers between devices  68 us (29%)
  local copies, waits for them, and re-layouts  26.2 us (11%)
  matrix products  24.8 us (11%)
  blocking collectives  20.2 us (9%)
  other arithmetic  8.92 us (4%)
    all_to_all x8, waiting for transfers between devices, exchange(): return lax.all_to_all(x, axes, 0, 0, tiled=True)  52 us
    all_to_all x8, starting transfers between devices, exchange(): return lax.all_to_all(x, axes, 0, 0, tiled=True)  46 us
    all_to_all x1, blocking collectives, exchange(): return lax.all_to_all(x, axes, 0, 0, tiled=True)  20.2 us
    unnamed x30, local copies, waits for them, and re-layouts  16.4 us
    ppermute x8, waiting for transfers between devices, shift(): return lax.ppermute(x, axis, [(i, (i + by) % size) for i in range(size)])  15.6 us
    dot_general x2, matrix products, per_device(): lax.dot_general(inputs, resid, (((0,), (0,)), ((), ())), preferred_elemen...  13.3 us
    dot_general x2, matrix products, per_device(): jnp.dot(inputs, weights, preferred_element_type=jnp.float32) * factor  11.6 us
    ppermute x3, waiting for transfers between devices, turned(): return lax.ppermute(x, ('c', 'x'), TURN)  11.1 us
  transfers between devices with their start and end apart: 20, of which 10 were waited for; matrix products, arithmetic and copies ran while one was open for 18% of the time, Pallas kernels for 0%

profile of v1, /device:TPU:1, one launch (start us, length us, event | category | flops | bytes accessed | tf_op | source)
XLA Modules:
  0.0 230.6 jit_solution(1988332044417103284)
XLA Ops:
  0.6 0.8 reshape.292
  1.4 0.7 broadcast_in_dim.18
  2.2 7.6 %all-to-all-start = ((f32[16,32,128]{2,1,0:T(8,128)}), f32[16,32,128]{2,1,0:T(8,128)S(1)}, u32[]{:S(2)}, u32[]{:S(2)}) async-start(f32[16,32,128]{2,1,0:T(8,128)} %bitcast.1), calls=%async_computation | async-start | bytes 524288 | tf_op jit(solution)/shard_map/all_to_all | solution.py:33
  9.7 4.4 %collective-permute-start = (bf16[256,2048]{1,0:T(8,128)(2,1)}, bf16[256,2048]{1,0:T(8,128)(2,1)}, u32[]{:S(2)}, u32[]{:S(2)}) collective-permute-start(bf16[256,2048]{1,0:T(8,128)(2,1)} %bitcast.145), channel_id=1, source_target_pairs={{0,0},{1,64},{64,1},{65,65},{2,2},{3,66},{66,3},{67,67},{4,4},{5,6... | collective-permute-start | bytes 3145736 | tf_op jit(solution)/shard_map/ppermute | solution.py:41
  14.1 1.9 collective-permute-start.10
  16.1 3.6 %collective-permute-start.9 = (s32[64]{0:T(128)}, s32[64]{0:T(128)S(1)}, u32[]{:S(2)}, u32[]{:S(2)}) collective-permute-start(s32[64]{0:T(128)} %bitcast.147), channel_id=1, source_target_pairs={{0,0},{1,64},{64,1},{65,65},{2,2},{3,66},{66,3},{67,67},{4,4},{5,6... | collective-permute-start | bytes 776 | tf_op jit(solution)/shard_map/ppermute | solution.py:41
  20.0 1.0 pad_maximum_fusion.1
  21.4 11.1 %collective-permute-done.9 = s32[64]{0:T(128)S(1)} collective-permute-done((s32[64]{0:T(128)}, s32[64]{0:T(128)S(1)}, u32[]{:S(2)}, u32[]{:S(2)}) %collective-permute-start.9) | collective-permute-done | bytes 288 | tf_op jit(solution)/shard_map/ppermute | solution.py:41
  35.8 0.9 copy_bitcast_fusion
  36.7 4.4 %all-to-all-start.3 = ((bf16[256,8,128]{2,0,1:T(8,128)(2,1)}), bf16[256,8,128]{2,0,1:T(8,128)(2,1)S(1)}, u32[]{:S(2)}, u32[]{:S(2)}) async-start(bf16[256,8,128]{2,0,1:T(8,128)(2,1)} %copy_bitcast_fusion), calls=%async_computation.3 | async-start | bytes 1048576 | tf_op jit(solution)/shard_map/all_to_all | solution.py:64
  42.4 2.7 %collective-permute-start.2 = (bf16[256,2048]{1,0:T(8,128)(2,1)}, bf16[256,2048]{1,0:T(8,128)(2,1)S(1)}, u32[]{:S(2)}, u32[]{:S(2)}) collective-permute-start(bf16[256,2048]{1,0:T(8,128)(2,1)} %collective-permute-done), channel_id=1, source_target_pairs={{0,6},{2,0},{4,2},{6,4},{1,7},{3,1},{5,3},{7,5},{8,14},{10,8},{12,... | collective-permute-start | bytes 3145736 | tf_op jit(solution)/shard_map/ppermute | solution.py:25
  48.2 0.7 collective-permute-start.1
  48.9 1.7 all-to-all-done.3
  50.6 0.9 broadcast_in_dim.21
  51.4 8.2 %all-to-all-start.2 = ((bf16[8,256,128]{2,1,0:T(8,128)(2,1)}), bf16[8,256,128]{2,1,0:T(8,128)(2,1)S(1)}, u32[]{:S(2)}, u32[]{:S(2)}) async-start(bf16[8,256,128]{2,1,0:T(8,128)(2,1)} %broadcast_in_dim.21), calls=%async_computation.2 | async-start | bytes 1048576 | tf_op jit(solution)/shard_map/all_to_all | solution.py:33
  64.0 7.6 %collective-permute-done.2 = bf16[256,2048]{1,0:T(8,128)(2,1)S(1)} collective-permute-done((bf16[256,2048]{1,0:T(8,128)(2,1)}, bf16[256,2048]{1,0:T(8,128)(2,1)S(1)}, u32[]{:S(2)}, u32[]{:S(2)}) %collective-permute-start.2) | collective-permute-done | bytes 1048608 | tf_op jit(solution)/shard_map/ppermute | solution.py:25
  71.5 0.9 collective-permute-start.3
  73.1 1.4 collective-permute-start.6
  74.8 2.3 %constant_dynamic-update-slice_fusion.8 = bf16[2048,2048]{1,0:T(8,128)(2,1)} fusion(bf16[256,2048]{1,0:T(8,128)(2,1)} %collective-permute-done), kind=kLoop, calls=%fused_computation.71 | loop fusion | bytes 2097152
  77.7 2.3 constant_dynamic-update-slice_fusion.7
  79.9 1.1 constant_dynamic-update-slice_fusion.6
  81.0 5.7 %collective-permute-done.6 = bf16[128,2048]{1,0:T(8,128)(2,1)S(1)} collective-permute-done((bf16[128,2048]{1,0:T(8,128)(2,1)S(1)}, bf16[128,2048]{1,0:T(8,128)(2,1)S(1)}, u32[]{:S(2)}, u32[]{:S(2)}) %collective-permute-start.6) | collective-permute-done | bytes 524320 | tf_op jit(solution)/shard_map/ppermute | solution.py:25
  86.7 2.3 %collective-permute-done.7 = bf16[128,2048]{1,0:T(8,128)(2,1)S(1)} collective-permute-done((bf16[128,2048]{1,0:T(8,128)(2,1)S(1)}, bf16[128,2048]{1,0:T(8,128)(2,1)S(1)}, u32[]{:S(2)}, u32[]{:S(2)}) %collective-permute-start.7) | collective-permute-done | bytes 524320 | tf_op jit(solution)/shard_map/ppermute | solution.py:25
  89.1 1.2 collective-permute-start.8
  90.3 1.1 constant_dynamic-update-slice_fusion.5
  91.4 1.1 constant_dynamic-update-slice_fusion.4
  92.5 1.1 constant_dynamic-update-slice_fusion.3
  93.6 0.9 constant_dynamic-update-slice_fusion.2
  94.4 0.8 constant_dynamic-update-slice_fusion.1
  95.2 1.1 constant_dynamic-update-slice_fusion
  96.4 0.9 broadcast_in_dim.19
  97.3 3.6 %all-to-all-start.1 = ((f32[16,2,32,128]{3,2,1,0:T(8,128)}), f32[16,2,32,128]{3,2,1,0:T(8,128)S(1)}, u32[]{:S(2)}, u32[]{:S(2)}) async-start(f32[16,2,32,128]{3,2,1,0:T(8,128)} %bitcast.5), calls=%async_computation.1 | async-start | bytes 1048576 | tf_op jit(solution)/shard_map/all_to_all | solution.py:33
  101.0 5.8 %fusion.5 = bf16[2048,128]{1,0:T(8,128)(2,1)S(1)} fusion(bf16[2048,2048]{1,0:T(8,128)(2,1)} %constant_dynamic-update-slice_fusion, bf16[2048,128]{1,0:T(8,128)(2,1)S(1)} %bitcast.138, bf16[2048,128]{1,0:T(8,128)(2,1)} %bitcast_dynamic-update-slice_fusion, f32[2048]{0:T(1024)S(1)} %concatenate.19), kind=kOutput, calls=%fused_computation.9 | convolution fusion | flops 1075052544 | bytes 9969664 | tf_op jit(solution)/shard_map/dot_general | solution.py:96
  106.8 6.6 %convolution_convert_fusion.1 = bf16[2048,128]{1,0:T(8,128)(2,1)} fusion(bf16[2048,2048]{1,0:T(8,128)(2,1)} %constant_dynamic-update-slice_fusion, bf16[2048,128]{1,0:T(8,128)(2,1)S(1)} %fusion.5), kind=kOutput, calls=%fused_computation.7 | convolution fusion | flops 1074003968 | bytes 9437184 | tf_op jit(solution)/shard_map/dot_general | solution.py:98
  113.3 8.2 %all-to-all-start.4 = ((bf16[8,256,128]{2,1,0:T(8,128)(2,1)}), bf16[8,256,128]{2,1,0:T(8,128)(2,1)S(1)}, u32[]{:S(2)}, u32[]{:S(2)}) async-start(bf16[8,256,128]{2,1,0:T(8,128)(2,1)} %bitcast.33), calls=%async_computation.4 | async-start | bytes 1048576 | tf_op jit(solution)/shard_map/all_to_all | solution.py:33
  122.9 16.6 %all-to-all-done.4 = bf16[8,256,128]{2,1,0:T(8,128)(2,1)S(1)} async-done(((bf16[8,256,128]{2,1,0:T(8,128)(2,1)}), bf16[8,256,128]{2,1,0:T(8,128)(2,1)S(1)}, u32[]{:S(2)}, u32[]{:S(2)}) %all-to-all-start.4) | async-done | bytes 524320 | tf_op jit(solution)/shard_map/all_to_all | solution.py:33
  139.8 20.2 %all_to_all.61 = bf16[8,256,128]{2,1,0:T(8,128)(2,1)S(1)} all-to-all(bf16[8,256,128]{2,1,0:T(8,128)(2,1)S(1)} %broadcast_in_dim.23), channel_id=1, replica_groups=mesh['h'=2,'c'=2,'z'=8,'yh'=2,'yl'=2,'x'=2] {'z'}, dimensions={0} | all-to-all | bytes 1048576 | tf_op jit(solution)/shard_map/all_to_all | solution.py:33
  160.0 5.8 %fusion.4 = bf16[2048,128]{1,0:T(8,128)(2,1)S(1)} fusion(bf16[2048,2048]{1,0:T(8,128)(2,1)} %constant_dynamic-update-slice_fusion, bf16[2048,128]{1,0:T(8,128)(2,1)S(1)} %bitcast.139, bf16[2048,128]{1,0:T(8,128)(2,1)} %bitcast_dynamic-update-slice_fusion, f32[2048]{0:T(1024)S(1)} %concatenate.19), kind=kOutput, calls=%fused_computation.8 | convolution fusion | flops 1075052544 | bytes 9969664 | tf_op jit(solution)/shard_map/dot_general | solution.py:96
  165.8 6.7 %convolution_convert_fusion = bf16[2048,128]{1,0:T(8,128)(2,1)} fusion(bf16[2048,2048]{1,0:T(8,128)(2,1)} %constant_dynamic-update-slice_fusion, bf16[2048,128]{1,0:T(8,128)(2,1)S(1)} %fusion.4), kind=kOutput, calls=%fused_computation.6 | convolution fusion | flops 1074003968 | bytes 9437184 | tf_op jit(solution)/shard_map/dot_general | solution.py:98
  172.5 3.5 %all-to-all-start.6 = ((bf16[8,256,128]{2,1,0:T(8,128)(2,1)}), bf16[8,256,128]{2,1,0:T(8,128)(2,1)S(1)}, u32[]{:S(2)}, u32[]{:S(2)}) async-start(bf16[8,256,128]{2,1,0:T(8,128)(2,1)} %bitcast.41), calls=%async_computation.6 | async-start | bytes 1048576 | tf_op jit(solution)/shard_map/all_to_all | solution.py:33
  176.0 17.8 %all-to-all-done.6 = bf16[8,256,128]{2,1,0:T(8,128)(2,1)S(1)} async-done(((bf16[8,256,128]{2,1,0:T(8,128)(2,1)}), bf16[8,256,128]{2,1,0:T(8,128)(2,1)S(1)}, u32[]{:S(2)}, u32[]{:S(2)}) %all-to-all-start.6) | async-done | bytes 524320 | tf_op jit(solution)/shard_map/all_to_all | solution.py:33
  194.6 5.7 %all-to-all-start.8 = ((bf16[16,32,128]{2,1,0:T(8,128)(2,1)}), bf16[16,32,128]{2,1,0:T(8,128)(2,1)S(1)}, u32[]{:S(2)}, u32[]{:S(2)}) async-start(bf16[16,32,128]{2,1,0:T(8,128)(2,1)} %bitcast.46), calls=%async_computation.8 | async-start | bytes 262144 | tf_op jit(solution)/shard_map/all_to_all | solution.py:33
  200.3 5.7 %all-to-all-done.8 = bf16[16,32,128]{2,1,0:T(8,128)(2,1)S(1)} async-done(((bf16[16,32,128]{2,1,0:T(8,128)(2,1)}), bf16[16,32,128]{2,1,0:T(8,128)(2,1)S(1)}, u32[]{:S(2)}, u32[]{:S(2)}) %all-to-all-start.8) | async-done | bytes 131104 | tf_op jit(solution)/shard_map/all_to_all | solution.py:33
  206.7 4.4 %all-to-all-start.9 = ((bf16[16,32,128]{2,1,0:T(8,128)(2,1)}), bf16[16,32,128]{2,1,0:T(8,128)(2,1)S(1)}, u32[]{:S(2)}, u32[]{:S(2)}) async-start(bf16[16,32,128]{2,1,0:T(8,128)(2,1)} %bitcast.50), calls=%async_computation.9 | async-start | bytes 262144 | tf_op jit(solution)/shard_map/all_to_all | solution.py:33
  211.3 5.5 %all-to-all-done.9 = bf16[16,32,128]{2,1,0:T(8,128)(2,1)S(1)} async-done(((bf16[16,32,128]{2,1,0:T(8,128)(2,1)}), bf16[16,32,128]{2,1,0:T(8,128)(2,1)S(1)}, u32[]{:S(2)}, u32[]{:S(2)}) %all-to-all-start.9) | async-done | bytes 131104 | tf_op jit(solution)/shard_map/all_to_all | solution.py:33
  217.5 4.8 %all-to-all-start.7 = ((bf16[16,32,128]{2,1,0:T(8,128)(2,1)}), bf16[16,32,128]{2,1,0:T(8,128)(2,1)S(1)}, u32[]{:S(2)}, u32[]{:S(2)}) async-start(bf16[16,32,128]{2,1,0:T(8,128)(2,1)} %bitcast.43), calls=%async_computation.7 | async-start | bytes 262144 | tf_op jit(solution)/shard_map/all_to_all | solution.py:33
  222.8 6.3 %all-to-all-done.7 = bf16[16,32,128]{2,1,0:T(8,128)(2,1)S(1)} async-done(((bf16[16,32,128]{2,1,0:T(8,128)(2,1)}), bf16[16,32,128]{2,1,0:T(8,128)(2,1)S(1)}, u32[]{:S(2)}, u32[]{:S(2)}) %all-to-all-start.7) | async-done | bytes 131104 | tf_op jit(solution)/shard_map/all_to_all | solution.py:33
  229.9 0.8 fusion.24
  (77 shorter events, 18.3 us)
Async XLA Ops:
  2.2 34.6 %all-to-all-start = ((f32[16,32,128]{2,1,0:T(8,128)}), f32[16,32,128]{2,1,0:T(8,128)S(1)}, u32[]{:S(2)}, u32[]{:S(2)}) async-start(f32[16,32,128]{2,1,0:T(8,128)} %bitcast.1), calls=%async_computation | async-start | bytes 524288 | tf_op jit(solution)/shard_map/all_to_all | solution.py:33
  9.7 32.7 %collective-permute-start = (bf16[256,2048]{1,0:T(8,128)(2,1)}, bf16[256,2048]{1,0:T(8,128)(2,1)}, u32[]{:S(2)}, u32[]{:S(2)}) collective-permute-start(bf16[256,2048]{1,0:T(8,128)(2,1)} %bitcast.145), channel_id=1, source_target_pairs={{0,0},{1,64},{64,1},{65,65},{2,2},{3,66},{66,3},{67,67},{4,4},{5,6... | collective-permute-start | bytes 3145736 | tf_op jit(solution)/shard_map/ppermute | solution.py:41
  14.1 21.7 %collective-permute-start.10 = (bf16[256,1024]{1,0:T(8,128)(2,1)}, bf16[256,1024]{1,0:T(8,128)(2,1)S(1)}, u32[]{:S(2)}, u32[]{:S(2)}) collective-permute-start(bf16[256,1024]{1,0:T(8,128)(2,1)} %bitcast.146), channel_id=1, source_target_pairs={{0,0},{1,64},{64,1},{65,65},{2,2},{3,66},{66,3},{67,67},{4,4},{5,6... | collective-permute-start | bytes 1572872 | tf_op jit(solution)/shard_map/ppermute | solution.py:41
  16.1 16.4 %collective-permute-start.9 = (s32[64]{0:T(128)}, s32[64]{0:T(128)S(1)}, u32[]{:S(2)}, u32[]{:S(2)}) collective-permute-start(s32[64]{0:T(128)} %bitcast.147), channel_id=1, source_target_pairs={{0,0},{1,64},{64,1},{65,65},{2,2},{3,66},{66,3},{67,67},{4,4},{5,6... | collective-permute-start | bytes 776 | tf_op jit(solution)/shard_map/ppermute | solution.py:41
  36.7 13.8 %all-to-all-start.3 = ((bf16[256,8,128]{2,0,1:T(8,128)(2,1)}), bf16[256,8,128]{2,0,1:T(8,128)(2,1)S(1)}, u32[]{:S(2)}, u32[]{:S(2)}) async-start(bf16[256,8,128]{2,0,1:T(8,128)(2,1)} %copy_bitcast_fusion), calls=%async_computation.3 | async-start | bytes 1048576 | tf_op jit(solution)/shard_map/all_to_all | solution.py:64
  42.4 29.1 %collective-permute-start.2 = (bf16[256,2048]{1,0:T(8,128)(2,1)}, bf16[256,2048]{1,0:T(8,128)(2,1)S(1)}, u32[]{:S(2)}, u32[]{:S(2)}) collective-permute-start(bf16[256,2048]{1,0:T(8,128)(2,1)} %collective-permute-done), channel_id=1, source_target_pairs={{0,6},{2,0},{4,2},{6,4},{1,7},{3,1},{5,3},{7,5},{8,14},{10,8},{12,... | collective-permute-start | bytes 3145736 | tf_op jit(solution)/shard_map/ppermute | solution.py:25
  45.7 28.7 %collective-permute-start.4 = (bf16[256,2048]{1,0:T(8,128)(2,1)}, bf16[256,2048]{1,0:T(8,128)(2,1)S(1)}, u32[]{:S(2)}, u32[]{:S(2)}) collective-permute-start(bf16[256,2048]{1,0:T(8,128)(2,1)} %collective-permute-done), channel_id=1, source_target_pairs={{0,2},{2,4},{4,6},{6,0},{1,3},{3,5},{5,7},{7,1},{8,10},{10,12},{12... | collective-permute-start | bytes 3145736 | tf_op jit(solution)/shard_map/ppermute | solution.py:25
  48.2 29.5 %collective-permute-start.1 = (bf16[256,2048]{1,0:T(8,128)(2,1)}, bf16[256,2048]{1,0:T(8,128)(2,1)}, u32[]{:S(2)}, u32[]{:S(2)}) collective-permute-start(bf16[256,2048]{1,0:T(8,128)(2,1)} %collective-permute-done), channel_id=1, source_target_pairs={{0,64},{64,0},{1,65},{65,1},{2,66},{66,2},{3,67},{67,3},{4,68},{68... | collective-permute-start | bytes 3145736 | tf_op jit(solution)/shard_map/ppermute | solution.py:25
  51.4 44.9 %all-to-all-start.2 = ((bf16[8,256,128]{2,1,0:T(8,128)(2,1)}), bf16[8,256,128]{2,1,0:T(8,128)(2,1)S(1)}, u32[]{:S(2)}, u32[]{:S(2)}) async-start(bf16[8,256,128]{2,1,0:T(8,128)(2,1)} %broadcast_in_dim.21), calls=%async_computation.2 | async-start | bytes 1048576 | tf_op jit(solution)/shard_map/all_to_all | solution.py:33
  71.5 18.8 %collective-permute-start.3 = (bf16[256,2048]{1,0:T(8,128)(2,1)S(1)}, bf16[256,2048]{1,0:T(8,128)(2,1)S(1)}, u32[]{:S(2)}, u32[]{:S(2)}) collective-permute-start(bf16[256,2048]{1,0:T(8,128)(2,1)S(1)} %collective-permute-done.2), channel_id=1, source_target_pairs={{0,64},{64,0},{1,65},{65,1},{2,66},{66,2},{3,67},{67,3},{4,68},{68... | collective-permute-start | bytes 3145736 | tf_op jit(solution)/shard_map/ppermute | solution.py:25
  73.1 13.6 %collective-permute-start.6 = (bf16[128,2048]{1,0:T(8,128)(2,1)S(1)}, bf16[128,2048]{1,0:T(8,128)(2,1)S(1)}, u32[]{:S(2)}, u32[]{:S(2)}) collective-permute-start(bf16[128,2048]{1,0:T(8,128)(2,1)S(1)} %slice.17), channel_id=1, source_target_pairs={{0,6},{2,0},{4,2},{6,4},{1,7},{3,1},{5,3},{7,5},{8,14},{10,8},{12,... | collective-permute-start | bytes 1572872 | tf_op jit(solution)/shard_map/ppermute | solution.py:25
  74.5 14.5 %collective-permute-start.7 = (bf16[128,2048]{1,0:T(8,128)(2,1)S(1)}, bf16[128,2048]{1,0:T(8,128)(2,1)S(1)}, u32[]{:S(2)}, u32[]{:S(2)}) collective-permute-start(bf16[128,2048]{1,0:T(8,128)(2,1)S(1)} %slice.18), channel_id=1, source_target_pairs={{0,2},{2,4},{4,6},{6,0},{1,3},{3,5},{5,7},{7,1},{8,10},{10,12},{12... | collective-permute-start | bytes 1572872 | tf_op jit(solution)/shard_map/ppermute | solution.py:25
  77.1 15.4 %collective-permute-start.5 = (bf16[256,2048]{1,0:T(8,128)(2,1)S(1)}, bf16[256,2048]{1,0:T(8,128)(2,1)S(1)}, u32[]{:S(2)}, u32[]{:S(2)}) collective-permute-start(bf16[256,2048]{1,0:T(8,128)(2,1)S(1)} %collective-permute-done.4), channel_id=1, source_target_pairs={{0,64},{64,0},{1,65},{65,1},{2,66},{66,2},{3,67},{67,3},{4,68},{68... | collective-permute-start | bytes 3145736 | tf_op jit(solution)/shard_map/ppermute | solution.py:25
  89.1 6.1 %collective-permute-start.8 = (bf16[256,2048]{1,0:T(8,128)(2,1)S(1)}, bf16[256,2048]{1,0:T(8,128)(2,1)S(1)}, u32[]{:S(2)}, u32[]{:S(2)}) collective-permute-start(bf16[256,2048]{1,0:T(8,128)(2,1)S(1)} %pad_maximum_fusion), channel_id=1, source_target_pairs={{0,64},{64,0},{1,65},{65,1},{2,66},{66,2},{3,67},{67,3},{4,68},{68... | collective-permute-start | bytes 3145736 | tf_op jit(solution)/shard_map/ppermute | solution.py:25
  97.3 16.0 %all-to-all-start.1 = ((f32[16,2,32,128]{3,2,1,0:T(8,128)}), f32[16,2,32,128]{3,2,1,0:T(8,128)S(1)}, u32[]{:S(2)}, u32[]{:S(2)}) async-start(f32[16,2,32,128]{3,2,1,0:T(8,128)} %bitcast.5), calls=%async_computation.1 | async-start | bytes 1048576 | tf_op jit(solution)/shard_map/all_to_all | solution.py:33
  113.3 26.2 %all-to-all-start.4 = ((bf16[8,256,128]{2,1,0:T(8,128)(2,1)}), bf16[8,256,128]{2,1,0:T(8,128)(2,1)S(1)}, u32[]{:S(2)}, u32[]{:S(2)}) async-start(bf16[8,256,128]{2,1,0:T(8,128)(2,1)} %bitcast.33), calls=%async_computation.4 | async-start | bytes 1048576 | tf_op jit(solution)/shard_map/all_to_all | solution.py:33
  165.8 63.4 %copy-start.2 = (f32[32,256]{1,0:T(8,128)S(1)}, f32[32,256]{1,0:T(8,128)}, u32[]{:S(2)}) copy-start(f32[32,256]{1,0:T(8,128)} %param.10) | copy-start | bytes 98308
  165.8 63.4 %copy-start.3 = (f32[32,256]{1,0:T(8,128)S(1)}, f32[32,256]{1,0:T(8,128)}, u32[]{:S(2)}) copy-start(f32[32,256]{1,0:T(8,128)} %param.11) | copy-start | bytes 98308
  165.8 64.0 %copy-start = (f32[1,32,1024]{2,1,0:T(8,128)S(1)}, f32[1,32,1024]{2,1,0:T(8,128)}, u32[]{:S(2)}) copy-start(f32[1,32,1024]{2,1,0:T(8,128)} %param.13) | copy-start | bytes 393220
  165.8 64.0 %copy-start.1 = (f32[1,32,1024]{2,1,0:T(8,128)S(1)}, f32[1,32,1024]{2,1,0:T(8,128)}, u32[]{:S(2)}) copy-start(f32[1,32,1024]{2,1,0:T(8,128)} %param.12) | copy-start | bytes 393220
  172.5 21.4 %all-to-all-start.6 = ((bf16[8,256,128]{2,1,0:T(8,128)(2,1)}), bf16[8,256,128]{2,1,0:T(8,128)(2,1)S(1)}, u32[]{:S(2)}, u32[]{:S(2)}) async-start(bf16[8,256,128]{2,1,0:T(8,128)(2,1)} %bitcast.41), calls=%async_computation.6 | async-start | bytes 1048576 | tf_op jit(solution)/shard_map/all_to_all | solution.py:33
  194.6 11.5 %all-to-all-start.8 = ((bf16[16,32,128]{2,1,0:T(8,128)(2,1)}), bf16[16,32,128]{2,1,0:T(8,128)(2,1)S(1)}, u32[]{:S(2)}, u32[]{:S(2)}) async-start(bf16[16,32,128]{2,1,0:T(8,128)(2,1)} %bitcast.46), calls=%async_computation.8 | async-start | bytes 262144 | tf_op jit(solution)/shard_map/all_to_all | solution.py:33
  206.7 10.2 %all-to-all-start.9 = ((bf16[16,32,128]{2,1,0:T(8,128)(2,1)}), bf16[16,32,128]{2,1,0:T(8,128)(2,1)S(1)}, u32[]{:S(2)}, u32[]{:S(2)}) async-start(bf16[16,32,128]{2,1,0:T(8,128)(2,1)} %bitcast.50), calls=%async_computation.9 | async-start | bytes 262144 | tf_op jit(solution)/shard_map/all_to_all | solution.py:33
  217.5 11.6 %all-to-all-start.7 = ((bf16[16,32,128]{2,1,0:T(8,128)(2,1)}), bf16[16,32,128]{2,1,0:T(8,128)(2,1)S(1)}, u32[]{:S(2)}, u32[]{:S(2)}) async-start(bf16[16,32,128]{2,1,0:T(8,128)(2,1)} %bitcast.43), calls=%async_computation.7 | async-start | bytes 262144 | tf_op jit(solution)/shard_map/all_to_all | solution.py:33

commit v2 on v1

v2 whole, which is shorter than its diff:
```python
import functools

import jax
import jax.numpy as jnp
from jax import lax
from jax.experimental import pallas as pl
from jax.experimental.pallas import tpu as pltpu
from jax.sharding import Mesh
from jax.sharding import PartitionSpec as P

D = 2048
STEPS = 2
PRIOR = 1000
BLOCK = 128
FIRST = 64
TURN = [(0, 0), (1, 2), (2, 1), (3, 3)]

OWN = ((0, FIRST, 256),)
LEAD = ((0, 0, FIRST), (1, 0, FIRST), (3, 0, FIRST), (2, 0, FIRST))
ABOVE = ((1, FIRST, 256),)
BELOW = ((3, FIRST, 256),)
FAR = ((2, FIRST, 128), (2, 128, 256))


def adam_moments(first, second, grad):
    return 0.9 * first + 0.1 * grad, 0.95 * second + 0.05 * grad * grad


def adam_update(param, first, second, step):
    upd = first / (1.0 - 0.9**step) / (jnp.sqrt(second / (1.0 - 0.95**step)) + 1e-08)
    return param - 0.1 * (upd + 0.1 * param)


def shift(x, axis, by):
    size = lax.axis_size(axis)
    return lax.ppermute(x, axis, [(i, (i + by) % size) for i in range(size)])


def other_core(x):
    return shift(x, "c", 1)


def exchange(x, axes):
    return lax.all_to_all(x, axes, 0, 0, tiled=True)


def pick(x, index, axis):
    return lax.dynamic_index_in_dim(x, index, axis, keepdims=False)


def after(x, *earlier):
    return lax.optimization_barrier((x, *earlier))[0]


def turned(x):
    return lax.ppermute(x, ("c", "x"), TURN)


def up(x):
    return shift(x, ("yh", "yl"), 1)


def down(x):
    return shift(x, ("yh", "yl"), -1)


def product_kernel(chunks, last, place, goals, weights, *refs):
    count = sum(len(blocks) for blocks, _ in chunks)
    blocks, refs = refs[:count], refs[count:]
    earlier, out, held, total, sems = refs if len(refs) == 5 else (None, *refs)
    copies, row = [], 0
    for at, block in enumerate(blocks):
        rows = block.shape[0]
        copy = pltpu.make_async_copy(block, held.at[pl.ds(row, rows)], sems.at[at])
        copy.start()
        copies.append(copy)
        row += rows
    if earlier is not None:
        total[...] = earlier[...]
    row = done = 0
    for number, (parts, rows_of) in enumerate(chunks):
        goal = []
        for core in range(2):
            for away, low, high in rows_of:
                source = lax.rem(place[0] + away, 4) * 2 + lax.rem(place[1] + core, 2)
                goal.append(goals[source, low:high])
        goal = jnp.concatenate(goal, 0).astype(jnp.float32)
        for copy in copies[done : done + len(parts)]:
            copy.wait()
        done += len(parts)
        inputs = held[row : row + goal.shape[0]]
        row += goal.shape[0]
        outputs = jnp.dot(inputs, weights[...], preferred_element_type=jnp.float32)
        resid = (outputs * D ** (-0.5) - goal).astype(jnp.bfloat16)
        grad = lax.dot_general(
            resid, inputs, (((0,), (0,)), ((), ())), preferred_element_type=jnp.float32
        )
        if number == 0 and earlier is None:
            total[...] = grad
        else:
            total[...] += grad
    if last:
        for z in range(8):
            out[z] = total[:, z * 256 : (z + 1) * 256].T.astype(jnp.bfloat16)
    else:
        out[...] = total[...]


def product(chunks, place, goals, weights, earlier=None, last=False):
    blocks = [block for parts, _ in chunks for block in parts]
    rows = sum(block.shape[0] for block in blocks)
    whole = pl.BlockSpec(memory_space=pltpu.VMEM)
    args = [place, goals, weights, *blocks]
    specs = [pl.BlockSpec(memory_space=pltpu.SMEM), whole, whole]
    specs += [pl.BlockSpec(memory_space=pl.ANY)] * len(blocks)
    if earlier is not None:
        args.append(earlier)
        specs.append(whole)
    shape = ((8, 256, BLOCK), jnp.bfloat16) if last else ((BLOCK, D), jnp.float32)
    return pl.pallas_call(
        functools.partial(product_kernel, [(len(p) * [0], r) for p, r in chunks], last),
        out_shape=jax.ShapeDtypeStruct(*shape),
        in_specs=specs,
        out_specs=whole,
        scratch_shapes=[
            pltpu.VMEM((rows, D), jnp.bfloat16),
            pltpu.VMEM((BLOCK, D), jnp.float32),
            pltpu.SemaphoreType.DMA((len(blocks),)),
        ],
        compiler_params=pltpu.CompilerParams(vmem_limit_bytes=40 * 2**20),
        cost_estimate=pl.CostEstimate(
            flops=8 * rows * D * BLOCK, bytes_accessed=2 * rows * D, transcendentals=0
        ),
    )(*args)


def gathered(param):
    weights = jnp.broadcast_to(param.astype(jnp.bfloat16)[None], (8, 256, BLOCK))
    return exchange(weights, "z").reshape(D, BLOCK)


def reduced(grad):
    return jnp.sum(exchange(grad, "z").astype(jnp.float32), 0)


def per_device(tokens, targets, lengths, outer_param, outer_mom, first_mom, second_mom):
    c, x = lax.axis_index("c"), lax.axis_index("x")
    h, y, yh = lax.axis_index("h"), lax.axis_index(("yh", "yl")), lax.axis_index("yh")
    place = jnp.stack([y, c]).astype(jnp.int32)

    own = lax.axis_index(("z", "yh", "yl", "x"))
    valid = lax.iota(jnp.int32, tokens.shape[1]) < pick(lengths[0], own, 0)
    masked = jnp.where(valid[:, None], tokens[0], jnp.zeros((), tokens.dtype))
    lead, rest = masked[:FIRST], masked[FIRST:]

    rest = turned(rest)
    lead_above, lead_below = down(lead), up(lead)

    start = jnp.moveaxis(outer_param.reshape(32, 2, BLOCK), 1, 0)
    start = jnp.broadcast_to(start[None, None, :, None], (2, 2, 2, 2, 32, BLOCK))
    start = exchange(start.reshape(16, 32, BLOCK), ("h", "yh", "yl", "x"))

    lead_far = down(lead_above)
    above, below = down(rest), up(rest)
    lead = turned(jnp.concatenate([lead, lead_above, lead_below, lead_far], 0))

    goals = after(targets[0], rest).reshape(256, 2, 2, 2, BLOCK)
    goals = turned(goals.transpose(1, 3, 2, 0, 4).reshape(8, 256, BLOCK))
    goals = exchange(goals, ("yh", "yl", "c"))
    start = pick(start.reshape(2, 256, BLOCK), yh, 0)
    weights = gathered(start)

    far_a, far_b = down(above[:FIRST]), up(below[FIRST:])
    chunks = [
        ((rest, other_core(rest)), OWN),
        ((lead, other_core(lead)), LEAD),
        ((above, other_core(above)), ABOVE),
        ((below, other_core(below)), BELOW),
        ((far_a, far_b, other_core(far_a), other_core(far_b)), FAR),
    ]
    grad = product(chunks[:2], place, goals, weights)
    grad = product(chunks[2:4], place, goals, weights, grad)
    grad = product(chunks[4:], place, goals, weights, grad, last=True)

    moments = jnp.stack([first_mom[0], second_mom[0]])
    moments = after(moments, grad)
    moments = moments.reshape(2, 32, 2, 2, 2, BLOCK)
    moments = moments.transpose(3, 2, 4, 0, 1, 5)[:, :, :, None]
    moments = jnp.broadcast_to(moments, (2, 2, 2, 2, 2, 32, BLOCK))
    moments = exchange(moments.reshape(16, 2, 32, BLOCK), ("c", "yh", "yl", "x"))
    moments = pick(moments.reshape(2, 8, 2, 32, BLOCK), x, 0)
    first = moments[:, 0].reshape(256, BLOCK)
    second = moments[:, 1].reshape(256, BLOCK)

    count = jnp.sum(lengths[0]).astype(jnp.float32).reshape(1)
    count = jnp.where(c == x, count, other_core(count))
    coef = D ** (-0.5) / count

    grad = reduced(grad) * coef
    grads = [grad.astype(jnp.bfloat16)]
    first, second = adam_moments(first, second, grad)
    param = adam_update(start, first, second, PRIOR + 1)

    grad = product(chunks, place, goals, gathered(param), last=True)
    grad = reduced(grad) * coef
    grads.append(grad.astype(jnp.bfloat16))
    first, second = adam_moments(first, second, grad)
    param = adam_update(param, first, second, PRIOR + 2)

    change = (start - param).astype(jnp.bfloat16).reshape(1, 8, 32, BLOCK)
    change = jnp.broadcast_to(change, (2, 8, 32, BLOCK)).reshape(16, 32, BLOCK)
    change = exchange(change, ("h", "yh", "yl", "x")).reshape(2, 2, 2, 2, 32, BLOCK)
    change = jnp.sum(pick(change, h, 1).astype(jnp.float32), (0, 2))
    pseudo = jnp.moveaxis(change, 0, 1).reshape(32, 2 * BLOCK) / 4
    new_mom = 0.9 * outer_mom + pseudo
    new_param = outer_param - 0.7 * (pseudo + 0.9 * new_mom)

    home = jnp.stack([grad.reshape(8, 32, BLOCK) for grad in grads], 1)[None]
    home = jnp.broadcast_to(home, (2, 8, 2, 32, BLOCK)).reshape(16, 2, 32, BLOCK)
    home = exchange(home, ("c", "yh", "yl", "x"))
    home = pick(home.reshape(2, 2, 2, 2, 2, 32, BLOCK), c, 3)
    home = home.transpose(3, 4, 1, 0, 2, 5).reshape(2, 32, 8 * BLOCK)
    first, second = first_mom[0], second_mom[0]
    for step in range(STEPS):
        first, second = adam_moments(first, second, home[step].astype(jnp.float32))
    return (new_param, new_mom, first[None], second[None])


def solution(mesh):
    fine = Mesh(
        mesh.devices.reshape(2, 2, 8, 2, 2, 2), ("h", "c", "z", "yh", "yl", "x")
    )
    group, fsdp = ("h", "c"), ("z", "yh", "yl", "x")
    in_specs = (
        P(group, fsdp, None),
        P(group, fsdp, None),
        P(group, None),
        P(fsdp, group),
        P(fsdp, group),
        P(group, fsdp, None),
        P(group, fsdp, None),
    )
    out_specs = (
        P(fsdp, group),
        P(fsdp, group),
        P(group, fsdp, None),
        P(group, fsdp, None),
    )
    return jax.shard_map(
        per_device, mesh=fine, in_specs=in_specs, out_specs=out_specs, check_vma=False
    )
```

time: 232 us -> 223 us (0.961)
  waiting for transfers between devices: 80.4 us -> 48 us
  blocking collectives: 20.2 us -> 49.3 us
  matrix products: 24.8 us -> 0 us
  Pallas kernels: 0 us -> 23.1 us
  local copies, waits for them, and re-layouts: 26.2 us -> 11.2 us
  starting transfers between devices: 68 us -> 78.1 us
    all_to_all x1 -> x3, blocking collectives: 20.2 us -> 49.3 us  [exchange(): return lax.all_to_all(x, axes, 0, 0, tiled=True)]
    dot_general x4 -> x0, matrix products: 24.8 us -> none  [the longest x2 13.3 us: per_device(): lax.dot_general(inputs, resid, (((0,), (0,)), ((), ())), preferred_elemen...]
    pallas_call x0 -> x4, Pallas kernels: none -> 23.1 us  [product(): pl.pallas_call(functools.partial(product_kernel, [(len(p) * [0], r) for p...]
    all_to_all x8 -> x6, waiting for transfers between devices: 52 us -> 29.4 us  [exchange(): return lax.all_to_all(x, axes, 0, 0, tiled=True)]
    unnamed x30 -> x24, local copies, waits for them, and re-layouts: 16.4 us -> 2.22 us
    ppermute x8 -> x14, starting transfers between devices: 7.73 us -> 16.9 us  [shift(): return lax.ppermute(x, axis, [(i, (i + by) % size) for i in range(size)])]
    ppermute x3, starting transfers between devices: 9.95 us -> 15.9 us  [turned(): return lax.ppermute(x, ('c', 'x'), TURN)]
    ppermute x3, waiting for transfers between devices: 11.1 us -> 5.7 us  [turned(): return lax.ppermute(x, ('c', 'x'), TURN)]
  transfers between devices with their start and end apart: 20 -> 23, of which waited for: 10 -> 7; matrix products, arithmetic and copies ran while one was open for 18% -> 4% of each run, Pallas kernels for 0% -> 4%
where the time goes in v2:
time: 223 us; the launch traced here: 221 us
  starting transfers between devices  78.1 us (35%)
  blocking collectives  49.3 us (22%)
  waiting for transfers between devices  48 us (22%)
  Pallas kernels  23.1 us (10%)
  local copies, waits for them, and re-layouts  11.2 us (5%)
  other arithmetic  9.02 us (4%)
  between operations  2.47 us (1%)
    all_to_all x3, blocking collectives, exchange(): return lax.all_to_all(x, axes, 0, 0, tiled=True)  49.3 us
    all_to_all x6, starting transfers between devices, exchange(): return lax.all_to_all(x, axes, 0, 0, tiled=True)  45.3 us
    all_to_all x6, waiting for transfers between devices, exchange(): return lax.all_to_all(x, axes, 0, 0, tiled=True)  29.4 us
    pallas_call x4, Pallas kernels, product(): pl.pallas_call(functools.partial(product_kernel, [(len(p) * [0], r) for p...  23.1 us
    ppermute x14, starting transfers between devices, shift(): return lax.ppermute(x, axis, [(i, (i + by) % size) for i in range(size)])  16.9 us
    ppermute x3, starting transfers between devices, turned(): return lax.ppermute(x, ('c', 'x'), TURN)  15.9 us
    ppermute x14, waiting for transfers between devices, shift(): return lax.ppermute(x, axis, [(i, (i + by) % size) for i in range(size)])  13 us
    ppermute x3, waiting for transfers between devices, turned(): return lax.ppermute(x, ('c', 'x'), TURN)  5.7 us
  transfers between devices with their start and end apart: 23, of which 7 were waited for; matrix products, arithmetic and copies ran while one was open for 4% of the time, Pallas kernels for 4%

profile of v2, /device:TPU:1, one launch (start us, length us, event | category | flops | bytes accessed | tf_op | source)
XLA Modules:
  0.0 221.2 jit_solution(8429151118431105661)
XLA Ops:
  0.6 1.2 constant_dynamic-slice_fusion
  1.9 0.6 iota_compare_fusion
  2.5 1.4 bitcast_select_fusion
  3.9 3.6 %collective-permute-start.11 = (bf16[64,2048]{1,0:T(8,128)(2,1)S(1)}, bf16[64,2048]{1,0:T(8,128)(2,1)S(1)}, u32[]{:S(2)}, u32[]{:S(2)}) collective-permute-start(bf16[64,2048]{1,0:T(8,128)(2,1)S(1)} %slice.37), channel_id=1, source_target_pairs={{0,6},{2,0},{4,2},{6,4},{1,7},{3,1},{5,3},{7,5},{8,14},{10,8},{12,... | collective-permute-start | bytes 786440 | tf_op jit(solution)/shard_map/ppermute | solution.py:36
  7.6 5.0 %collective-permute-done.11 = bf16[64,2048]{1,0:T(8,128)(2,1)S(1)} collective-permute-done((bf16[64,2048]{1,0:T(8,128)(2,1)S(1)}, bf16[64,2048]{1,0:T(8,128)(2,1)S(1)}, u32[]{:S(2)}, u32[]{:S(2)}) %collective-permute-start.11) | collective-permute-done | bytes 262176 | tf_op jit(solution)/shard_map/ppermute | solution.py:36
  12.6 3.4 %collective-permute-start.13 = (bf16[64,2048]{1,0:T(8,128)(2,1)S(1)}, bf16[64,2048]{1,0:T(8,128)(2,1)S(1)}, u32[]{:S(2)}, u32[]{:S(2)}) collective-permute-start(bf16[64,2048]{1,0:T(8,128)(2,1)S(1)} %collective-permute-done.11), channel_id=1, source_target_pairs={{0,6},{2,0},{4,2},{6,4},{1,7},{3,1},{5,3},{7,5},{8,14},{10,8},{12,... | collective-permute-start | bytes 786440 | tf_op jit(solution)/shard_map/ppermute | solution.py:36
  16.0 4.8 %collective-permute-start = (bf16[192,2048]{1,0:T(8,128)(2,1)S(1)}, bf16[192,2048]{1,0:T(8,128)(2,1)}, u32[]{:S(2)}, u32[]{:S(2)}) collective-permute-start(bf16[192,2048]{1,0:T(8,128)(2,1)S(1)} %slice.34), channel_id=1, source_target_pairs={{0,0},{1,64},{64,1},{65,65},{2,2},{3,66},{66,3},{67,67},{4,4},{5,6... | collective-permute-start | bytes 2359304 | tf_op jit(solution)/shard_map/ppermute | solution.py:56
  20.9 1.0 pad_maximum_fusion
  21.9 4.6 %collective-permute-start.14 = (bf16[256,2048]{1,0:T(8,128)(2,1)}, bf16[256,2048]{1,0:T(8,128)(2,1)}, u32[]{:S(2)}, u32[]{:S(2)}) collective-permute-start(bf16[256,2048]{1,0:T(8,128)(2,1)} %pad_maximum_fusion), channel_id=1, source_target_pairs={{0,0},{1,64},{64,1},{65,65},{2,2},{3,66},{66,3},{67,67},{4,4},{5,6... | collective-permute-start | bytes 3145736 | tf_op jit(solution)/shard_map/ppermute | solution.py:56
  26.6 0.7 broadcast_in_dim.28
  27.3 11.0 %all-to-all-start = ((f32[16,32,128]{2,1,0:T(8,128)}), f32[16,32,128]{2,1,0:T(8,128)S(1)}, u32[]{:S(2)}, u32[]{:S(2)}) async-start(f32[16,32,128]{2,1,0:T(8,128)} %bitcast.1), calls=%async_computation | async-start | bytes 524288 | tf_op jit(solution)/shard_map/all_to_all | solution.py:44
  38.3 1.4 collective-permute-start.4
  39.7 1.3 collective-permute-start.2
  41.0 4.8 %all-to-all-done = f32[16,32,128]{2,1,0:T(8,128)S(1)} async-done(((f32[16,32,128]{2,1,0:T(8,128)}), f32[16,32,128]{2,1,0:T(8,128)S(1)}, u32[]{:S(2)}, u32[]{:S(2)}) %all-to-all-start) | async-done | bytes 262176 | tf_op jit(solution)/shard_map/all_to_all | solution.py:44
  45.9 0.9 broadcast_in_dim.32
  46.8 8.2 %all-to-all-start.2 = ((bf16[8,256,128]{2,1,0:T(8,128)(2,1)}), bf16[8,256,128]{2,1,0:T(8,128)(2,1)S(1)}, u32[]{:S(2)}, u32[]{:S(2)}) async-start(bf16[8,256,128]{2,1,0:T(8,128)(2,1)} %broadcast_in_dim.32), calls=%async_computation.2 | async-start | bytes 1048576 | tf_op jit(solution)/shard_map/all_to_all | solution.py:44
  55.5 6.5 %collective-permute-start.1 = (bf16[8,256,128]{2,1,0:T(8,128)(2,1)S(1)}, bf16[8,256,128]{2,1,0:T(8,128)(2,1)S(1)}, u32[]{:S(2)}, u32[]{:S(2)}) collective-permute-start(bf16[8,256,128]{2,1,0:T(8,128)(2,1)S(1)} %bitcast.96), channel_id=1, source_target_pairs={{0,0},{1,64},{64,1},{65,65},{2,2},{3,66},{66,3},{67,67},{4,4},{5,6... | collective-permute-start | bytes 1572872 | tf_op jit(solution)/shard_map/ppermute | solution.py:56
  62.5 0.8 slice.36
  63.5 5.7 %collective-permute-done.1 = bf16[8,256,128]{2,1,0:T(8,128)(2,1)S(1)} collective-permute-done((bf16[8,256,128]{2,1,0:T(8,128)(2,1)S(1)}, bf16[8,256,128]{2,1,0:T(8,128)(2,1)S(1)}, u32[]{:S(2)}, u32[]{:S(2)}) %collective-permute-start.1) | collective-permute-done | bytes 524320 | tf_op jit(solution)/shard_map/ppermute | solution.py:56
  69.2 0.8 copy-done.3
  70.0 6.9 %all-to-all-start.1 = ((bf16[8,256,128]{2,1,0:T(8,128)(2,1)}), bf16[8,256,128]{2,1,0:T(8,128)(2,1)S(1)}, u32[]{:S(2)}, u32[]{:S(2)}) async-start(bf16[8,256,128]{2,1,0:T(8,128)(2,1)} %copy-done.3), calls=%async_computation.1 | async-start | bytes 1048576 | tf_op jit(solution)/shard_map/all_to_all | solution.py:44
  76.8 0.7 slice.35
  77.6 2.6 %collective-permute-start.3 = (bf16[64,2048]{1,0:T(8,128)(2,1)}, bf16[64,2048]{1,0:T(8,128)(2,1)}, u32[]{:S(2)}, u32[]{:S(2)}) collective-permute-start(bf16[64,2048]{1,0:T(8,128)(2,1)} %slice.35), channel_id=1, source_target_pairs={{0,6},{2,0},{4,2},{6,4},{1,7},{3,1},{5,3},{7,5},{8,14},{10,8},{12,... | collective-permute-start | bytes 786440 | tf_op jit(solution)/shard_map/ppermute | solution.py:36
  80.9 1.7 pad_maximum_fusion.1
  82.6 8.0 %collective-permute-done.3.refs_0_.refs_8_ = bf16[64,2048]{1,0:T(8,128)(2,1)} collective-permute-done((bf16[64,2048]{1,0:T(8,128)(2,1)}, bf16[64,2048]{1,0:T(8,128)(2,1)}, u32[]{:S(2)}, u32[]{:S(2)}) %collective-permute-start.3) | collective-permute-done | bytes 262176 | tf_op jit(solution)/shard_map/ppermute | solution.py:36
  90.6 0.9 collective-permute-start.6
  91.5 5.1 %shard_map.102.refs_4_ = f32[128,2048]{1,0:T(8,128)S(1)} custom-call(s32[2]{0:T(128)S(1)} %pad_add_fusion.place, bf16[8,256,128]{2,1,0:T(8,128)(2,1)S(1)} %all-to-all-done.1.goals, bf16[2048,128]{1,0:T(8,128)(2,1)S(1)} %bitcast.84, bf16[192,2048]{1,0:T(8,128)(2,1)} %collective-permute-done.refs_0_, bf16[192,2048]{1,0:T(8,128)(2,1)} %collective-permute-done.10.refs_1_, ...), custom_call_target="tpu_custom_call" | custom-call | flops 1879048192 | bytes 3670016 | tf_op jit(solution)/shard_map/pallas_call | solution.py:120
  96.6 3.8 %shard_map.103.refs_4_ = f32[128,2048]{1,0:T(8,128)S(1)} custom-call(s32[2]{0:T(128)S(1)} %pad_add_fusion.place, bf16[8,256,128]{2,1,0:T(8,128)(2,1)S(1)} %all-to-all-done.1.goals, bf16[2048,128]{1,0:T(8,128)(2,1)S(1)} %bitcast.85, bf16[192,2048]{1,0:T(8,128)(2,1)S(1)} %collective-permute-done.2.refs_0_.refs_4_, ...), custom_call_target="tpu_custom_call" | custom-call | flops 1610612736 | bytes 3145728 | tf_op jit(solution)/shard_map/pallas_call | solution.py:120
  100.4 4.3 %shard_map.104 = bf16[8,256,128]{2,1,0:T(8,128)(2,1)} custom-call(s32[2]{0:T(128)S(1)} %pad_add_fusion.place, bf16[8,256,128]{2,1,0:T(8,128)(2,1)S(1)} %all-to-all-done.1.goals, bf16[2048,128]{1,0:T(8,128)(2,1)S(1)} %bitcast.86, bf16[64,2048]{1,0:T(8,128)(2,1)} %collective-permute-done.3.refs_0_.refs_8_, ...), custom_call_target="tpu_custom_call" | custom-call | flops 805306368 | bytes 1572864 | tf_op jit(solution)/shard_map/pallas_call | solution.py:120
  104.7 1.2 reshape.285
  106.0 13.4 %all_to_all.45 = f32[16,2,32,128]{3,2,1,0:T(8,128)} all-to-all(f32[16,2,32,128]{3,2,1,0:T(8,128)S(1)} %bitcast.88), channel_id=1, replica_groups=mesh['h'=2,'c'=2,'z'=8,'yh'=2,'yl'=2,'x'=2] {'c','yh','yl','x'}, dimensions={0} | all-to-all | bytes 1048576 | tf_op jit(solution)/shard_map/all_to_all | solution.py:44
  119.4 4.6 %all-to-all-start.4 = ((bf16[8,256,128]{2,1,0:T(8,128)(2,1)}), bf16[8,256,128]{2,1,0:T(8,128)(2,1)}, u32[]{:S(2)}, u32[]{:S(2)}) async-start(bf16[8,256,128]{2,1,0:T(8,128)(2,1)} %shard_map.104), calls=%async_computation.4 | async-start | bytes 1048576 | tf_op jit(solution)/shard_map/all_to_all | solution.py:44
  125.3 2.3 %collective-permute-start.16 = (f32[1]{0:T(128)}, f32[1]{0:T(128)}, u32[]{:S(2)}, u32[]{:S(2)}) collective-permute-start(f32[1]{0:T(128)} %bitcast.19), channel_id=1, source_target_pairs={{0,64},{64,0},{1,65},{65,1},{2,66},{66,2},{3,67},{67,3},{4,68},{68... | collective-permute-start | bytes 20 | tf_op jit(solution)/shard_map/ppermute | solution.py:36
  128.3 1.0 dynamic-slice_bitcast_fusion
  129.3 11.9 %all-to-all-done.4 = bf16[8,256,128]{2,1,0:T(8,128)(2,1)} async-done(((bf16[8,256,128]{2,1,0:T(8,128)(2,1)}), bf16[8,256,128]{2,1,0:T(8,128)(2,1)}, u32[]{:S(2)}, u32[]{:S(2)}) %all-to-all-start.4) | async-done | bytes 524320 | tf_op jit(solution)/shard_map/all_to_all | solution.py:44
  141.2 1.1 convert_reduce_fusion.1
  142.3 0.7 fusion.26
  143.2 17.9 %all_to_all.46 = bf16[8,256,128]{2,1,0:T(8,128)(2,1)S(1)} all-to-all(bf16[8,256,128]{2,1,0:T(8,128)(2,1)S(1)} %broadcast_in_dim.35), channel_id=1, replica_groups=mesh['h'=2,'c'=2,'z'=8,'yh'=2,'yl'=2,'x'=2] {'z'}, dimensions={0} | all-to-all | bytes 1048576 | tf_op jit(solution)/shard_map/all_to_all | solution.py:44
  161.1 9.9 %shard_map.105 = bf16[8,256,128]{2,1,0:T(8,128)(2,1)S(1)} custom-call(s32[2]{0:T(128)S(1)} %pad_add_fusion.place, bf16[8,256,128]{2,1,0:T(8,128)(2,1)S(1)} %all-to-all-done.1.goals, bf16[2048,128]{1,0:T(8,128)(2,1)S(1)} %bitcast.87, bf16[192,2048]{1,0:T(8,128)(2,1)} %collective-permute-done.refs_0_, bf16[192,2048]{1,0:T(8,128)(2,1)} %collective-permute-done.10.refs_1_, ...), custom_call_target="tpu_custom_call" | custom-call | flops 4294967296 | bytes 8388608 | tf_op jit(solution)/shard_map/pallas_call | solution.py:120
  171.0 18.0 %all_to_all.47 = bf16[8,256,128]{2,1,0:T(8,128)(2,1)S(1)} all-to-all(bf16[8,256,128]{2,1,0:T(8,128)(2,1)S(1)} %shard_map.105), channel_id=1, replica_groups=mesh['h'=2,'c'=2,'z'=8,'yh'=2,'yl'=2,'x'=2] {'z'}, dimensions={0} | all-to-all | bytes 1048576 | tf_op jit(solution)/shard_map/all_to_all | solution.py:44
  189.3 0.7 broadcast_in_dim.64
  190.0 7.9 %all-to-all-start.7 = ((bf16[16,32,128]{2,1,0:T(8,128)(2,1)}), bf16[16,32,128]{2,1,0:T(8,128)(2,1)S(1)}, u32[]{:S(2)}, u32[]{:S(2)}) async-start(bf16[16,32,128]{2,1,0:T(8,128)(2,1)} %bitcast.29), calls=%async_computation.7 | async-start | bytes 262144 | tf_op jit(solution)/shard_map/all_to_all | solution.py:44
  198.0 6.8 %all-to-all-done.7 = bf16[16,32,128]{2,1,0:T(8,128)(2,1)S(1)} async-done(((bf16[16,32,128]{2,1,0:T(8,128)(2,1)}), bf16[16,32,128]{2,1,0:T(8,128)(2,1)S(1)}, u32[]{:S(2)}, u32[]{:S(2)}) %all-to-all-start.7) | async-done | bytes 131104 | tf_op jit(solution)/shard_map/all_to_all | solution.py:44
  204.7 0.7 broadcast_in_dim.65
  205.5 6.8 %all-to-all-start.8 = ((bf16[16,2,32,128]{3,2,1,0:T(8,128)(2,1)}), bf16[16,2,32,128]{3,2,1,0:T(8,128)(2,1)S(1)}, u32[]{:S(2)}, u32[]{:S(2)}) async-start(bf16[16,2,32,128]{3,2,1,0:T(8,128)(2,1)} %bitcast.34), calls=%async_computation.8 | async-start | bytes 524288 | tf_op jit(solution)/shard_map/all_to_all | solution.py:44
  213.0 5.9 %all-to-all-done.8 = bf16[16,2,32,128]{3,2,1,0:T(8,128)(2,1)S(1)} async-done(((bf16[16,2,32,128]{3,2,1,0:T(8,128)(2,1)}), bf16[16,2,32,128]{3,2,1,0:T(8,128)(2,1)S(1)}, u32[]{:S(2)}, u32[]{:S(2)}) %all-to-all-start.8) | async-done | bytes 262176 | tf_op jit(solution)/shard_map/all_to_all | solution.py:44
  219.8 0.7 copy.64
  220.5 0.7 copy.65
  (72 shorter events, 4.9 us)
Async XLA Ops:
  3.9 8.6 %collective-permute-start.11 = (bf16[64,2048]{1,0:T(8,128)(2,1)S(1)}, bf16[64,2048]{1,0:T(8,128)(2,1)S(1)}, u32[]{:S(2)}, u32[]{:S(2)}) collective-permute-start(bf16[64,2048]{1,0:T(8,128)(2,1)S(1)} %slice.37), channel_id=1, source_target_pairs={{0,6},{2,0},{4,2},{6,4},{1,7},{3,1},{5,3},{7,5},{8,14},{10,8},{12,... | collective-permute-start | bytes 786440 | tf_op jit(solution)/shard_map/ppermute | solution.py:36
  7.6 13.3 %collective-permute-start.12 = (bf16[64,2048]{1,0:T(8,128)(2,1)S(1)}, bf16[64,2048]{1,0:T(8,128)(2,1)S(1)}, u32[]{:S(2)}, u32[]{:S(2)}) collective-permute-start(bf16[64,2048]{1,0:T(8,128)(2,1)S(1)} %slice.37), channel_id=1, source_target_pairs={{0,2},{2,4},{4,6},{6,0},{1,3},{3,5},{5,7},{7,1},{8,10},{10,12},{12... | collective-permute-start | bytes 786440 | tf_op jit(solution)/shard_map/ppermute | solution.py:36
  12.6 8.3 %collective-permute-start.13 = (bf16[64,2048]{1,0:T(8,128)(2,1)S(1)}, bf16[64,2048]{1,0:T(8,128)(2,1)S(1)}, u32[]{:S(2)}, u32[]{:S(2)}) collective-permute-start(bf16[64,2048]{1,0:T(8,128)(2,1)S(1)} %collective-permute-done.11), channel_id=1, source_target_pairs={{0,6},{2,0},{4,2},{6,4},{1,7},{3,1},{5,3},{7,5},{8,14},{10,8},{12,... | collective-permute-start | bytes 786440 | tf_op jit(solution)/shard_map/ppermute | solution.py:36
  16.0 10.5 %copy-start.7 = (f32[32,256]{1,0:T(8,128)S(1)}, f32[32,256]{1,0:T(8,128)}, u32[]{:S(2)}) copy-start(f32[32,256]{1,0:T(8,128)} %param.10) | copy-start | bytes 98308
  16.0 22.2 %collective-permute-start = (bf16[192,2048]{1,0:T(8,128)(2,1)S(1)}, bf16[192,2048]{1,0:T(8,128)(2,1)}, u32[]{:S(2)}, u32[]{:S(2)}) collective-permute-start(bf16[192,2048]{1,0:T(8,128)(2,1)S(1)} %slice.34), channel_id=1, source_target_pairs={{0,0},{1,64},{64,1},{65,65},{2,2},{3,66},{66,3},{67,67},{4,4},{5,6... | collective-permute-start | bytes 2359304 | tf_op jit(solution)/shard_map/ppermute | solution.py:56
  21.9 40.1 %collective-permute-start.14 = (bf16[256,2048]{1,0:T(8,128)(2,1)}, bf16[256,2048]{1,0:T(8,128)(2,1)}, u32[]{:S(2)}, u32[]{:S(2)}) collective-permute-start(bf16[256,2048]{1,0:T(8,128)(2,1)} %pad_maximum_fusion), channel_id=1, source_target_pairs={{0,0},{1,64},{64,1},{65,65},{2,2},{3,66},{66,3},{67,67},{4,4},{5,6... | collective-permute-start | bytes 3145736 | tf_op jit(solution)/shard_map/ppermute | solution.py:56
  27.3 18.6 %all-to-all-start = ((f32[16,32,128]{2,1,0:T(8,128)}), f32[16,32,128]{2,1,0:T(8,128)S(1)}, u32[]{:S(2)}, u32[]{:S(2)}) async-start(f32[16,32,128]{2,1,0:T(8,128)} %bitcast.1), calls=%async_computation | async-start | bytes 524288 | tf_op jit(solution)/shard_map/all_to_all | solution.py:44
  38.3 16.7 %copy-start.2 = (bf16[1,256,1024]{2,1,0:T(8,128)(2,1)S(1)}, bf16[1,256,1024]{2,1,0:T(8,128)(2,1)}, u32[]{:S(2)}) copy-start(bf16[1,256,1024]{2,1,0:T(8,128)(2,1)} %param.8) | copy-start | bytes 1572868
  38.3 24.2 %collective-permute-start.4 = (bf16[192,2048]{1,0:T(8,128)(2,1)}, bf16[192,2048]{1,0:T(8,128)(2,1)S(1)}, u32[]{:S(2)}, u32[]{:S(2)}) collective-permute-start(bf16[192,2048]{1,0:T(8,128)(2,1)} %collective-permute-done.refs_0_), channel_id=1, source_target_pairs={{0,2},{2,4},{4,6},{6,0},{1,3},{3,5},{5,7},{7,1},{8,10},{10,12},{12... | collective-permute-start | bytes 2359304 | tf_op jit(solution)/shard_map/ppermute | solution.py:36
  39.7 23.6 %collective-permute-start.2 = (bf16[192,2048]{1,0:T(8,128)(2,1)}, bf16[192,2048]{1,0:T(8,128)(2,1)S(1)}, u32[]{:S(2)}, u32[]{:S(2)}) collective-permute-start(bf16[192,2048]{1,0:T(8,128)(2,1)} %collective-permute-done.refs_0_), channel_id=1, source_target_pairs={{0,6},{2,0},{4,2},{6,4},{1,7},{3,1},{5,3},{7,5},{8,14},{10,8},{12,... | collective-permute-start | bytes 2359304 | tf_op jit(solution)/shard_map/ppermute | solution.py:36
  46.8 23.2 %all-to-all-start.2 = ((bf16[8,256,128]{2,1,0:T(8,128)(2,1)}), bf16[8,256,128]{2,1,0:T(8,128)(2,1)S(1)}, u32[]{:S(2)}, u32[]{:S(2)}) async-start(bf16[8,256,128]{2,1,0:T(8,128)(2,1)} %broadcast_in_dim.32), calls=%async_computation.2 | async-start | bytes 1048576 | tf_op jit(solution)/shard_map/all_to_all | solution.py:44
  55.5 13.7 %collective-permute-start.1 = (bf16[8,256,128]{2,1,0:T(8,128)(2,1)S(1)}, bf16[8,256,128]{2,1,0:T(8,128)(2,1)S(1)}, u32[]{:S(2)}, u32[]{:S(2)}) collective-permute-start(bf16[8,256,128]{2,1,0:T(8,128)(2,1)S(1)} %bitcast.96), channel_id=1, source_target_pairs={{0,0},{1,64},{64,1},{65,65},{2,2},{3,66},{66,3},{67,67},{4,4},{5,6... | collective-permute-start | bytes 1572872 | tf_op jit(solution)/shard_map/ppermute | solution.py:56
  61.9 15.7 %collective-permute-start.10 = (bf16[192,2048]{1,0:T(8,128)(2,1)}, bf16[192,2048]{1,0:T(8,128)(2,1)}, u32[]{:S(2)}, u32[]{:S(2)}) collective-permute-start(bf16[192,2048]{1,0:T(8,128)(2,1)} %collective-permute-done.refs_0_), channel_id=1, source_target_pairs={{0,64},{64,0},{1,65},{65,1},{2,66},{66,2},{3,67},{67,3},{4,68},{68... | collective-permute-start | bytes 2359304 | tf_op jit(solution)/shard_map/ppermute | solution.py:36
  62.0 29.4 %collective-permute-start.15 = (bf16[256,2048]{1,0:T(8,128)(2,1)}, bf16[256,2048]{1,0:T(8,128)(2,1)}, u32[]{:S(2)}, u32[]{:S(2)}) collective-permute-start(bf16[256,2048]{1,0:T(8,128)(2,1)} %collective-permute-done.14.refs_2_), channel_id=1, source_target_pairs={{0,64},{64,0},{1,65},{65,1},{2,66},{66,2},{3,67},{67,3},{4,68},{68... | collective-permute-start | bytes 3145736 | tf_op jit(solution)/shard_map/ppermute | solution.py:36
  63.4 16.9 %collective-permute-start.5 = (bf16[128,2048]{1,0:T(8,128)(2,1)}, bf16[128,2048]{1,0:T(8,128)(2,1)}, u32[]{:S(2)}, u32[]{:S(2)}) collective-permute-start(bf16[128,2048]{1,0:T(8,128)(2,1)} %slice.36), channel_id=1, source_target_pairs={{0,2},{2,4},{4,6},{6,0},{1,3},{3,5},{5,7},{7,1},{8,10},{10,12},{12... | collective-permute-start | bytes 1572872 | tf_op jit(solution)/shard_map/ppermute | solution.py:36
  63.4 33.2 %collective-permute-start.8 = (bf16[192,2048]{1,0:T(8,128)(2,1)S(1)}, bf16[192,2048]{1,0:T(8,128)(2,1)S(1)}, u32[]{:S(2)}, u32[]{:S(2)}) collective-permute-start(bf16[192,2048]{1,0:T(8,128)(2,1)S(1)} %collective-permute-done.2.refs_0_.refs_4_), channel_id=1, source_target_pairs={{0,64},{64,0},{1,65},{65,1},{2,66},{66,2},{3,67},{67,3},{4,68},{68... | collective-permute-start | bytes 2359304 | tf_op jit(solution)/shard_map/ppermute | solution.py:36
  69.2 0.8 copy-start.3
  69.2 27.4 %collective-permute-start.9 = (bf16[192,2048]{1,0:T(8,128)(2,1)S(1)}, bf16[192,2048]{1,0:T(8,128)(2,1)}, u32[]{:S(2)}, u32[]{:S(2)}) collective-permute-start(bf16[192,2048]{1,0:T(8,128)(2,1)S(1)} %collective-permute-done.4.refs_2_.refs_6_), channel_id=1, source_target_pairs={{0,64},{64,0},{1,65},{65,1},{2,66},{66,2},{3,67},{67,3},{4,68},{68... | collective-permute-start | bytes 2359304 | tf_op jit(solution)/shard_map/ppermute | solution.py:36
  70.0 21.5 %all-to-all-start.1 = ((bf16[8,256,128]{2,1,0:T(8,128)(2,1)}), bf16[8,256,128]{2,1,0:T(8,128)(2,1)S(1)}, u32[]{:S(2)}, u32[]{:S(2)}) async-start(bf16[8,256,128]{2,1,0:T(8,128)(2,1)} %copy-done.3), calls=%async_computation.1 | async-start | bytes 1048576 | tf_op jit(solution)/shard_map/all_to_all | solution.py:44
  77.6 13.0 %collective-permute-start.3 = (bf16[64,2048]{1,0:T(8,128)(2,1)}, bf16[64,2048]{1,0:T(8,128)(2,1)}, u32[]{:S(2)}, u32[]{:S(2)}) collective-permute-start(bf16[64,2048]{1,0:T(8,128)(2,1)} %slice.35), channel_id=1, source_target_pairs={{0,6},{2,0},{4,2},{6,4},{1,7},{3,1},{5,3},{7,5},{8,14},{10,8},{12,... | collective-permute-start | bytes 786440 | tf_op jit(solution)/shard_map/ppermute | solution.py:36
  80.2 20.2 %collective-permute-start.7 = (bf16[128,2048]{1,0:T(8,128)(2,1)}, bf16[128,2048]{1,0:T(8,128)(2,1)}, u32[]{:S(2)}, u32[]{:S(2)}) collective-permute-start(bf16[128,2048]{1,0:T(8,128)(2,1)} %collective-permute-done.5.refs_1_.refs_9_), channel_id=1, source_target_pairs={{0,64},{64,0},{1,65},{65,1},{2,66},{66,2},{3,67},{67,3},{4,68},{68... | collective-permute-start | bytes 1572872 | tf_op jit(solution)/shard_map/ppermute | solution.py:36
  90.6 9.8 %collective-permute-start.6 = (bf16[64,2048]{1,0:T(8,128)(2,1)}, bf16[64,2048]{1,0:T(8,128)(2,1)}, u32[]{:S(2)}, u32[]{:S(2)}) collective-permute-start(bf16[64,2048]{1,0:T(8,128)(2,1)} %collective-permute-done.3.refs_0_.refs_8_), channel_id=1, source_target_pairs={{0,64},{64,0},{1,65},{65,1},{2,66},{66,2},{3,67},{67,3},{4,68},{68... | collective-permute-start | bytes 786440 | tf_op jit(solution)/shard_map/ppermute | solution.py:36
  106.0 18.0 %copy-start.10 = (s32[1,64]{1,0:T(1,128)S(1)}, s32[1,64]{1,0:T(1,128)}, u32[]{:S(2)}) copy-start(s32[1,64]{1,0:T(1,128)} %param.9) | copy-start | bytes 772
  119.4 21.8 %all-to-all-start.4 = ((bf16[8,256,128]{2,1,0:T(8,128)(2,1)}), bf16[8,256,128]{2,1,0:T(8,128)(2,1)}, u32[]{:S(2)}, u32[]{:S(2)}) async-start(bf16[8,256,128]{2,1,0:T(8,128)(2,1)} %shard_map.104), calls=%async_computation.4 | async-start | bytes 1048576 | tf_op jit(solution)/shard_map/all_to_all | solution.py:44
  125.3 2.3 %collective-permute-start.16 = (f32[1]{0:T(128)}, f32[1]{0:T(128)}, u32[]{:S(2)}, u32[]{:S(2)}) collective-permute-start(f32[1]{0:T(128)} %bitcast.19), channel_id=1, source_target_pairs={{0,64},{64,0},{1,65},{65,1},{2,66},{66,2},{3,67},{67,3},{4,68},{68... | collective-permute-start | bytes 20 | tf_op jit(solution)/shard_map/ppermute | solution.py:36
  129.2 13.8 %copy-start = (f32[8,2,32,128]{3,2,1,0:T(8,128)}, f32[8,2,32,128]{3,2,1,0:T(8,128)S(1)}, u32[]{:S(2)}) copy-start(f32[8,2,32,128]{3,2,1,0:T(8,128)S(1)} %dynamic-slice_bitcast_fusion) | copy-start | bytes 786436
  171.0 18.1 %copy-start.1 = (f32[8,2,32,128]{3,2,1,0:T(8,128)S(1)}, f32[8,2,32,128]{3,2,1,0:T(8,128)}, u32[]{:S(2)}) copy-start(f32[8,2,32,128]{3,2,1,0:T(8,128)} %copy-done) | copy-start | bytes 786436
  189.0 9.0 %copy-start.6 = (bf16[256,128]{1,0:T(8,128)(2,1)S(1)}, bf16[256,128]{1,0:T(8,128)(2,1)}, u32[]{:S(2)}) copy-start(bf16[256,128]{1,0:T(8,128)(2,1)} %get-tuple-element.20) | copy-start | bytes 196612
  189.3 23.0 %copy-start.4 = (f32[1,32,1024]{2,1,0:T(8,128)S(1)}, f32[1,32,1024]{2,1,0:T(8,128)}, u32[]{:S(2)}) copy-start(f32[1,32,1024]{2,1,0:T(8,128)} %param.13) | copy-start | bytes 393220
  189.3 23.0 %copy-start.5 = (f32[1,32,1024]{2,1,0:T(8,128)S(1)}, f32[1,32,1024]{2,1,0:T(8,128)}, u32[]{:S(2)}) copy-start(f32[1,32,1024]{2,1,0:T(8,128)} %param.12) | copy-start | bytes 393220
  190.0 14.7 %all-to-all-start.7 = ((bf16[16,32,128]{2,1,0:T(8,128)(2,1)}), bf16[16,32,128]{2,1,0:T(8,128)(2,1)S(1)}, u32[]{:S(2)}, u32[]{:S(2)}) async-start(bf16[16,32,128]{2,1,0:T(8,128)(2,1)} %bitcast.29), calls=%async_computation.7 | async-start | bytes 262144 | tf_op jit(solution)/shard_map/all_to_all | solution.py:44
  197.9 14.5 %copy-start.8 = (f32[32,256]{1,0:T(8,128)S(1)}, f32[32,256]{1,0:T(8,128)}, u32[]{:S(2)}) copy-start(f32[32,256]{1,0:T(8,128)} %param.10) | copy-start | bytes 98308
  197.9 14.5 %copy-start.9 = (f32[32,256]{1,0:T(8,128)S(1)}, f32[32,256]{1,0:T(8,128)}, u32[]{:S(2)}) copy-start(f32[32,256]{1,0:T(8,128)} %param.11) | copy-start | bytes 98308
  205.5 13.4 %all-to-all-start.8 = ((bf16[16,2,32,128]{3,2,1,0:T(8,128)(2,1)}), bf16[16,2,32,128]{3,2,1,0:T(8,128)(2,1)S(1)}, u32[]{:S(2)}, u32[]{:S(2)}) async-start(bf16[16,2,32,128]{3,2,1,0:T(8,128)(2,1)} %bitcast.34), calls=%async_computation.8 | async-start | bytes 524288 | tf_op jit(solution)/shard_map/all_to_all | solution.py:44

commit v3 on v2

v3 whole, which is shorter than its diff:
```python
import functools

import jax
import jax.numpy as jnp
from jax import lax
from jax.experimental import pallas as pl
from jax.experimental.pallas import tpu as pltpu
from jax.sharding import Mesh
from jax.sharding import PartitionSpec as P

D = 2048
STEPS = 2
PRIOR = 1000
BLOCK = 128
TURN = [(0, 0), (1, 2), (2, 1), (3, 3)]
WIDE = 2 * BLOCK
PEERS = [[z * 4 + (colour + 2 * z) % 4 for z in range(8)] for colour in range(4)]


def adam_moments(first, second, grad):
    return 0.9 * first + 0.1 * grad, 0.95 * second + 0.05 * grad * grad


def adam_update(param, first, second, step):
    upd = first / (1.0 - 0.9**step) / (jnp.sqrt(second / (1.0 - 0.95**step)) + 1e-08)
    return param - 0.1 * (upd + 0.1 * param)


def shift(x, axis, by):
    size = lax.axis_size(axis)
    return lax.ppermute(x, axis, [(i, (i + by) % size) for i in range(size)])


def other_core(x):
    return shift(x, "c", 1)


def exchange(x, axes):
    return lax.all_to_all(x, axes, 0, 0, tiled=True)


def pick(x, index, axis):
    return lax.dynamic_index_in_dim(x, index, axis, keepdims=False)


def after(x, *earlier):
    return lax.optimization_barrier((x, *earlier))[0]


def turned(x):
    return lax.ppermute(x, ("c", "x"), TURN)


def up(x):
    return shift(x, ("yh", "yl"), 1)


def down(x):
    return shift(x, ("yh", "yl"), -1)


def product_kernel(layout, last, core, weights, *refs):
    count = len(layout)
    blocks, refs = refs[:count], refs[count:]
    earlier, out, held, goals, total, sems = refs if len(refs) == 6 else (None, *refs)
    copies, row = [], 0
    for at, (rows, inputs_at, goals_at) in enumerate(layout):
        half = pl.multiple_of(goals_at + core[0] * BLOCK, BLOCK)
        sources = blocks[at].at[:, pl.ds(inputs_at, D)], blocks[at].at[:, pl.ds(half, BLOCK)]
        here = pl.ds(row, rows)
        for kind, (source, target) in enumerate(zip(sources, (held, goals))):
            copy = pltpu.make_async_copy(source, target.at[here], sems.at[kind, at])
            copy.start()
            copies.append(copy)
        row += rows
    if earlier is not None:
        total[...] = earlier[...]
    row = at = 0
    while at < count:
        size = 0
        while size < 512:
            copies[2 * at].wait()
            copies[2 * at + 1].wait()
            size += layout[at][0]
            at += 1
        inputs = held[row : row + size]
        goal = goals[row : row + size].astype(jnp.float32)
        outputs = jnp.dot(inputs, weights[...], preferred_element_type=jnp.float32)
        resid = (outputs * D ** (-0.5) - goal).astype(jnp.bfloat16)
        grad = lax.dot_general(
            resid, inputs, (((0,), (0,)), ((), ())), preferred_element_type=jnp.float32
        )
        if row == 0 and earlier is None:
            total[...] = grad
        else:
            total[...] += grad
        row += size
    if last:
        for z in range(8):
            out[z] = total[:, z * 256 : (z + 1) * 256].T.astype(jnp.bfloat16)
    else:
        out[...] = total[...]


def product(parts, core, weights, earlier=None, last=False):
    blocks = [block for block, _, _ in parts]
    layout = [(block.shape[0], *places) for block, *places in parts]
    rows = sum(block.shape[0] for block in blocks)
    whole = pl.BlockSpec(memory_space=pltpu.VMEM)
    args = [core, weights, *blocks]
    specs = [pl.BlockSpec(memory_space=pltpu.SMEM), whole]
    specs += [pl.BlockSpec(memory_space=pl.ANY)] * len(blocks)
    if earlier is not None:
        args.append(earlier)
        specs.append(whole)
    shape = ((8, 256, BLOCK), jnp.bfloat16) if last else ((BLOCK, D), jnp.float32)
    return pl.pallas_call(
        functools.partial(product_kernel, layout, last),
        out_shape=jax.ShapeDtypeStruct(*shape),
        in_specs=specs,
        out_specs=whole,
        scratch_shapes=[
            pltpu.VMEM((rows, D), jnp.bfloat16),
            pltpu.VMEM((rows, BLOCK), jnp.bfloat16),
            pltpu.VMEM((BLOCK, D), jnp.float32),
            pltpu.SemaphoreType.DMA((2, len(blocks))),
        ],
        compiler_params=pltpu.CompilerParams(vmem_limit_bytes=40 * 2**20),
        cost_estimate=pl.CostEstimate(
            flops=8 * rows * D * BLOCK, bytes_accessed=2 * rows * D, transcendentals=0
        ),
    )(*args)


def among_peers(x):
    axes = ("z", "yh", "yl")
    return lax.all_to_all(x, axes, 0, 0, axis_index_groups=PEERS, tiled=True)


def gathered(param):
    weights = jnp.broadcast_to(param.astype(jnp.bfloat16)[None], (8, 256, BLOCK))
    return among_peers(weights).reshape(D, BLOCK)


def reduced(grad):
    return jnp.sum(among_peers(grad).astype(jnp.float32), 0)


def per_device(tokens, targets, lengths, outer_param, outer_mom, first_mom, second_mom):
    c, x, z = (lax.axis_index(axis) for axis in ("c", "x", "z"))
    h, y = lax.axis_index("h"), lax.axis_index(("yh", "yl"))
    odd = z % 2
    colour = (y + 2 * odd) % 4
    core = c.reshape(1).astype(jnp.int32)

    own = lax.axis_index(("z", "yh", "yl", "x"))
    valid = lax.iota(jnp.int32, tokens.shape[1]) < pick(lengths[0], own, 0)
    masked = jnp.where(valid[:, None], tokens[0], jnp.zeros((), tokens.dtype))

    goals = targets[0].reshape(256, 2, 2, 2, BLOCK).transpose(1, 3, 0, 2, 4)
    goals = goals.reshape(4, 256, WIDE)
    goals = [pick(goals, (colour + away) % 4, 0) for away in range(4)]
    mine = jnp.concatenate([goals[1], masked, goals[3], goals[2], goals[0]], 1)
    mine = turned(mine)
    from_below = up(mine[:, : D + WIDE])
    from_above = down(mine[:, WIDE : D + 2 * WIDE])
    half = mine.shape[0] // 2
    before = shift(mine[:half, WIDE : D + 3 * WIDE], "z", 1)
    behind = shift(mine[half:, WIDE : D + 3 * WIDE], "z", -1)

    start = jnp.moveaxis(outer_param.astype(jnp.bfloat16).reshape(32, 2, BLOCK), 1, 0)
    start = jnp.broadcast_to(start[None, None, :, None], (2, 2, 2, 2, 32, BLOCK))
    start = exchange(start.reshape(16, 32, BLOCK), ("h", "yh", "yl", "x"))
    start = start.reshape(2, 256, BLOCK)
    here = pick(start, colour // 2, 0)
    there = pick(start, 1 - colour // 2, 0)
    weights = jnp.where(
        (jnp.arange(8) % 2 == odd)[:, None, None], here[None], there[None]
    )
    weights = exchange(weights, "z").reshape(D, BLOCK)
    start = here.astype(jnp.float32)

    count = (jnp.sum(lengths[0]) // 128).astype(jnp.bfloat16)
    moments = jnp.concatenate([first_mom[0], second_mom[0]], 0).astype(jnp.bfloat16)
    moments = moments.reshape(64, 2, 2, 2, BLOCK)
    moments = jnp.where(odd == 1, moments[:, ::-1], moments).transpose(2, 1, 3, 0, 4)
    moments = jnp.concatenate(
        [moments, jnp.broadcast_to(count, (2, 2, 2, 16, BLOCK))], 3
    )
    moments = jnp.broadcast_to(moments[:, :, :, None], (2, 2, 2, 2, 80, BLOCK))
    moments = exchange(
        after(moments.reshape(16, 80, BLOCK), mine), ("c", "yh", "yl", "x")
    )
    moments = pick(moments.reshape(2, 8, 80, BLOCK), x, 0)
    weights, moments = lax.optimization_barrier((weights, moments))
    first = moments[:, :32].reshape(256, BLOCK).astype(jnp.float32)
    second = moments[:, 32:64].reshape(256, BLOCK).astype(jnp.float32)
    coef = D ** (-0.5) / (128.0 * moments[0, 64, 0].astype(jnp.float32))

    near = [(block, WIDE, D + 3 * WIDE) for block in (mine, other_core(mine))]
    near += [
        (block, 0, D + WIDE)
        for block in (before, behind, other_core(before), other_core(behind))
    ]
    sides = [(block, WIDE, 0) for block in (from_below, other_core(from_below))]
    sides += [(block, 0, D) for block in (from_above, other_core(from_above))]
    grad = product(near, core, weights)
    grad = product(sides, core, weights, grad, last=True)

    grad = reduced(grad) * coef
    grads = [grad]
    first, second = adam_moments(first, second, grad)
    param = adam_update(start, first, second, PRIOR + 1)

    grad = product(near + sides, core, gathered(param), last=True)
    grad = reduced(grad) * coef
    grads.append(grad)
    first, second = adam_moments(first, second, grad)
    param = adam_update(param, first, second, PRIOR + 2)

    leaving = jnp.stack([start - param, *grads]).astype(jnp.bfloat16)
    leaving = jnp.moveaxis(leaving.reshape(3, 8, 32, BLOCK), 1, 0)
    leaving = jnp.broadcast_to(leaving[None], (4, 8, 3, 32, BLOCK))
    arrived = exchange(leaving.reshape(32, 3, 32, BLOCK), ("h", "c", "yh", "yl", "x"))
    arrived = arrived.reshape(2, 2, 2, 2, 2, 3, 32, BLOCK)

    change = pick(pick(arrived[:, :, :, :, :, 0], (h + odd) % 2, 2), c, 1)
    change = jnp.sum(change.astype(jnp.float32), (0, 2))
    pseudo = jnp.moveaxis(change, 0, 1).reshape(32, WIDE) / 4
    new_mom = 0.9 * outer_mom + pseudo
    new_param = outer_param - 0.7 * (pseudo + 0.9 * new_mom)

    home = pick(pick(arrived[:, :, :, :, :, 1:], c, 4), h, 0)
    home = jnp.where(odd == 1, home[:, ::-1], home)
    home = home.transpose(3, 4, 1, 0, 2, 5).reshape(2, 32, 8 * BLOCK)
    first, second = first_mom[0], second_mom[0]
    for step in range(STEPS):
        first, second = adam_moments(first, second, home[step].astype(jnp.float32))
    return (new_param, new_mom, first[None], second[None])


def solution(mesh):
    fine = Mesh(
        mesh.devices.reshape(2, 2, 8, 2, 2, 2), ("h", "c", "z", "yh", "yl", "x")
    )
    group, fsdp = ("h", "c"), ("z", "yh", "yl", "x")
    in_specs = (
        P(group, fsdp, None),
        P(group, fsdp, None),
        P(group, None),
        P(fsdp, group),
        P(fsdp, group),
        P(group, fsdp, None),
        P(group, fsdp, None),
    )
    out_specs = (
        P(fsdp, group),
        P(fsdp, group),
        P(group, fsdp, None),
        P(group, fsdp, None),
    )
    return jax.shard_map(
        per_device, mesh=fine, in_specs=in_specs, out_specs=out_specs, check_vma=False
    )
```

time: 223 us -> 194 us (0.87)
  blocking collectives: 49.3 us -> 17.1 us
  starting transfers between devices: 78.1 us -> 59.8 us
  waiting for transfers between devices: 48 us -> 66.2 us
  local copies, waits for them, and re-layouts: 11.2 us -> 16.2 us
  Pallas kernels: 23.1 us -> 20.1 us
    all_to_all x3 -> x1, blocking collectives: 49.3 us -> 17.1 us  [among_peers(): return lax.all_to_all(x, axes, 0, 0, axis_index_groups=PEERS, tiled=True)]
    all_to_all x0 -> x2, waiting for transfers between devices: none -> 23.9 us  [among_peers(): return lax.all_to_all(x, axes, 0, 0, axis_index_groups=PEERS, tiled=True)]
    ppermute x14 -> x9, waiting for transfers between devices: 13 us -> 0.08 us  [shift(): return lax.ppermute(x, axis, [(i, (i + by) % size) for i in range(size)])]
    ppermute x3 -> x1, starting transfers between devices: 15.9 us -> 4.5 us  [turned(): return lax.ppermute(x, ('c', 'x'), TURN)]
    all_to_all x6 -> x4, starting transfers between devices: 45.3 us -> 34.7 us  [exchange(): return lax.all_to_all(x, axes, 0, 0, tiled=True)]
    all_to_all x0 -> x2, starting transfers between devices: none -> 9.38 us  [among_peers(): return lax.all_to_all(x, axes, 0, 0, axis_index_groups=PEERS, tiled=True)]
    ppermute x14 -> x9, starting transfers between devices: 16.9 us -> 11.2 us  [shift(): return lax.ppermute(x, axis, [(i, (i + by) % size) for i in range(size)])]
    ppermute x3 -> x1, waiting for transfers between devices: 5.7 us -> 11.2 us  [turned(): return lax.ppermute(x, ('c', 'x'), TURN)]
  transfers between devices with their start and end apart: 23 -> 16, of which waited for: 7 -> 7; matrix products, arithmetic and copies ran while one was open for 4% -> 6% of each run, Pallas kernels for 4% -> 2%
where the time goes in v3:
time: 194 us; the launch traced here: 193 us
  waiting for transfers between devices  66.2 us (34%)
  starting transfers between devices  59.8 us (31%)
  Pallas kernels  20.1 us (10%)
  blocking collectives  17.1 us (9%)
  local copies, waits for them, and re-layouts  16.2 us (8%)
  other arithmetic  8.74 us (5%)
  between operations  4.63 us (2%)
    all_to_all x4, starting transfers between devices, exchange(): return lax.all_to_all(x, axes, 0, 0, tiled=True)  34.7 us
    all_to_all x4, waiting for transfers between devices, exchange(): return lax.all_to_all(x, axes, 0, 0, tiled=True)  31 us
    all_to_all x2, waiting for transfers between devices, among_peers(): return lax.all_to_all(x, axes, 0, 0, axis_index_groups=PEERS, tiled=True)  23.9 us
    pallas_call x3, Pallas kernels, product(): pl.pallas_call(functools.partial(product_kernel, layout, last), out_shape...  20.1 us
    all_to_all x1, blocking collectives, among_peers(): return lax.all_to_all(x, axes, 0, 0, axis_index_groups=PEERS, tiled=True)  17.1 us
    ppermute x1, waiting for transfers between devices, turned(): return lax.ppermute(x, ('c', 'x'), TURN)  11.2 us
    ppermute x9, starting transfers between devices, shift(): return lax.ppermute(x, axis, [(i, (i + by) % size) for i in range(size)])  11.2 us
    all_to_all x2, starting transfers between devices, among_peers(): return lax.all_to_all(x, axes, 0, 0, axis_index_groups=PEERS, tiled=True)  9.38 us
  transfers between devices with their start and end apart: 16, of which 7 were waited for; matrix products, arithmetic and copies ran while one was open for 6% of the time, Pallas kernels for 2%

profile of v3, /device:TPU:1, one launch (start us, length us, event | category | flops | bytes accessed | tf_op | source)
XLA Modules:
  0.0 192.8 jit_solution(16283389325576267269)
XLA Ops:
  0.8 1.5 reshape_squeeze.3
  2.9 0.6 constant_dynamic-slice_fusion
  3.5 0.6 iota_compare_fusion
  4.2 0.7 bitcast_dynamic-update-slice_fusion.3
  4.9 1.3 fusion
  6.1 0.7 bitcast_dynamic-update-slice_fusion.2
  6.8 0.7 bitcast_dynamic-update-slice_fusion.1
  7.5 0.7 bitcast_dynamic-update-slice_fusion
  8.2 4.5 %collective-permute-start = (bf16[256,3072]{1,0:T(8,128)(2,1)}, bf16[256,3072]{1,0:T(8,128)(2,1)S(1)}, u32[]{:S(2)}, u32[]{:S(2)}) collective-permute-start(bf16[256,3072]{1,0:T(8,128)(2,1)} %bitcast_dynamic-update-slice_fusion), channel_id=1, source_target_pairs={{0,0},{1,64},{64,1},{65,65},{2,2},{3,66},{66,3},{67,67},{4,4},{5,6... | collective-permute-start | bytes 4718600 | tf_op jit(solution)/shard_map/ppermute | solution.py:51
  12.7 0.7 broadcast_in_dim.73
  13.4 6.5 %all-to-all-start = ((bf16[16,32,128]{2,1,0:T(8,128)(2,1)}), bf16[16,32,128]{2,1,0:T(8,128)(2,1)S(1)}, u32[]{:S(2)}, u32[]{:S(2)}) async-start(bf16[16,32,128]{2,1,0:T(8,128)(2,1)} %bitcast.1), calls=%async_computation | async-start | bytes 262144 | tf_op jit(solution)/shard_map/all_to_all | solution.py:39
  19.9 0.7 broadcast_multiply_fusion
  20.8 11.2 %collective-permute-done.refs_0_ = bf16[256,3072]{1,0:T(8,128)(2,1)S(1)} collective-permute-done((bf16[256,3072]{1,0:T(8,128)(2,1)}, bf16[256,3072]{1,0:T(8,128)(2,1)S(1)}, u32[]{:S(2)}, u32[]{:S(2)}) %collective-permute-start) | collective-permute-done | bytes 1572896 | tf_op jit(solution)/shard_map/ppermute | solution.py:51
  32.1 1.6 fusion.24
  33.7 1.3 collective-permute-start.1
  35.0 1.4 collective-permute-start.3
  36.7 1.2 fusion.23
  37.9 1.6 collective-permute-start.6
  39.5 3.9 %collective-permute-start.7 = (bf16[128,2560]{1,0:T(8,128)(2,1)}, bf16[128,2560]{1,0:T(8,128)(2,1)}, u32[]{:S(2)}, u32[]{:S(2)}) collective-permute-start(bf16[128,2560]{1,0:T(8,128)(2,1)} %get-tuple-element.24), channel_id=1, source_target_pairs={{0,56},{8,0},{16,8},{24,16},{32,24},{40,32},{48,40},{56,48},{1,57}... | collective-permute-start | bytes 1966088 | tf_op jit(solution)/shard_map/ppermute | solution.py:31
  43.5 0.6 reduce_sum.36
  46.8 0.8 broadcast_in_dim.79
  47.6 5.2 %all-to-all-start.2 = ((bf16[16,80,128]{2,1,0:T(8,128)(2,1)}), bf16[16,80,128]{2,1,0:T(8,128)(2,1)S(1)}, u32[]{:S(2)}, u32[]{:S(2)}) async-start(bf16[16,80,128]{2,1,0:T(8,128)(2,1)} %bitcast.7), calls=%async_computation.2 | async-start | bytes 655360 | tf_op jit(solution)/shard_map/all_to_all | solution.py:39
  53.1 0.3 collective-permute-start.4
  53.4 0.9 broadcast_select_fusion
  54.4 5.5 %all-to-all-done.2 = bf16[16,80,128]{2,1,0:T(8,128)(2,1)S(1)} async-done(((bf16[16,80,128]{2,1,0:T(8,128)(2,1)}), bf16[16,80,128]{2,1,0:T(8,128)(2,1)S(1)}, u32[]{:S(2)}, u32[]{:S(2)}) %all-to-all-start.2) | async-done | bytes 327712 | tf_op jit(solution)/shard_map/all_to_all | solution.py:39
  59.9 0.7 copy-done.4
  60.7 5.6 %all-to-all-start.1 = ((bf16[8,256,128]{2,1,0:T(8,128)(2,1)}), bf16[8,256,128]{2,1,0:T(8,128)(2,1)S(1)}, u32[]{:S(2)}, u32[]{:S(2)}) async-start(bf16[8,256,128]{2,1,0:T(8,128)(2,1)} %broadcast_select_fusion), calls=%async_computation.1 | async-start | bytes 1048576 | tf_op jit(solution)/shard_map/all_to_all | solution.py:39
  66.2 2.0 %collective-permute-start.8 = (bf16[128,2560]{1,0:T(8,128)(2,1)}, bf16[128,2560]{1,0:T(8,128)(2,1)}, u32[]{:S(2)}, u32[]{:S(2)}) collective-permute-start(bf16[128,2560]{1,0:T(8,128)(2,1)} %collective-permute-done.6.refs_2_), channel_id=1, source_target_pairs={{0,64},{64,0},{1,65},{65,1},{2,66},{66,2},{3,67},{67,3},{4,68},{68... | collective-permute-start | bytes 1966088 | tf_op jit(solution)/shard_map/ppermute | solution.py:31
  68.5 1.6 dynamic-slice_bitcast_fusion
  70.1 12.0 %all-to-all-done.1 = bf16[8,256,128]{2,1,0:T(8,128)(2,1)S(1)} async-done(((bf16[8,256,128]{2,1,0:T(8,128)(2,1)}), bf16[8,256,128]{2,1,0:T(8,128)(2,1)S(1)}, u32[]{:S(2)}, u32[]{:S(2)}) %all-to-all-start.1) | async-done | bytes 524320 | tf_op jit(solution)/shard_map/all_to_all | solution.py:39
  82.1 4.7 %shard_map.102.refs_4_ = f32[128,2048]{1,0:T(8,128)S(1)} custom-call(s32[1]{0:T(128)} %bitcast.18.core, bf16[2048,128]{1,0:T(8,128)(2,1)S(1)} %bitcast.102, bf16[256,3072]{1,0:T(8,128)(2,1)S(1)} %collective-permute-done.refs_0_, bf16[256,3072]{1,0:T(8,128)(2,1)} %collective-permute-done.5.refs_1_, bf16[128,2560]{1,0:T(8,128)(2,1)} %collective-permute-done.6.refs_2_, ...), custom_call_target="tpu_custom_call" | custom-call | flops 2147483648 | bytes 4194304 | tf_op jit(solution)/shard_map/pallas_call | solution.py:117
  86.9 5.6 %shard_map.103 = bf16[8,256,128]{2,1,0:T(8,128)(2,1)} custom-call(s32[1]{0:T(128)} %bitcast.18.core, bf16[2048,128]{1,0:T(8,128)(2,1)S(1)} %bitcast.103, bf16[256,2304]{1,0:T(8,128)(2,1)S(1)} %collective-permute-done.1.refs_0_.refs_6_, bf16[256,2304]{1,0:T(8,128)(2,1)} %collective-permute-done.2.refs_1_.refs_7_, ...), custom_call_target="tpu_custom_call" | custom-call | flops 2147483648 | bytes 4194304 | tf_op jit(solution)/shard_map/pallas_call | solution.py:117
  92.5 3.5 %all-to-all-start.3 = ((bf16[8,256,128]{2,1,0:T(8,128)(2,1)}), bf16[8,256,128]{2,1,0:T(8,128)(2,1)S(1)}, u32[]{:S(2)}, u32[]{:S(2)}) async-start(bf16[8,256,128]{2,1,0:T(8,128)(2,1)} %shard_map.103), calls=%async_computation.3 | async-start | bytes 1048576 | tf_op jit(solution)/shard_map/all_to_all | solution.py:137
  96.0 1.2 slice.40
  97.9 1.5 convert_multiply_fusion.1
  99.4 11.1 %all-to-all-done.3 = bf16[8,256,128]{2,1,0:T(8,128)(2,1)S(1)} async-done(((bf16[8,256,128]{2,1,0:T(8,128)(2,1)}), bf16[8,256,128]{2,1,0:T(8,128)(2,1)S(1)}, u32[]{:S(2)}, u32[]{:S(2)}) %all-to-all-start.3) | async-done | bytes 524320 | tf_op jit(solution)/shard_map/all_to_all | solution.py:137
  110.6 1.1 convert_bitcast_fusion
  111.7 17.1 %all_to_all.35 = bf16[8,256,128]{2,1,0:T(8,128)(2,1)S(1)} all-to-all(bf16[8,256,128]{2,1,0:T(8,128)(2,1)S(1)} %broadcast_in_dim.83), channel_id=1, replica_groups={{0,12,16,28,32,44,48,60},{2,14,18,30,34,46,50,62},{4,8,20,24,36,40,52,5..., dimensions={0} | all-to-all | bytes 1048576 | tf_op jit(solution)/shard_map/all_to_all | solution.py:137
  128.9 9.8 %shard_map.104 = bf16[8,256,128]{2,1,0:T(8,128)(2,1)} custom-call(s32[1]{0:T(128)} %bitcast.18.core, bf16[2048,128]{1,0:T(8,128)(2,1)S(1)} %bitcast.104, bf16[256,3072]{1,0:T(8,128)(2,1)S(1)} %collective-permute-done.refs_0_, bf16[256,3072]{1,0:T(8,128)(2,1)} %collective-permute-done.5.refs_1_, bf16[128,2560]{1,0:T(8,128)(2,1)} %collective-permute-done.6.refs_2_, ...), custom_call_target="tpu_custom_call" | custom-call | flops 4294967296 | bytes 8388608 | tf_op jit(solution)/shard_map/pallas_call | solution.py:117
  138.7 5.9 %all-to-all-start.5 = ((bf16[8,256,128]{2,1,0:T(8,128)(2,1)}), bf16[8,256,128]{2,1,0:T(8,128)(2,1)S(1)}, u32[]{:S(2)}, u32[]{:S(2)}) async-start(bf16[8,256,128]{2,1,0:T(8,128)(2,1)} %shard_map.104), calls=%async_computation.5 | async-start | bytes 1048576 | tf_op jit(solution)/shard_map/all_to_all | solution.py:137
  144.6 12.7 %all-to-all-done.5 = bf16[8,256,128]{2,1,0:T(8,128)(2,1)S(1)} async-done(((bf16[8,256,128]{2,1,0:T(8,128)(2,1)}), bf16[8,256,128]{2,1,0:T(8,128)(2,1)S(1)}, u32[]{:S(2)}, u32[]{:S(2)}) %all-to-all-start.5) | async-done | bytes 524320 | tf_op jit(solution)/shard_map/all_to_all | solution.py:137
  157.7 1.0 broadcast_in_dim.84
  158.7 17.4 %all-to-all-start.6 = ((bf16[32,3,32,128]{3,2,1,0:T(8,128)(2,1)}), bf16[32,3,32,128]{3,2,1,0:T(8,128)(2,1)S(1)}, u32[]{:S(2)}, u32[]{:S(2)}) async-start(bf16[32,3,32,128]{3,2,1,0:T(8,128)(2,1)} %bitcast.32), calls=%async_computation.6 | async-start | bytes 1572864 | tf_op jit(solution)/shard_map/all_to_all | solution.py:39
  176.2 13.5 %all-to-all-done.6 = bf16[32,3,32,128]{3,2,1,0:T(8,128)(2,1)S(1)} async-done(((bf16[32,3,32,128]{3,2,1,0:T(8,128)(2,1)}), bf16[32,3,32,128]{3,2,1,0:T(8,128)(2,1)S(1)}, u32[]{:S(2)}, u32[]{:S(2)}) %all-to-all-start.6) | async-done | bytes 786464 | tf_op jit(solution)/shard_map/all_to_all | solution.py:39
  190.2 0.6 fusion.14
  190.8 0.7 copy.68
  191.5 0.7 copy.69
  192.2 0.6 fusion.21
  (67 shorter events, 2.6 us)
Async XLA Ops:
  0.7 2.2 %copy-start.12 = (s32[1,64]{1,0:T(1,128)S(1)}, s32[1,64]{1,0:T(1,128)}, u32[]{:S(2)}) copy-start(s32[1,64]{1,0:T(1,128)} %param.9) | copy-start | bytes 772
  0.7 4.1 %copy-start.3 = (bf16[1,256,2048]{2,1,0:T(8,128)(2,1)S(1)}, bf16[1,256,2048]{2,1,0:T(8,128)(2,1)}, u32[]{:S(2)}) copy-start(bf16[1,256,2048]{2,1,0:T(8,128)(2,1)} %param.7) | copy-start | bytes 3145732
  4.2 8.5 %copy-start.9 = (f32[32,256]{1,0:T(8,128)S(1)}, f32[32,256]{1,0:T(8,128)}, u32[]{:S(2)}) copy-start(f32[32,256]{1,0:T(8,128)} %param.10) | copy-start | bytes 98308
  4.9 15.0 %copy-start.7 = (f32[1,32,1024]{2,1,0:T(8,128)S(1)}, f32[1,32,1024]{2,1,0:T(8,128)}, u32[]{:S(2)}) copy-start(f32[1,32,1024]{2,1,0:T(8,128)} %param.13) | copy-start | bytes 393220
  4.9 15.0 %copy-start.8 = (f32[1,32,1024]{2,1,0:T(8,128)S(1)}, f32[1,32,1024]{2,1,0:T(8,128)}, u32[]{:S(2)}) copy-start(f32[1,32,1024]{2,1,0:T(8,128)} %param.12) | copy-start | bytes 393220
  8.2 23.9 %collective-permute-start = (bf16[256,3072]{1,0:T(8,128)(2,1)}, bf16[256,3072]{1,0:T(8,128)(2,1)S(1)}, u32[]{:S(2)}, u32[]{:S(2)}) collective-permute-start(bf16[256,3072]{1,0:T(8,128)(2,1)} %bitcast_dynamic-update-slice_fusion), channel_id=1, source_target_pairs={{0,0},{1,64},{64,1},{65,65},{2,2},{3,66},{66,3},{67,67},{4,4},{5,6... | collective-permute-start | bytes 4718600 | tf_op jit(solution)/shard_map/ppermute | solution.py:51
  13.4 34.2 %all-to-all-start = ((bf16[16,32,128]{2,1,0:T(8,128)(2,1)}), bf16[16,32,128]{2,1,0:T(8,128)(2,1)S(1)}, u32[]{:S(2)}, u32[]{:S(2)}) async-start(bf16[16,32,128]{2,1,0:T(8,128)(2,1)} %bitcast.1), calls=%async_computation | async-start | bytes 262144 | tf_op jit(solution)/shard_map/all_to_all | solution.py:39
  33.7 19.1 %collective-permute-start.1 = (bf16[256,2304]{1,0:T(8,128)(2,1)}, bf16[256,2304]{1,0:T(8,128)(2,1)S(1)}, u32[]{:S(2)}, u32[]{:S(2)}) collective-permute-start(bf16[256,2304]{1,0:T(8,128)(2,1)} %get-tuple-element.27), channel_id=1, source_target_pairs={{0,2},{2,4},{4,6},{6,0},{1,3},{3,5},{5,7},{7,1},{8,10},{10,12},{12... | collective-permute-start | bytes 3538952 | tf_op jit(solution)/shard_map/ppermute | solution.py:31
  35.0 18.1 %collective-permute-start.3 = (bf16[256,2304]{1,0:T(8,128)(2,1)}, bf16[256,2304]{1,0:T(8,128)(2,1)}, u32[]{:S(2)}, u32[]{:S(2)}) collective-permute-start(bf16[256,2304]{1,0:T(8,128)(2,1)} %get-tuple-element.26), channel_id=1, source_target_pairs={{0,6},{2,0},{4,2},{6,4},{1,7},{3,1},{5,3},{7,5},{8,14},{10,8},{12,... | collective-permute-start | bytes 3538952 | tf_op jit(solution)/shard_map/ppermute | solution.py:31
  36.6 45.5 %collective-permute-start.5 = (bf16[256,3072]{1,0:T(8,128)(2,1)S(1)}, bf16[256,3072]{1,0:T(8,128)(2,1)}, u32[]{:S(2)}, u32[]{:S(2)}) collective-permute-start(bf16[256,3072]{1,0:T(8,128)(2,1)S(1)} %collective-permute-done.refs_0_), channel_id=1, source_target_pairs={{0,64},{64,0},{1,65},{65,1},{2,66},{66,2},{3,67},{67,3},{4,68},{68... | collective-permute-start | bytes 4718600 | tf_op jit(solution)/shard_map/ppermute | solution.py:31
  37.9 28.4 %collective-permute-start.6 = (bf16[128,2560]{1,0:T(8,128)(2,1)}, bf16[128,2560]{1,0:T(8,128)(2,1)}, u32[]{:S(2)}, u32[]{:S(2)}) collective-permute-start(bf16[128,2560]{1,0:T(8,128)(2,1)} %get-tuple-element.25), channel_id=1, source_target_pairs={{0,8},{8,16},{16,24},{24,32},{32,40},{40,48},{48,56},{56,0},{1,9},... | collective-permute-start | bytes 1966088 | tf_op jit(solution)/shard_map/ppermute | solution.py:31
  39.5 28.7 %collective-permute-start.7 = (bf16[128,2560]{1,0:T(8,128)(2,1)}, bf16[128,2560]{1,0:T(8,128)(2,1)}, u32[]{:S(2)}, u32[]{:S(2)}) collective-permute-start(bf16[128,2560]{1,0:T(8,128)(2,1)} %get-tuple-element.24), channel_id=1, source_target_pairs={{0,56},{8,0},{16,8},{24,16},{32,24},{40,32},{48,40},{56,48},{1,57}... | collective-permute-start | bytes 1966088 | tf_op jit(solution)/shard_map/ppermute | solution.py:31
  47.6 12.3 %copy-start.1 = (bf16[16,32,128]{2,1,0:T(8,128)(2,1)}, bf16[16,32,128]{2,1,0:T(8,128)(2,1)S(1)}, u32[]{:S(2)}) copy-start(bf16[16,32,128]{2,1,0:T(8,128)(2,1)S(1)} %all-to-all-done) | copy-start | bytes 393220
  47.6 12.3 %all-to-all-start.2 = ((bf16[16,80,128]{2,1,0:T(8,128)(2,1)}), bf16[16,80,128]{2,1,0:T(8,128)(2,1)S(1)}, u32[]{:S(2)}, u32[]{:S(2)}) async-start(bf16[16,80,128]{2,1,0:T(8,128)(2,1)} %bitcast.7), calls=%async_computation.2 | async-start | bytes 655360 | tf_op jit(solution)/shard_map/all_to_all | solution.py:39
  52.8 34.0 %collective-permute-start.2 = (bf16[256,2304]{1,0:T(8,128)(2,1)S(1)}, bf16[256,2304]{1,0:T(8,128)(2,1)}, u32[]{:S(2)}, u32[]{:S(2)}) collective-permute-start(bf16[256,2304]{1,0:T(8,128)(2,1)S(1)} %collective-permute-done.1.refs_0_.refs_6_), channel_id=1, source_target_pairs={{0,64},{64,0},{1,65},{65,1},{2,66},{66,2},{3,67},{67,3},{4,68},{68... | collective-permute-start | bytes 3538952 | tf_op jit(solution)/shard_map/ppermute | solution.py:31
  53.1 33.8 %collective-permute-start.4 = (bf16[256,2304]{1,0:T(8,128)(2,1)}, bf16[256,2304]{1,0:T(8,128)(2,1)}, u32[]{:S(2)}, u32[]{:S(2)}) collective-permute-start(bf16[256,2304]{1,0:T(8,128)(2,1)} %collective-permute-done.3.refs_2_.refs_8_), channel_id=1, source_target_pairs={{0,64},{64,0},{1,65},{65,1},{2,66},{66,2},{3,67},{67,3},{4,68},{68... | collective-permute-start | bytes 3538952 | tf_op jit(solution)/shard_map/ppermute | solution.py:31
  59.9 0.7 copy-start.4
  60.7 21.4 %all-to-all-start.1 = ((bf16[8,256,128]{2,1,0:T(8,128)(2,1)}), bf16[8,256,128]{2,1,0:T(8,128)(2,1)S(1)}, u32[]{:S(2)}, u32[]{:S(2)}) async-start(bf16[8,256,128]{2,1,0:T(8,128)(2,1)} %broadcast_select_fusion), calls=%async_computation.1 | async-start | bytes 1048576 | tf_op jit(solution)/shard_map/all_to_all | solution.py:39
  66.2 15.9 %collective-permute-start.8 = (bf16[128,2560]{1,0:T(8,128)(2,1)}, bf16[128,2560]{1,0:T(8,128)(2,1)}, u32[]{:S(2)}, u32[]{:S(2)}) collective-permute-start(bf16[128,2560]{1,0:T(8,128)(2,1)} %collective-permute-done.6.refs_2_), channel_id=1, source_target_pairs={{0,64},{64,0},{1,65},{65,1},{2,66},{66,2},{3,67},{67,3},{4,68},{68... | collective-permute-start | bytes 1966088 | tf_op jit(solution)/shard_map/ppermute | solution.py:31
  68.2 13.9 %collective-permute-start.9 = (bf16[128,2560]{1,0:T(8,128)(2,1)}, bf16[128,2560]{1,0:T(8,128)(2,1)}, u32[]{:S(2)}, u32[]{:S(2)}) collective-permute-start(bf16[128,2560]{1,0:T(8,128)(2,1)} %collective-permute-done.7.refs_3_), channel_id=1, source_target_pairs={{0,64},{64,0},{1,65},{65,1},{2,66},{66,2},{3,67},{67,3},{4,68},{68... | collective-permute-start | bytes 1966088 | tf_op jit(solution)/shard_map/ppermute | solution.py:31
  92.5 18.1 %all-to-all-start.3 = ((bf16[8,256,128]{2,1,0:T(8,128)(2,1)}), bf16[8,256,128]{2,1,0:T(8,128)(2,1)S(1)}, u32[]{:S(2)}, u32[]{:S(2)}) async-start(bf16[8,256,128]{2,1,0:T(8,128)(2,1)} %shard_map.103), calls=%async_computation.3 | async-start | bytes 1048576 | tf_op jit(solution)/shard_map/all_to_all | solution.py:137
  138.7 18.7 %copy-start = (f32[8,32,128]{2,1,0:T(8,128)S(1)}, f32[8,32,128]{2,1,0:T(8,128)}, u32[]{:S(2)}) copy-start(f32[8,32,128]{2,1,0:T(8,128)} %get-tuple-element.31) | copy-start | bytes 393220
  138.7 18.7 %copy-start.2 = (bf16[16,32,128]{2,1,0:T(8,128)(2,1)S(1)}, bf16[16,32,128]{2,1,0:T(8,128)(2,1)}, u32[]{:S(2)}) copy-start(bf16[16,32,128]{2,1,0:T(8,128)(2,1)} %copy-done.1) | copy-start | bytes 393220
  138.7 18.6 %all-to-all-start.5 = ((bf16[8,256,128]{2,1,0:T(8,128)(2,1)}), bf16[8,256,128]{2,1,0:T(8,128)(2,1)S(1)}, u32[]{:S(2)}, u32[]{:S(2)}) async-start(bf16[8,256,128]{2,1,0:T(8,128)(2,1)} %shard_map.104), calls=%async_computation.5 | async-start | bytes 1048576 | tf_op jit(solution)/shard_map/all_to_all | solution.py:137
  158.7 31.0 %all-to-all-start.6 = ((bf16[32,3,32,128]{3,2,1,0:T(8,128)(2,1)}), bf16[32,3,32,128]{3,2,1,0:T(8,128)(2,1)S(1)}, u32[]{:S(2)}, u32[]{:S(2)}) async-start(bf16[32,3,32,128]{3,2,1,0:T(8,128)(2,1)} %bitcast.32), calls=%async_computation.6 | async-start | bytes 1572864 | tf_op jit(solution)/shard_map/all_to_all | solution.py:39
  176.1 14.0 %copy-start.5 = (f32[1,32,1024]{2,1,0:T(8,128)S(1)}, f32[1,32,1024]{2,1,0:T(8,128)}, u32[]{:S(2)}) copy-start(f32[1,32,1024]{2,1,0:T(8,128)} %get-tuple-element.32) | copy-start | bytes 393220
  176.2 14.0 %copy-start.6 = (f32[1,32,1024]{2,1,0:T(8,128)S(1)}, f32[1,32,1024]{2,1,0:T(8,128)}, u32[]{:S(2)}) copy-start(f32[1,32,1024]{2,1,0:T(8,128)} %get-tuple-element.41) | copy-start | bytes 393220
  189.8 2.4 %copy-start.10 = (f32[32,256]{1,0:T(8,128)S(1)}, f32[32,256]{1,0:T(8,128)}, u32[]{:S(2)}) copy-start(f32[32,256]{1,0:T(8,128)} %param.10) | copy-start | bytes 98308
  189.8 2.4 %copy-start.11 = (f32[32,256]{1,0:T(8,128)S(1)}, f32[32,256]{1,0:T(8,128)}, u32[]{:S(2)}) copy-start(f32[32,256]{1,0:T(8,128)} %param.11) | copy-start | bytes 98308

commit v4 on v3

--- a/solution.py
+++ b/solution.py
@@ -57,6 +57,106 @@
 
 def down(x):
     return shift(x, ("yh", "yl"), -1)
+
+
+def place():
+    z, y = lax.axis_index("z"), lax.axis_index("yh") * 2 + lax.axis_index("yl")
+    odd = lax.rem(z, 2)
+    return z, y, odd, lax.rem(y + 2 * odd, 4)
+
+
+def prepare_kernel(lengths, tokens, targets, out):
+    z, y, _, colour = place()
+    length = lengths[0, (z * 4 + y) * 2 + lax.axis_index("x")]
+    valid = lax.broadcasted_iota(jnp.int32, tokens.shape[1:], 0) < length
+    inputs = tokens[0]
+    out[:, WIDE : WIDE + D] = jnp.where(valid, inputs, jnp.zeros_like(inputs))
+    for away, at in ((1, 0), (3, D + WIDE), (2, D + 2 * WIDE), (0, D + 3 * WIDE)):
+        wanted = lax.rem(colour + away, 4)
+        source = wanted // 2 * (2 * WIDE) + lax.rem(wanted, 2) * BLOCK
+        for core in range(2):
+            column = pl.multiple_of(source + core * WIDE, BLOCK)
+            out[:, at + core * BLOCK : at + (core + 1) * BLOCK] = targets[
+                0, :, pl.ds(column, BLOCK)
+            ]
+
+
+def prepare(lengths, tokens, targets):
+    whole = pl.BlockSpec(memory_space=pltpu.VMEM)
+    return pl.pallas_call(
+        prepare_kernel,
+        out_shape=jax.ShapeDtypeStruct((256, D + 4 * WIDE), jnp.bfloat16),
+        in_specs=[pl.BlockSpec(memory_space=pltpu.SMEM), whole, whole],
+        out_specs=whole,
+        compiler_params=pltpu.CompilerParams(vmem_limit_bytes=16 * 2**20),
+    )(lengths, tokens, targets)
+
+
+def pack_kernel(lengths, param, first, second, weights, moments):
+    _, _, odd, _ = place()
+    count = lax.fori_loop(0, lengths.shape[1], lambda i, t: t + lengths[0, i], 0)
+    count = (count // 128).astype(jnp.float32)
+    for slot in range(16):
+        core, yh, yl = slot // 8, slot // 4 % 2, slot // 2 % 2
+        half = slice(yl * BLOCK, (yl + 1) * BLOCK)
+        weights[slot] = param[:, half].astype(jnp.bfloat16)
+        column = lax.rem(yh + odd, 2) * (2 * WIDE) + core * WIDE + yl * BLOCK
+        columns = pl.ds(pl.multiple_of(column, BLOCK), BLOCK)
+        moments[slot, 0:32] = first[0, :, columns].astype(jnp.bfloat16)
+        moments[slot, 32:64] = second[0, :, columns].astype(jnp.bfloat16)
+        moments[slot, 64:80] = jnp.full((16, BLOCK), count).astype(jnp.bfloat16)
+
+
+def pack(lengths, param, first, second):
+    whole = pl.BlockSpec(memory_space=pltpu.VMEM)
+    return pl.pallas_call(
+        pack_kernel,
+        out_shape=[
+            jax.ShapeDtypeStruct((16, 32, BLOCK), jnp.bfloat16),
+            jax.ShapeDtypeStruct((16, 80, BLOCK), jnp.bfloat16),
+        ],
+        in_specs=[pl.BlockSpec(memory_space=pltpu.SMEM), whole, whole, whole],
+        out_specs=[whole, whole],
+        compiler_params=pltpu.CompilerParams(vmem_limit_bytes=16 * 2**20),
+    )(lengths, param, first, second)
+
+
+def finish_kernel(
+    arrived, param, mom, first, second, new_param, new_mom, new_first, new_second
+):
+    _, _, odd, _ = place()
+    h, c = lax.axis_index("h"), lax.axis_index("c")
+    for yl in range(2):
+        columns = slice(yl * BLOCK, (yl + 1) * BLOCK)
+        total = jnp.zeros((32, BLOCK), jnp.float32)
+        for group in range(4):
+            yh = lax.rem(h + odd, 2)
+            source = group // 2 * 16 + c * 8 + yh * 4 + yl * 2 + group % 2
+            total += arrived[source, 0].astype(jnp.float32)
+        pseudo = total / 4
+        momentum = 0.9 * mom[:, columns] + pseudo
+        new_mom[:, columns] = momentum
+        new_param[:, columns] = param[:, columns] - 0.7 * (pseudo + 0.9 * momentum)
+    for block in range(8):
+        fh, core, fl = block // 4, block // 2 % 2, block % 2
+        columns = slice(block * BLOCK, (block + 1) * BLOCK)
+        source = h * 16 + core * 8 + lax.rem(fh + odd, 2) * 4 + fl * 2 + c
+        moments = first[0, :, columns], second[0, :, columns]
+        for step in range(STEPS):
+            grad = arrived[source, 1 + step].astype(jnp.float32)
+            moments = adam_moments(*moments, grad)
+        new_first[0, :, columns], new_second[0, :, columns] = moments
+
+
+def finish(*arrays):
+    whole = pl.BlockSpec(memory_space=pltpu.VMEM)
+    return pl.pallas_call(
+        finish_kernel,
+        out_shape=[jax.ShapeDtypeStruct(a.shape, a.dtype) for a in arrays[1:]],
+        in_specs=[whole] * 5,
+        out_specs=[whole] * 4,
+        compiler_params=pltpu.CompilerParams(vmem_limit_bytes=16 * 2**20),
+    )(*arrays)
 
 
 def product_kernel(layout, last, core, weights, *refs):
@@ -147,30 +247,16 @@
 
 
 def per_device(tokens, targets, lengths, outer_param, outer_mom, first_mom, second_mom):
-    c, x, z = (lax.axis_index(axis) for axis in ("c", "x", "z"))
-    h, y = lax.axis_index("h"), lax.axis_index(("yh", "yl"))
-    odd = z % 2
-    colour = (y + 2 * odd) % 4
+    c, x = lax.axis_index("c"), lax.axis_index("x")
+    _, _, odd, colour = place()
     core = c.reshape(1).astype(jnp.int32)
 
-    own = lax.axis_index(("z", "yh", "yl", "x"))
-    valid = lax.iota(jnp.int32, tokens.shape[1]) < pick(lengths[0], own, 0)
-    masked = jnp.where(valid[:, None], tokens[0], jnp.zeros((), tokens.dtype))
-
-    goals = targets[0].reshape(256, 2, 2, 2, BLOCK).transpose(1, 3, 0, 2, 4)
-    goals = goals.reshape(4, 256, WIDE)
-    goals = [pick(goals, (colour + away) % 4, 0) for away in range(4)]
-    mine = jnp.concatenate([goals[1], masked, goals[3], goals[2], goals[0]], 1)
-    mine = turned(mine)
+    mine = turned(prepare(lengths, tokens, targets))
     from_below = up(mine[:, : D + WIDE])
     from_above = down(mine[:, WIDE : D + 2 * WIDE])
-    half = mine.shape[0] // 2
-    before = shift(mine[:half, WIDE : D + 3 * WIDE], "z", 1)
-    behind = shift(mine[half:, WIDE : D + 3 * WIDE], "z", -1)
-
-    start = jnp.moveaxis(outer_param.astype(jnp.bfloat16).reshape(32, 2, BLOCK), 1, 0)
-    start = jnp.broadcast_to(start[None, None, :, None], (2, 2, 2, 2, 32, BLOCK))
-    start = exchange(start.reshape(16, 32, BLOCK), ("h", "yh", "yl", "x"))
+
+    start, moments = pack(lengths, outer_param, first_mom, second_mom)
+    start = exchange(start, ("h", "yh", "yl", "x"))
     start = start.reshape(2, 256, BLOCK)
     here = pick(start, colour // 2, 0)
     there = pick(start, 1 - colour // 2, 0)
@@ -179,24 +265,16 @@
     )
     weights = exchange(weights, "z").reshape(D, BLOCK)
     start = here.astype(jnp.float32)
-
-    count = (jnp.sum(lengths[0]) // 128).astype(jnp.bfloat16)
-    moments = jnp.concatenate([first_mom[0], second_mom[0]], 0).astype(jnp.bfloat16)
-    moments = moments.reshape(64, 2, 2, 2, BLOCK)
-    moments = jnp.where(odd == 1, moments[:, ::-1], moments).transpose(2, 1, 3, 0, 4)
-    moments = jnp.concatenate(
-        [moments, jnp.broadcast_to(count, (2, 2, 2, 16, BLOCK))], 3
-    )
-    moments = jnp.broadcast_to(moments[:, :, :, None], (2, 2, 2, 2, 80, BLOCK))
-    moments = exchange(
-        after(moments.reshape(16, 80, BLOCK), mine), ("c", "yh", "yl", "x")
-    )
+    mine = after(mine, weights)
+    half = mine.shape[0] // 2
+    before = shift(mine[:half, WIDE : D + 3 * WIDE], "z", 1)
+    behind = shift(mine[half:, WIDE : D + 3 * WIDE], "z", -1)
+
+    moments = exchange(after(moments, weights), ("c", "yh", "yl", "x"))
     moments = pick(moments.reshape(2, 8, 80, BLOCK), x, 0)
-    weights, moments = lax.optimization_barrier((weights, moments))
-    first = moments[:, :32].reshape(256, BLOCK).astype(jnp.float32)
-    second = moments[:, 32:64].reshape(256, BLOCK).astype(jnp.float32)
-    coef = D ** (-0.5) / (128.0 * moments[0, 64, 0].astype(jnp.float32))
-
+    from_below, from_above, moments = lax.optimization_barrier(
+        (from_below, from_above, moments)
+    )
     near = [(block, WIDE, D + 3 * WIDE) for block in (mine, other_core(mine))]
     near += [
         (block, 0, D + WIDE)
@@ -207,6 +285,9 @@
     grad = product(near, core, weights)
     grad = product(sides, core, weights, grad, last=True)
 
+    first = moments[:, :32].reshape(256, BLOCK).astype(jnp.float32)
+    second = moments[:, 32:64].reshape(256, BLOCK).astype(jnp.float32)
+    coef = D ** (-0.5) / (128.0 * moments[0, 64, 0].astype(jnp.float32))
     grad = reduced(grad) * coef
     grads = [grad]
     first, second = adam_moments(first, second, grad)
@@ -222,21 +303,7 @@
     leaving = jnp.moveaxis(leaving.reshape(3, 8, 32, BLOCK), 1, 0)
     leaving = jnp.broadcast_to(leaving[None], (4, 8, 3, 32, BLOCK))
     arrived = exchange(leaving.reshape(32, 3, 32, BLOCK), ("h", "c", "yh", "yl", "x"))
-    arrived = arrived.reshape(2, 2, 2, 2, 2, 3, 32, BLOCK)
-
-    change = pick(pick(arrived[:, :, :, :, :, 0], (h + odd) % 2, 2), c, 1)
-    change = jnp.sum(change.astype(jnp.float32), (0, 2))
-    pseudo = jnp.moveaxis(change, 0, 1).reshape(32, WIDE) / 4
-    new_mom = 0.9 * outer_mom + pseudo
-    new_param = outer_param - 0.7 * (pseudo + 0.9 * new_mom)
-
-    home = pick(pick(arrived[:, :, :, :, :, 1:], c, 4), h, 0)
-    home = jnp.where(odd == 1, home[:, ::-1], home)
-    home = home.transpose(3, 4, 1, 0, 2, 5).reshape(2, 32, 8 * BLOCK)
-    first, second = first_mom[0], second_mom[0]
-    for step in range(STEPS):
-        first, second = adam_moments(first, second, home[step].astype(jnp.float32))
-    return (new_param, new_mom, first[None], second[None])
+    return tuple(finish(arrived, outer_param, outer_mom, first_mom, second_mom))
 
 
 def solution(mesh):

time: 194 us -> 197 us (1.015)
  blocking collectives: 17.1 us -> 42.5 us
  starting transfers between devices: 59.8 us -> 41.6 us
  local copies, waits for them, and re-layouts: 16.2 us -> 10.2 us
  waiting for transfers between devices: 66.2 us -> 70 us
  Pallas kernels: 20.1 us -> 23.5 us
  between operations: 4.63 us -> 1.63 us
    all_to_all x0 -> x1, blocking collectives: none -> 21.4 us  [exchange(): return lax.all_to_all(x, axes, 0, 0, tiled=True)]
    all_to_all x4 -> x3, starting transfers between devices: 34.7 us -> 19.1 us  [exchange(): return lax.all_to_all(x, axes, 0, 0, tiled=True)]
    ppermute x1, waiting for transfers between devices: 11.2 us -> 0.01 us  [turned(): return lax.ppermute(x, ('c', 'x'), TURN)]
    ppermute x9, waiting for transfers between devices: 0.08 us -> 7.88 us  [shift(): return lax.ppermute(x, axis, [(i, (i + by) % size) for i in range(size)])]
    all_to_all x4 -> x3, waiting for transfers between devices: 31 us -> 36.1 us  [exchange(): return lax.all_to_all(x, axes, 0, 0, tiled=True)]
    all_to_all x1, blocking collectives: 17.1 us -> 21 us  [among_peers(): return lax.all_to_all(x, axes, 0, 0, axis_index_groups=PEERS, tiled=True)]
    ppermute x9, starting transfers between devices: 11.2 us -> 7.4 us  [shift(): return lax.ppermute(x, axis, [(i, (i + by) % size) for i in range(size)])]
    pallas_call x0 -> x3, Pallas kernels: none -> 3.29 us  [the longest x1 1.72 us: pack(): pl.pallas_call(pack_kernel, out_shape=[jax.ShapeDtypeStruct((16, 32, BLOC...]
  transfers between devices with their start and end apart: 16 -> 15, of which waited for: 7 -> 8; matrix products, arithmetic and copies ran while one was open for 6% -> 5% of each run, Pallas kernels for 2% -> 3%
where the time goes in v4:
time: 197 us; the launch traced here: 196 us
  waiting for transfers between devices  70 us (36%)
  blocking collectives  42.5 us (22%)
  starting transfers between devices  41.6 us (21%)
  Pallas kernels  23.5 us (12%)
  local copies, waits for them, and re-layouts  10.2 us (5%)
  other arithmetic  6.87 us (3%)
    all_to_all x3, waiting for transfers between devices, exchange(): return lax.all_to_all(x, axes, 0, 0, tiled=True)  36.1 us
    all_to_all x2, waiting for transfers between devices, among_peers(): return lax.all_to_all(x, axes, 0, 0, axis_index_groups=PEERS, tiled=True)  26.1 us
    all_to_all x1, blocking collectives, exchange(): return lax.all_to_all(x, axes, 0, 0, tiled=True)  21.4 us
    all_to_all x1, blocking collectives, among_peers(): return lax.all_to_all(x, axes, 0, 0, axis_index_groups=PEERS, tiled=True)  21 us
    pallas_call x3, Pallas kernels, product(): pl.pallas_call(functools.partial(product_kernel, layout, last), out_shape...  20.2 us
    all_to_all x3, starting transfers between devices, exchange(): return lax.all_to_all(x, axes, 0, 0, tiled=True)  19.1 us
    all_to_all x2, starting transfers between devices, among_peers(): return lax.all_to_all(x, axes, 0, 0, axis_index_groups=PEERS, tiled=True)  10.6 us
    ppermute x9, waiting for transfers between devices, shift(): return lax.ppermute(x, axis, [(i, (i + by) % size) for i in range(size)])  7.88 us
  transfers between devices with their start and end apart: 15, of which 8 were waited for; matrix products, arithmetic and copies ran while one was open for 5% of the time, Pallas kernels for 3%

profile of v4, /device:TPU:1, one launch (start us, length us, event | category | flops | bytes accessed | tf_op | source)
XLA Modules:
  0.0 196.3 jit_solution(9492146752186809908)
XLA Ops:
  0.6 1.2 copy-done
  1.9 1.0 copy-done.3
  2.9 0.7 copy-done.7
  3.6 0.8 shard_map.103
  4.3 4.5 %collective-permute-start = (bf16[256,3072]{1,0:T(8,128)(2,1)S(1)}, bf16[256,3072]{1,0:T(8,128)(2,1)S(1)}, u32[]{:S(2)}, u32[]{:S(2)}) collective-permute-start(bf16[256,3072]{1,0:T(8,128)(2,1)S(1)} %shard_map.103), channel_id=1, source_target_pairs={{0,0},{1,64},{64,1},{65,65},{2,2},{3,66},{66,3},{67,67},{4,4},{5,6... | collective-permute-start | bytes 4718600 | tf_op jit(solution)/shard_map/ppermute | solution.py:51
  8.9 1.7 shard_map.102
  10.6 0.7 copy-done.5
  11.3 6.5 %all-to-all-start = ((bf16[16,32,128]{2,1,0:T(8,128)(2,1)}), bf16[16,32,128]{2,1,0:T(8,128)(2,1)}, u32[]{:S(2)}, u32[]{:S(2)}) async-start(bf16[16,32,128]{2,1,0:T(8,128)(2,1)} %copy-done.5), calls=%async_computation | async-start | bytes 262144 | tf_op jit(solution)/shard_map/all_to_all | solution.py:39
  17.9 15.2 %all-to-all-done = bf16[16,32,128]{2,1,0:T(8,128)(2,1)} async-done(((bf16[16,32,128]{2,1,0:T(8,128)(2,1)}), bf16[16,32,128]{2,1,0:T(8,128)(2,1)}, u32[]{:S(2)}, u32[]{:S(2)}) %all-to-all-start) | async-done | bytes 131104 | tf_op jit(solution)/shard_map/all_to_all | solution.py:39
  33.1 0.9 dynamic-slice_bitcast_fusion.2
  33.9 0.9 broadcast_select_fusion
  34.8 8.2 %all-to-all-start.1 = ((bf16[8,256,128]{2,1,0:T(8,128)(2,1)}), bf16[8,256,128]{2,1,0:T(8,128)(2,1)}, u32[]{:S(2)}, u32[]{:S(2)}) async-start(bf16[8,256,128]{2,1,0:T(8,128)(2,1)} %broadcast_select_fusion), calls=%async_computation.1 | async-start | bytes 1048576 | tf_op jit(solution)/shard_map/all_to_all | solution.py:39
  43.0 1.6 fusion.15
  44.6 2.7 %collective-permute-start.2 = (bf16[256,2304]{1,0:T(8,128)(2,1)}, bf16[256,2304]{1,0:T(8,128)(2,1)}, u32[]{:S(2)}, u32[]{:S(2)}) collective-permute-start(bf16[256,2304]{1,0:T(8,128)(2,1)} %get-tuple-element.20), channel_id=1, source_target_pairs={{0,6},{2,0},{4,2},{6,4},{1,7},{3,1},{5,3},{7,5},{8,14},{10,8},{12,... | collective-permute-start | bytes 3538952 | tf_op jit(solution)/shard_map/ppermute | solution.py:31
  47.3 13.1 %all-to-all-done.1 = bf16[8,256,128]{2,1,0:T(8,128)(2,1)} async-done(((bf16[8,256,128]{2,1,0:T(8,128)(2,1)}), bf16[8,256,128]{2,1,0:T(8,128)(2,1)}, u32[]{:S(2)}, u32[]{:S(2)}) %all-to-all-start.1) | async-done | bytes 524320 | tf_op jit(solution)/shard_map/all_to_all | solution.py:39
  60.4 4.4 %all-to-all-start.2 = ((bf16[16,80,128]{2,1,0:T(8,128)(2,1)}), bf16[16,80,128]{2,1,0:T(8,128)(2,1)}, u32[]{:S(2)}, u32[]{:S(2)}) async-start(bf16[16,80,128]{2,1,0:T(8,128)(2,1)} %get-tuple-element.13), calls=%async_computation.2 | async-start | bytes 655360 | tf_op jit(solution)/shard_map/all_to_all | solution.py:39
  64.8 0.3 collective-permute-start.5
  65.1 1.1 fusion.14
  66.3 2.7 %collective-permute-start.7 = (bf16[128,2560]{1,0:T(8,128)(2,1)}, bf16[128,2560]{1,0:T(8,128)(2,1)}, u32[]{:S(2)}, u32[]{:S(2)}) collective-permute-start(bf16[128,2560]{1,0:T(8,128)(2,1)} %get-tuple-element.18), channel_id=1, source_target_pairs={{0,56},{8,0},{16,8},{24,16},{32,24},{40,32},{48,40},{56,48},{1,57}... | collective-permute-start | bytes 1966088 | tf_op jit(solution)/shard_map/ppermute | solution.py:31
  68.9 7.8 %all-to-all-done.2 = bf16[16,80,128]{2,1,0:T(8,128)(2,1)} async-done(((bf16[16,80,128]{2,1,0:T(8,128)(2,1)}), bf16[16,80,128]{2,1,0:T(8,128)(2,1)}, u32[]{:S(2)}, u32[]{:S(2)}) %all-to-all-start.2) | async-done | bytes 327712 | tf_op jit(solution)/shard_map/all_to_all | solution.py:39
  76.7 1.6 dynamic-slice_bitcast_fusion
  78.3 0.6 collective-permute-start.3
  79.0 0.1 collective-permute-start.4
  79.0 4.9 %collective-permute-done.6.refs_2_ = bf16[128,2560]{1,0:T(8,128)(2,1)} collective-permute-done((bf16[128,2560]{1,0:T(8,128)(2,1)}, bf16[128,2560]{1,0:T(8,128)(2,1)}, u32[]{:S(2)}, u32[]{:S(2)}) %collective-permute-start.6) | collective-permute-done | bytes 655392 | tf_op jit(solution)/shard_map/ppermute | solution.py:31
  83.9 1.0 collective-permute-start.8
  84.9 0.0 collective-permute-start.9
  84.9 2.1 %collective-permute-done.8.refs_4_ = bf16[128,2560]{1,0:T(8,128)(2,1)} collective-permute-done((bf16[128,2560]{1,0:T(8,128)(2,1)}, bf16[128,2560]{1,0:T(8,128)(2,1)}, u32[]{:S(2)}, u32[]{:S(2)}) %collective-permute-start.8) | collective-permute-done | bytes 655392 | tf_op jit(solution)/shard_map/ppermute | solution.py:31
  87.0 0.9 collective-permute-done.9.refs_5_
  87.9 4.7 %shard_map.104.refs_4_ = f32[128,2048]{1,0:T(8,128)S(1)} custom-call(s32[1]{0:T(128)} %bitcast.7.core, bf16[2048,128]{1,0:T(8,128)(2,1)} %bitcast.3.weights, bf16[256,3072]{1,0:T(8,128)(2,1)S(1)} %collective-permute-done.refs_0_, bf16[256,3072]{1,0:T(8,128)(2,1)S(1)} %collective-permute-done.5.refs_1_, bf16[128,2560]{1,0:T(8,128)(2,1)} %collective-permute-done.6.refs_2_, ...), custom_call_target="tpu_custom_call" | custom-call | flops 2147483648 | bytes 4194304 | tf_op jit(solution)/shard_map/pallas_call | solution.py:217
  92.6 6.9 %shard_map.105 = bf16[8,256,128]{2,1,0:T(8,128)(2,1)} custom-call(s32[1]{0:T(128)} %bitcast.7.core, bf16[2048,128]{1,0:T(8,128)(2,1)} %bitcast.3.weights, bf16[256,2304]{1,0:T(8,128)(2,1)} %collective-permute-done.1.refs_0_.refs_6_, bf16[256,2304]{1,0:T(8,128)(2,1)} %collective-permute-done.3.refs_1_.refs_7_, ...), custom_call_target="tpu_custom_call" | custom-call | flops 2147483648 | bytes 4194304 | tf_op jit(solution)/shard_map/pallas_call | solution.py:217
  99.5 5.7 %all-to-all-start.3 = ((bf16[8,256,128]{2,1,0:T(8,128)(2,1)}), bf16[8,256,128]{2,1,0:T(8,128)(2,1)}, u32[]{:S(2)}, u32[]{:S(2)}) async-start(bf16[8,256,128]{2,1,0:T(8,128)(2,1)} %shard_map.105), calls=%async_computation.3 | async-start | bytes 1048576 | tf_op jit(solution)/shard_map/all_to_all | solution.py:237
  105.2 1.2 slice.26
  107.1 1.6 convert_multiply_fusion.1
  108.7 12.4 %all-to-all-done.3 = bf16[8,256,128]{2,1,0:T(8,128)(2,1)} async-done(((bf16[8,256,128]{2,1,0:T(8,128)(2,1)}), bf16[8,256,128]{2,1,0:T(8,128)(2,1)}, u32[]{:S(2)}, u32[]{:S(2)}) %all-to-all-start.3) | async-done | bytes 524320 | tf_op jit(solution)/shard_map/all_to_all | solution.py:237
  121.1 1.1 convert_reduce_fusion.1
  122.2 1.2 convert_bitcast_fusion
  123.4 0.1 broadcast_in_dim.51
  123.5 21.0 %all_to_all.35 = bf16[8,256,128]{2,1,0:T(8,128)(2,1)S(1)} all-to-all(bf16[8,256,128]{2,1,0:T(8,128)(2,1)S(1)} %broadcast_in_dim.51), channel_id=1, replica_groups={{0,12,16,28,32,44,48,60},{2,14,18,30,34,46,50,62},{4,8,20,24,36,40,52,5..., dimensions={0} | all-to-all | bytes 1048576 | tf_op jit(solution)/shard_map/all_to_all | solution.py:237
  144.5 8.7 %shard_map.106 = bf16[8,256,128]{2,1,0:T(8,128)(2,1)} custom-call(s32[1]{0:T(128)} %bitcast.7.core, bf16[2048,128]{1,0:T(8,128)(2,1)S(1)} %bitcast.64, bf16[256,3072]{1,0:T(8,128)(2,1)S(1)} %collective-permute-done.refs_0_, bf16[256,3072]{1,0:T(8,128)(2,1)S(1)} %collective-permute-done.5.refs_1_, bf16[128,2560]{1,0:T(8,128)(2,1)} %collective-permute-done.6.refs_2_, ...), custom_call_target="tpu_custom_call" | custom-call | flops 4294967296 | bytes 8388608 | tf_op jit(solution)/shard_map/pallas_call | solution.py:217
  153.2 0.0 copy-start.12
  153.2 5.0 %all-to-all-start.5 = ((bf16[8,256,128]{2,1,0:T(8,128)(2,1)}), bf16[8,256,128]{2,1,0:T(8,128)(2,1)S(1)}, u32[]{:S(2)}, u32[]{:S(2)}) async-start(bf16[8,256,128]{2,1,0:T(8,128)(2,1)} %shard_map.106), calls=%async_computation.5 | async-start | bytes 1048576 | tf_op jit(solution)/shard_map/all_to_all | solution.py:237
  158.2 0.9 multiply_convert_fusion.1
  159.1 13.6 %all-to-all-done.5 = bf16[8,256,128]{2,1,0:T(8,128)(2,1)S(1)} async-done(((bf16[8,256,128]{2,1,0:T(8,128)(2,1)}), bf16[8,256,128]{2,1,0:T(8,128)(2,1)S(1)}, u32[]{:S(2)}, u32[]{:S(2)}) %all-to-all-start.5) | async-done | bytes 524320 | tf_op jit(solution)/shard_map/all_to_all | solution.py:237
  172.7 0.1 convert_reduce_fusion
  172.9 1.1 fusion.2
  173.9 0.1 broadcast_in_dim.52
  174.1 21.4 %all_to_all.36.arrived = bf16[32,3,32,128]{3,2,1,0:T(8,128)(2,1)S(1)} all-to-all(bf16[32,3,32,128]{3,2,1,0:T(8,128)(2,1)S(1)} %bitcast.65), channel_id=1, replica_groups=mesh['h'=2,'c'=2,'z'=8,'yh'=2,'yl'=2,'x'=2] {'h','c','yh','yl','x'}, dimensions={0} | all-to-all | bytes 1572864 | tf_op jit(solution)/shard_map/all_to_all | solution.py:39
  195.5 0.8 shard_map.107
  (33 shorter events, 0.1 us)
Async XLA Ops:
  0.6 1.2 copy-start
  1.9 1.0 copy-start.3
  2.9 0.7 copy-start.7
  3.6 5.3 %copy-start.1 = (f32[1,32,1024]{2,1,0:T(8,128)S(1)}, f32[1,32,1024]{2,1,0:T(8,128)}, u32[]{:S(2)}) copy-start(f32[1,32,1024]{2,1,0:T(8,128)} %first.3) | copy-start | bytes 393220
  3.6 5.3 %copy-start.2 = (f32[1,32,1024]{2,1,0:T(8,128)S(1)}, f32[1,32,1024]{2,1,0:T(8,128)}, u32[]{:S(2)}) copy-start(f32[1,32,1024]{2,1,0:T(8,128)} %second.3) | copy-start | bytes 393220
  3.6 5.3 %copy-start.4 = (f32[32,256]{1,0:T(8,128)S(1)}, f32[32,256]{1,0:T(8,128)}, u32[]{:S(2)}) copy-start(f32[32,256]{1,0:T(8,128)} %param.17) | copy-start | bytes 98308
  3.6 5.3 %copy-start.8 = (s32[1,64]{1,0:T(1,128)S(1)}, s32[1,64]{1,0:T(1,128)}, u32[]{:S(2)}) copy-start(s32[1,64]{1,0:T(1,128)} %lengths.3) | copy-start | bytes 772
  4.3 38.7 %collective-permute-start = (bf16[256,3072]{1,0:T(8,128)(2,1)S(1)}, bf16[256,3072]{1,0:T(8,128)(2,1)S(1)}, u32[]{:S(2)}, u32[]{:S(2)}) collective-permute-start(bf16[256,3072]{1,0:T(8,128)(2,1)S(1)} %shard_map.103), channel_id=1, source_target_pairs={{0,0},{1,64},{64,1},{65,65},{2,2},{3,66},{66,3},{67,67},{4,4},{5,6... | collective-permute-start | bytes 4718600 | tf_op jit(solution)/shard_map/ppermute | solution.py:51
  10.6 0.7 copy-start.5
  11.3 21.8 %all-to-all-start = ((bf16[16,32,128]{2,1,0:T(8,128)(2,1)}), bf16[16,32,128]{2,1,0:T(8,128)(2,1)}, u32[]{:S(2)}, u32[]{:S(2)}) async-start(bf16[16,32,128]{2,1,0:T(8,128)(2,1)} %copy-done.5), calls=%async_computation | async-start | bytes 262144 | tf_op jit(solution)/shard_map/all_to_all | solution.py:39
  34.8 25.6 %all-to-all-start.1 = ((bf16[8,256,128]{2,1,0:T(8,128)(2,1)}), bf16[8,256,128]{2,1,0:T(8,128)(2,1)}, u32[]{:S(2)}, u32[]{:S(2)}) async-start(bf16[8,256,128]{2,1,0:T(8,128)(2,1)} %broadcast_select_fusion), calls=%async_computation.1 | async-start | bytes 1048576 | tf_op jit(solution)/shard_map/all_to_all | solution.py:39
  44.6 33.7 %collective-permute-start.1 = (bf16[256,2304]{1,0:T(8,128)(2,1)}, bf16[256,2304]{1,0:T(8,128)(2,1)}, u32[]{:S(2)}, u32[]{:S(2)}) collective-permute-start(bf16[256,2304]{1,0:T(8,128)(2,1)} %get-tuple-element.21), channel_id=1, source_target_pairs={{0,2},{2,4},{4,6},{6,0},{1,3},{3,5},{5,7},{7,1},{8,10},{10,12},{12... | collective-permute-start | bytes 3538952 | tf_op jit(solution)/shard_map/ppermute | solution.py:31
  44.6 33.7 %collective-permute-start.2 = (bf16[256,2304]{1,0:T(8,128)(2,1)}, bf16[256,2304]{1,0:T(8,128)(2,1)}, u32[]{:S(2)}, u32[]{:S(2)}) collective-permute-start(bf16[256,2304]{1,0:T(8,128)(2,1)} %get-tuple-element.20), channel_id=1, source_target_pairs={{0,6},{2,0},{4,2},{6,4},{1,7},{3,1},{5,3},{7,5},{8,14},{10,8},{12,... | collective-permute-start | bytes 3538952 | tf_op jit(solution)/shard_map/ppermute | solution.py:31
  60.4 16.3 %all-to-all-start.2 = ((bf16[16,80,128]{2,1,0:T(8,128)(2,1)}), bf16[16,80,128]{2,1,0:T(8,128)(2,1)}, u32[]{:S(2)}, u32[]{:S(2)}) async-start(bf16[16,80,128]{2,1,0:T(8,128)(2,1)} %get-tuple-element.13), calls=%async_computation.2 | async-start | bytes 655360 | tf_op jit(solution)/shard_map/all_to_all | solution.py:39
  64.8 23.1 %collective-permute-start.5 = (bf16[256,3072]{1,0:T(8,128)(2,1)S(1)}, bf16[256,3072]{1,0:T(8,128)(2,1)S(1)}, u32[]{:S(2)}, u32[]{:S(2)}) collective-permute-start(bf16[256,3072]{1,0:T(8,128)(2,1)S(1)} %collective-permute-done.refs_0_), channel_id=1, source_target_pairs={{0,64},{64,0},{1,65},{65,1},{2,66},{66,2},{3,67},{67,3},{4,68},{68... | collective-permute-start | bytes 4718600 | tf_op jit(solution)/shard_map/ppermute | solution.py:31
  66.3 17.7 %collective-permute-start.6 = (bf16[128,2560]{1,0:T(8,128)(2,1)}, bf16[128,2560]{1,0:T(8,128)(2,1)}, u32[]{:S(2)}, u32[]{:S(2)}) collective-permute-start(bf16[128,2560]{1,0:T(8,128)(2,1)} %get-tuple-element.19), channel_id=1, source_target_pairs={{0,8},{8,16},{16,24},{24,32},{32,40},{40,48},{48,56},{56,0},{1,9},... | collective-permute-start | bytes 1966088 | tf_op jit(solution)/shard_map/ppermute | solution.py:31
  66.3 18.7 %collective-permute-start.7 = (bf16[128,2560]{1,0:T(8,128)(2,1)}, bf16[128,2560]{1,0:T(8,128)(2,1)}, u32[]{:S(2)}, u32[]{:S(2)}) collective-permute-start(bf16[128,2560]{1,0:T(8,128)(2,1)} %get-tuple-element.18), channel_id=1, source_target_pairs={{0,56},{8,0},{16,8},{24,16},{32,24},{40,32},{48,40},{56,48},{1,57}... | collective-permute-start | bytes 1966088 | tf_op jit(solution)/shard_map/ppermute | solution.py:31
  78.3 14.3 %collective-permute-start.3 = (bf16[256,2304]{1,0:T(8,128)(2,1)}, bf16[256,2304]{1,0:T(8,128)(2,1)}, u32[]{:S(2)}, u32[]{:S(2)}) collective-permute-start(bf16[256,2304]{1,0:T(8,128)(2,1)} %collective-permute-done.1.refs_0_.refs_6_), channel_id=1, source_target_pairs={{0,64},{64,0},{1,65},{65,1},{2,66},{66,2},{3,67},{67,3},{4,68},{68... | collective-permute-start | bytes 3538952 | tf_op jit(solution)/shard_map/ppermute | solution.py:31
  79.0 13.7 %collective-permute-start.4 = (bf16[256,2304]{1,0:T(8,128)(2,1)}, bf16[256,2304]{1,0:T(8,128)(2,1)}, u32[]{:S(2)}, u32[]{:S(2)}) collective-permute-start(bf16[256,2304]{1,0:T(8,128)(2,1)} %collective-permute-done.2.refs_2_.refs_8_), channel_id=1, source_target_pairs={{0,64},{64,0},{1,65},{65,1},{2,66},{66,2},{3,67},{67,3},{4,68},{68... | collective-permute-start | bytes 3538952 | tf_op jit(solution)/shard_map/ppermute | solution.py:31
  83.9 3.1 %collective-permute-start.8 = (bf16[128,2560]{1,0:T(8,128)(2,1)}, bf16[128,2560]{1,0:T(8,128)(2,1)}, u32[]{:S(2)}, u32[]{:S(2)}) collective-permute-start(bf16[128,2560]{1,0:T(8,128)(2,1)} %collective-permute-done.6.refs_2_), channel_id=1, source_target_pairs={{0,64},{64,0},{1,65},{65,1},{2,66},{66,2},{3,67},{67,3},{4,68},{68... | collective-permute-start | bytes 1966088 | tf_op jit(solution)/shard_map/ppermute | solution.py:31
  84.9 3.0 %collective-permute-start.9 = (bf16[128,2560]{1,0:T(8,128)(2,1)}, bf16[128,2560]{1,0:T(8,128)(2,1)}, u32[]{:S(2)}, u32[]{:S(2)}) collective-permute-start(bf16[128,2560]{1,0:T(8,128)(2,1)} %collective-permute-done.7.refs_3_), channel_id=1, source_target_pairs={{0,64},{64,0},{1,65},{65,1},{2,66},{66,2},{3,67},{67,3},{4,68},{68... | collective-permute-start | bytes 1966088 | tf_op jit(solution)/shard_map/ppermute | solution.py:31
  99.5 21.6 %all-to-all-start.3 = ((bf16[8,256,128]{2,1,0:T(8,128)(2,1)}), bf16[8,256,128]{2,1,0:T(8,128)(2,1)}, u32[]{:S(2)}, u32[]{:S(2)}) async-start(bf16[8,256,128]{2,1,0:T(8,128)(2,1)} %shard_map.105), calls=%async_computation.3 | async-start | bytes 1048576 | tf_op jit(solution)/shard_map/all_to_all | solution.py:237
  122.2 1.2 copy-start.9
  153.2 19.6 %copy-start.10 = (f32[256,128]{1,0:T(8,128)S(1)}, f32[256,128]{1,0:T(8,128)}, u32[]{:S(2)}) copy-start(f32[256,128]{1,0:T(8,128)} %copy-done.9) | copy-start | bytes 393220
  153.2 19.6 %copy-start.11 = (f32[8,32,128]{2,1,0:T(8,128)S(1)}, f32[8,32,128]{2,1,0:T(8,128)}, u32[]{:S(2)}) copy-start(f32[8,32,128]{2,1,0:T(8,128)} %get-tuple-element.22) | copy-start | bytes 393220
  153.2 19.6 %copy-start.12 = (f32[8,32,128]{2,1,0:T(8,128)S(1)}, f32[8,32,128]{2,1,0:T(8,128)}, u32[]{:S(2)}) copy-start(f32[8,32,128]{2,1,0:T(8,128)} %get-tuple-element.23) | copy-start | bytes 393220
  153.2 19.5 %all-to-all-start.5 = ((bf16[8,256,128]{2,1,0:T(8,128)(2,1)}), bf16[8,256,128]{2,1,0:T(8,128)(2,1)S(1)}, u32[]{:S(2)}, u32[]{:S(2)}) async-start(bf16[8,256,128]{2,1,0:T(8,128)(2,1)} %shard_map.106), calls=%async_computation.5 | async-start | bytes 1048576 | tf_op jit(solution)/shard_map/all_to_all | solution.py:237
  173.9 21.6 %copy-start.6 = (f32[32,256]{1,0:T(8,128)S(1)}, f32[32,256]{1,0:T(8,128)}, u32[]{:S(2)}) copy-start(f32[32,256]{1,0:T(8,128)} %mom.1) | copy-start | bytes 98308

commit v5 on v4

--- a/solution.py
+++ b/solution.py
@@ -43,8 +43,8 @@
     return lax.dynamic_index_in_dim(x, index, axis, keepdims=False)
 
 
-def after(x, *earlier):
-    return lax.optimization_barrier((x, *earlier))[0]
+def together(*arrays):
+    return lax.optimization_barrier(arrays)
 
 
 def turned(x):
@@ -65,30 +65,43 @@
     return z, y, odd, lax.rem(y + 2 * odd, 4)
 
 
-def prepare_kernel(lengths, tokens, targets, out):
+def prepare_kernel(lengths, tokens, targets, out, inputs, goals, sems):
+    copies = [
+        pltpu.make_async_copy(tokens.at[0], inputs, sems.at[0]),
+        pltpu.make_async_copy(targets.at[0], goals, sems.at[1]),
+    ]
+    for copy in copies:
+        copy.start()
     z, y, _, colour = place()
     length = lengths[0, (z * 4 + y) * 2 + lax.axis_index("x")]
-    valid = lax.broadcasted_iota(jnp.int32, tokens.shape[1:], 0) < length
-    inputs = tokens[0]
-    out[:, WIDE : WIDE + D] = jnp.where(valid, inputs, jnp.zeros_like(inputs))
+    valid = lax.broadcasted_iota(jnp.int32, inputs.shape, 0) < length
+    copies[0].wait()
+    out[:, WIDE : WIDE + D] = jnp.where(valid, inputs[...], jnp.zeros_like(inputs))
+    copies[1].wait()
     for away, at in ((1, 0), (3, D + WIDE), (2, D + 2 * WIDE), (0, D + 3 * WIDE)):
         wanted = lax.rem(colour + away, 4)
         source = wanted // 2 * (2 * WIDE) + lax.rem(wanted, 2) * BLOCK
         for core in range(2):
             column = pl.multiple_of(source + core * WIDE, BLOCK)
-            out[:, at + core * BLOCK : at + (core + 1) * BLOCK] = targets[
-                0, :, pl.ds(column, BLOCK)
+            out[:, at + core * BLOCK : at + (core + 1) * BLOCK] = goals[
+                :, pl.ds(column, BLOCK)
             ]
 
 
 def prepare(lengths, tokens, targets):
-    whole = pl.BlockSpec(memory_space=pltpu.VMEM)
+    rows = tokens.shape[1]
     return pl.pallas_call(
         prepare_kernel,
-        out_shape=jax.ShapeDtypeStruct((256, D + 4 * WIDE), jnp.bfloat16),
-        in_specs=[pl.BlockSpec(memory_space=pltpu.SMEM), whole, whole],
-        out_specs=whole,
-        compiler_params=pltpu.CompilerParams(vmem_limit_bytes=16 * 2**20),
+        out_shape=jax.ShapeDtypeStruct((rows, D + 4 * WIDE), jnp.bfloat16),
+        in_specs=[pl.BlockSpec(memory_space=pltpu.SMEM)]
+        + [pl.BlockSpec(memory_space=pl.ANY)] * 2,
+        out_specs=pl.BlockSpec(memory_space=pltpu.VMEM),
+        scratch_shapes=[
+            pltpu.VMEM((rows, D), jnp.bfloat16),
+            pltpu.VMEM((rows, 4 * WIDE), jnp.bfloat16),
+            pltpu.SemaphoreType.DMA((2,)),
+        ],
+        compiler_params=pltpu.CompilerParams(vmem_limit_bytes=60 * 2**20),
     )(lengths, tokens, targets)
 
 
@@ -252,11 +265,18 @@
     core = c.reshape(1).astype(jnp.int32)
 
     mine = turned(prepare(lengths, tokens, targets))
-    from_below = up(mine[:, : D + WIDE])
-    from_above = down(mine[:, WIDE : D + 2 * WIDE])
-
     start, moments = pack(lengths, outer_param, first_mom, second_mom)
     start = exchange(start, ("h", "yh", "yl", "x"))
+    mine, start = together(mine, start)
+    theirs = other_core(mine)
+
+    below, above = up(mine[:, : D + WIDE]), down(mine[:, WIDE : D + 2 * WIDE])
+    half = mine.shape[0] // 2
+    plane = jnp.concatenate(
+        [mine[:, WIDE : WIDE + D], mine[:, D + 2 * WIDE : D + 3 * WIDE]], 1
+    )
+    before, behind = shift(plane[:half], "z", 1), shift(plane[half:], "z", -1)
+
     start = start.reshape(2, 256, BLOCK)
     here = pick(start, colour // 2, 0)
     there = pick(start, 1 - colour // 2, 0)
@@ -265,23 +285,19 @@
     )
     weights = exchange(weights, "z").reshape(D, BLOCK)
     start = here.astype(jnp.float32)
-    mine = after(mine, weights)
-    half = mine.shape[0] // 2
-    before = shift(mine[:half, WIDE : D + 3 * WIDE], "z", 1)
-    behind = shift(mine[half:, WIDE : D + 3 * WIDE], "z", -1)
-
-    moments = exchange(after(moments, weights), ("c", "yh", "yl", "x"))
+
+    moments, weights = together(moments, weights)
+    moments = exchange(moments, ("c", "yh", "yl", "x"))
     moments = pick(moments.reshape(2, 8, 80, BLOCK), x, 0)
-    from_below, from_above, moments = lax.optimization_barrier(
-        (from_below, from_above, moments)
-    )
-    near = [(block, WIDE, D + 3 * WIDE) for block in (mine, other_core(mine))]
+
+    weights, above = together(weights, above)
+    near = [(block, WIDE, D + 3 * WIDE) for block in (mine, theirs)]
     near += [
-        (block, 0, D + WIDE)
+        (block, 0, D)
         for block in (before, behind, other_core(before), other_core(behind))
     ]
-    sides = [(block, WIDE, 0) for block in (from_below, other_core(from_below))]
-    sides += [(block, 0, D) for block in (from_above, other_core(from_above))]
+    sides = [(block, WIDE, 0) for block in (below, other_core(below))]
+    sides += [(block, 0, D) for block in (above, other_core(above))]
     grad = product(near, core, weights)
     grad = product(sides, core, weights, grad, last=True)
 

time: 197 us -> 186 us (0.944)
  local copies, waits for them, and re-layouts: 10.2 us -> 4.07 us
  other arithmetic: 6.87 us -> 2.62 us
  Pallas kernels: 23.5 us -> 26.4 us
  blocking collectives: 42.5 us -> 40 us
    all_to_all x3, waiting for transfers between devices: 36.1 us -> 30 us  [exchange(): return lax.all_to_all(x, axes, 0, 0, tiled=True)]
    all_to_all x2, waiting for transfers between devices: 26.1 us -> 30.7 us  [among_peers(): return lax.all_to_all(x, axes, 0, 0, axis_index_groups=PEERS, tiled=True)]
    unnamed x26 -> x12, local copies, waits for them, and re-layouts: 3.61 us -> 0.77 us
    pallas_call x1, Pallas kernels: 0.77 us -> 3.47 us  [prepare(): pl.pallas_call(prepare_kernel, out_shape=jax.ShapeDtypeStruct((rows, D +...]
    all_to_all x1, blocking collectives: 21 us -> 18.5 us  [among_peers(): return lax.all_to_all(x, axes, 0, 0, axis_index_groups=PEERS, tiled=True)]
  transfers between devices with their start and end apart: 15 -> 15, of which waited for: 8 -> 6; matrix products, arithmetic and copies ran while one was open for 5% -> 2% of each run, Pallas kernels for 3% -> 7%
where the time goes in v5:
time: 186 us; the launch traced here: 185 us
  waiting for transfers between devices  69.7 us (37%)
  starting transfers between devices  40.6 us (22%)
  blocking collectives  40 us (22%)
  Pallas kernels  26.4 us (14%)
  local copies, waits for them, and re-layouts  4.07 us (2%)
  other arithmetic  2.62 us (1%)
    all_to_all x2, waiting for transfers between devices, among_peers(): return lax.all_to_all(x, axes, 0, 0, axis_index_groups=PEERS, tiled=True)  30.7 us
    all_to_all x3, waiting for transfers between devices, exchange(): return lax.all_to_all(x, axes, 0, 0, tiled=True)  30 us
    all_to_all x1, blocking collectives, exchange(): return lax.all_to_all(x, axes, 0, 0, tiled=True)  21.5 us
    pallas_call x3, Pallas kernels, product(): pl.pallas_call(functools.partial(product_kernel, layout, last), out_shape...  20.4 us
    all_to_all x1, blocking collectives, among_peers(): return lax.all_to_all(x, axes, 0, 0, axis_index_groups=PEERS, tiled=True)  18.5 us
    all_to_all x3, starting transfers between devices, exchange(): return lax.all_to_all(x, axes, 0, 0, tiled=True)  18.3 us
    all_to_all x2, starting transfers between devices, among_peers(): return lax.all_to_all(x, axes, 0, 0, axis_index_groups=PEERS, tiled=True)  11.2 us
    ppermute x9, waiting for transfers between devices, shift(): return lax.ppermute(x, axis, [(i, (i + by) % size) for i in range(size)])  9.05 us
  transfers between devices with their start and end apart: 15, of which 6 were waited for; matrix products, arithmetic and copies ran while one was open for 2% of the time, Pallas kernels for 7%

profile of v5, /device:TPU:1, one launch (start us, length us, event | category | flops | bytes accessed | tf_op | source)
XLA Modules:
  0.0 185.1 jit_solution(1095819250641325460)
XLA Ops:
  0.7 3.5 %shard_map.102 = bf16[256,3072]{1,0:T(8,128)(2,1)} custom-call(s32[1,64]{1,0:T(1,128)} %lengths.3, bf16[1,256,2048]{2,1,0:T(8,128)(2,1)} %tokens.1, bf16[1,256,1024]{2,1,0:T(8,128)(2,1)} %targets.1), custom_call_target="tpu_custom_call" | custom-call | tf_op jit(solution)/shard_map/pallas_call | solution.py:93
  4.2 4.5 %collective-permute-start = (bf16[256,3072]{1,0:T(8,128)(2,1)}, bf16[256,3072]{1,0:T(8,128)(2,1)S(1)}, u32[]{:S(2)}, u32[]{:S(2)}) collective-permute-start(bf16[256,3072]{1,0:T(8,128)(2,1)} %shard_map.102), channel_id=1, source_target_pairs={{0,0},{1,64},{64,1},{65,65},{2,2},{3,66},{66,3},{67,67},{4,4},{5,6... | collective-permute-start | bytes 4718600 | tf_op jit(solution)/shard_map/ppermute | solution.py:51
  8.7 1.8 shard_map.103
  10.5 6.5 %all-to-all-start = ((bf16[16,32,128]{2,1,0:T(8,128)(2,1)}), bf16[16,32,128]{2,1,0:T(8,128)(2,1)S(1)}, u32[]{:S(2)}, u32[]{:S(2)}) async-start(bf16[16,32,128]{2,1,0:T(8,128)(2,1)} %get-tuple-element.12), calls=%async_computation | async-start | bytes 262144 | tf_op jit(solution)/shard_map/all_to_all | solution.py:39
  17.0 16.0 %all-to-all-done = bf16[16,32,128]{2,1,0:T(8,128)(2,1)S(1)} async-done(((bf16[16,32,128]{2,1,0:T(8,128)(2,1)}), bf16[16,32,128]{2,1,0:T(8,128)(2,1)S(1)}, u32[]{:S(2)}, u32[]{:S(2)}) %all-to-all-start) | async-done | bytes 131104 | tf_op jit(solution)/shard_map/all_to_all | solution.py:39
  33.0 0.0 collective-permute-done.refs_0_
  33.0 1.6 fusion.15
  34.5 0.0 collective-permute-start.2
  34.5 2.7 %collective-permute-start.1 = (bf16[256,2304]{1,0:T(8,128)(2,1)}, bf16[256,2304]{1,0:T(8,128)(2,1)}, u32[]{:S(2)}, u32[]{:S(2)}) collective-permute-start(bf16[256,2304]{1,0:T(8,128)(2,1)} %get-tuple-element.21), channel_id=1, source_target_pairs={{0,6},{2,0},{4,2},{6,4},{1,7},{3,1},{5,3},{7,5},{8,14},{10,8},{12,... | collective-permute-start | bytes 3538952 | tf_op jit(solution)/shard_map/ppermute | solution.py:31
  37.2 0.9 broadcast_select_fusion
  38.2 8.2 %all-to-all-start.1 = ((bf16[8,256,128]{2,1,0:T(8,128)(2,1)}), bf16[8,256,128]{2,1,0:T(8,128)(2,1)S(1)}, u32[]{:S(2)}, u32[]{:S(2)}) async-start(bf16[8,256,128]{2,1,0:T(8,128)(2,1)} %broadcast_select_fusion), calls=%async_computation.1 | async-start | bytes 1048576 | tf_op jit(solution)/shard_map/all_to_all | solution.py:39
  46.4 0.0 collective-permute-start.5
  46.4 0.1 slice.30
  46.5 1.1 pad_maximum_fusion
  47.6 2.7 %collective-permute-start.7 = (bf16[128,2304]{1,0:T(8,128)(2,1)}, bf16[128,2304]{1,0:T(8,128)(2,1)S(1)}, u32[]{:S(2)}, u32[]{:S(2)}) collective-permute-start(bf16[128,2304]{1,0:T(8,128)(2,1)} %get-tuple-element.22), channel_id=1, source_target_pairs={{0,56},{8,0},{16,8},{24,16},{32,24},{40,32},{48,40},{56,48},{1,57}... | collective-permute-start | bytes 1769480 | tf_op jit(solution)/shard_map/ppermute | solution.py:31
  50.3 0.0 collective-permute-start.6
  50.3 14.0 %all-to-all-done.1 = bf16[8,256,128]{2,1,0:T(8,128)(2,1)S(1)} async-done(((bf16[8,256,128]{2,1,0:T(8,128)(2,1)}), bf16[8,256,128]{2,1,0:T(8,128)(2,1)S(1)}, u32[]{:S(2)}, u32[]{:S(2)}) %all-to-all-start.1) | async-done | bytes 524320 | tf_op jit(solution)/shard_map/all_to_all | solution.py:39
  64.3 0.0 collective-permute-done.1.refs_2_.refs_8_
  64.3 0.6 collective-permute-start.3
  64.9 0.1 collective-permute-start.4
  65.0 8.1 %collective-permute-done.7.refs_3_ = bf16[128,2304]{1,0:T(8,128)(2,1)S(1)} collective-permute-done((bf16[128,2304]{1,0:T(8,128)(2,1)}, bf16[128,2304]{1,0:T(8,128)(2,1)S(1)}, u32[]{:S(2)}, u32[]{:S(2)}) %collective-permute-start.7) | collective-permute-done | bytes 589856 | tf_op jit(solution)/shard_map/ppermute | solution.py:31
  73.1 0.1 collective-permute-start.9
  73.2 0.9 collective-permute-done.6.refs_2_
  74.2 0.4 collective-permute-start.8
  74.6 3.6 %all-to-all-start.2 = ((bf16[16,80,128]{2,1,0:T(8,128)(2,1)}), bf16[16,80,128]{2,1,0:T(8,128)(2,1)S(1)}, u32[]{:S(2)}, u32[]{:S(2)}) async-start(bf16[16,80,128]{2,1,0:T(8,128)(2,1)} %get-tuple-element.15), calls=%async_computation.2 | async-start | bytes 655360 | tf_op jit(solution)/shard_map/all_to_all | solution.py:39
  78.2 0.0 collective-permute-done.9.refs_5_
  78.2 4.7 %shard_map.104.refs_4_ = f32[128,2048]{1,0:T(8,128)S(1)} custom-call(s32[1]{0:T(128)} %bitcast.7.core, bf16[2048,128]{1,0:T(8,128)(2,1)S(1)} %bitcast.64, bf16[256,3072]{1,0:T(8,128)(2,1)S(1)} %collective-permute-done.refs_0_, bf16[256,3072]{1,0:T(8,128)(2,1)} %collective-permute-done.5.refs_1_, bf16[128,2304]{1,0:T(8,128)(2,1)} %collective-permute-done.6.refs_2_, ...), custom_call_target="tpu_custom_call" | custom-call | flops 2147483648 | bytes 4194304 | tf_op jit(solution)/shard_map/pallas_call | solution.py:230
  83.0 0.0 collective-permute-done.3.refs_1_.refs_7_
  83.0 0.0 collective-permute-done.4.refs_3_.refs_9_
  83.0 5.8 %shard_map.105 = bf16[8,256,128]{2,1,0:T(8,128)(2,1)} custom-call(s32[1]{0:T(128)} %bitcast.7.core, bf16[2048,128]{1,0:T(8,128)(2,1)S(1)} %bitcast.65, bf16[256,2304]{1,0:T(8,128)(2,1)} %collective-permute-done.2.refs_0_.refs_6_, bf16[256,2304]{1,0:T(8,128)(2,1)} %collective-permute-done.3.refs_1_.refs_7_, ...), custom_call_target="tpu_custom_call" | custom-call | flops 2147483648 | bytes 4194304 | tf_op jit(solution)/shard_map/pallas_call | solution.py:230
  88.8 0.7 copy-done.5
  89.6 7.0 %all-to-all-start.3 = ((bf16[8,256,128]{2,1,0:T(8,128)(2,1)}), bf16[8,256,128]{2,1,0:T(8,128)(2,1)S(1)}, u32[]{:S(2)}, u32[]{:S(2)}) async-start(bf16[8,256,128]{2,1,0:T(8,128)(2,1)} %shard_map.105), calls=%async_computation.3 | async-start | bytes 1048576 | tf_op jit(solution)/shard_map/all_to_all | solution.py:250
  96.6 0.9 dynamic-slice_bitcast_fusion
  97.5 0.5 slice.39
  98.8 15.7 %all-to-all-done.3 = bf16[8,256,128]{2,1,0:T(8,128)(2,1)S(1)} async-done(((bf16[8,256,128]{2,1,0:T(8,128)(2,1)}), bf16[8,256,128]{2,1,0:T(8,128)(2,1)S(1)}, u32[]{:S(2)}, u32[]{:S(2)}) %all-to-all-start.3) | async-done | bytes 524320 | tf_op jit(solution)/shard_map/all_to_all | solution.py:250
  114.5 0.1 convert_reduce_fusion.1
  114.6 0.1 convert_bitcast_fusion
  114.7 0.1 broadcast_in_dim.51
  114.8 18.5 %all_to_all.35 = bf16[8,256,128]{2,1,0:T(8,128)(2,1)S(1)} all-to-all(bf16[8,256,128]{2,1,0:T(8,128)(2,1)S(1)} %broadcast_in_dim.51), channel_id=1, replica_groups={{0,12,16,28,32,44,48,60},{2,14,18,30,34,46,50,62},{4,8,20,24,36,40,52,5..., dimensions={0} | all-to-all | bytes 1048576 | tf_op jit(solution)/shard_map/all_to_all | solution.py:250
  133.3 9.8 %shard_map.106 = bf16[8,256,128]{2,1,0:T(8,128)(2,1)} custom-call(s32[1]{0:T(128)} %bitcast.7.core, bf16[2048,128]{1,0:T(8,128)(2,1)S(1)} %bitcast.66, bf16[256,3072]{1,0:T(8,128)(2,1)S(1)} %collective-permute-done.refs_0_, bf16[256,3072]{1,0:T(8,128)(2,1)} %collective-permute-done.5.refs_1_, bf16[128,2304]{1,0:T(8,128)(2,1)} %collective-permute-done.6.refs_2_, ...), custom_call_target="tpu_custom_call" | custom-call | flops 4294967296 | bytes 8388608 | tf_op jit(solution)/shard_map/pallas_call | solution.py:230
  143.1 4.2 %all-to-all-start.5 = ((bf16[8,256,128]{2,1,0:T(8,128)(2,1)}), bf16[8,256,128]{2,1,0:T(8,128)(2,1)S(1)}, u32[]{:S(2)}, u32[]{:S(2)}) async-start(bf16[8,256,128]{2,1,0:T(8,128)(2,1)} %shard_map.106), calls=%async_computation.5 | async-start | bytes 1048576 | tf_op jit(solution)/shard_map/all_to_all | solution.py:250
  147.3 15.0 %all-to-all-done.5 = bf16[8,256,128]{2,1,0:T(8,128)(2,1)S(1)} async-done(((bf16[8,256,128]{2,1,0:T(8,128)(2,1)}), bf16[8,256,128]{2,1,0:T(8,128)(2,1)S(1)}, u32[]{:S(2)}, u32[]{:S(2)}) %all-to-all-start.5) | async-done | bytes 524320 | tf_op jit(solution)/shard_map/all_to_all | solution.py:250
  162.3 0.1 convert_reduce_fusion
  162.4 0.2 fusion.3
  162.6 0.0 copy-start.3
  162.7 0.1 broadcast_in_dim.52
  162.8 21.5 %all_to_all.36.arrived = bf16[32,3,32,128]{3,2,1,0:T(8,128)(2,1)S(1)} all-to-all(bf16[32,3,32,128]{3,2,1,0:T(8,128)(2,1)S(1)} %bitcast.67), channel_id=1, replica_groups=mesh['h'=2,'c'=2,'z'=8,'yh'=2,'yl'=2,'x'=2] {'h','c','yh','yl','x'}, dimensions={0} | all-to-all | bytes 1572864 | tf_op jit(solution)/shard_map/all_to_all | solution.py:39
  184.3 0.8 shard_map.107
  (21 shorter events, 0.1 us)
Async XLA Ops:
  0.6 8.0 %copy-start.4 = (s32[1,64]{1,0:T(1,128)S(1)}, s32[1,64]{1,0:T(1,128)}, u32[]{:S(2)}) copy-start(s32[1,64]{1,0:T(1,128)} %lengths.3) | copy-start | bytes 772
  0.6 8.0 %copy-start.1 = (f32[1,32,1024]{2,1,0:T(8,128)S(1)}, f32[1,32,1024]{2,1,0:T(8,128)}, u32[]{:S(2)}) copy-start(f32[1,32,1024]{2,1,0:T(8,128)} %second.3) | copy-start | bytes 393220
  0.7 8.0 %copy-start = (f32[1,32,1024]{2,1,0:T(8,128)S(1)}, f32[1,32,1024]{2,1,0:T(8,128)}, u32[]{:S(2)}) copy-start(f32[1,32,1024]{2,1,0:T(8,128)} %first.3) | copy-start | bytes 393220
  0.7 8.0 %copy-start.2 = (f32[32,256]{1,0:T(8,128)S(1)}, f32[32,256]{1,0:T(8,128)}, u32[]{:S(2)}) copy-start(f32[32,256]{1,0:T(8,128)} %param.17) | copy-start | bytes 98308
  4.2 28.8 %collective-permute-start = (bf16[256,3072]{1,0:T(8,128)(2,1)}, bf16[256,3072]{1,0:T(8,128)(2,1)S(1)}, u32[]{:S(2)}, u32[]{:S(2)}) collective-permute-start(bf16[256,3072]{1,0:T(8,128)(2,1)} %shard_map.102), channel_id=1, source_target_pairs={{0,0},{1,64},{64,1},{65,65},{2,2},{3,66},{66,3},{67,67},{4,4},{5,6... | collective-permute-start | bytes 4718600 | tf_op jit(solution)/shard_map/ppermute | solution.py:51
  10.5 22.5 %all-to-all-start = ((bf16[16,32,128]{2,1,0:T(8,128)(2,1)}), bf16[16,32,128]{2,1,0:T(8,128)(2,1)S(1)}, u32[]{:S(2)}, u32[]{:S(2)}) async-start(bf16[16,32,128]{2,1,0:T(8,128)(2,1)} %get-tuple-element.12), calls=%async_computation | async-start | bytes 262144 | tf_op jit(solution)/shard_map/all_to_all | solution.py:39
  34.5 29.8 %collective-permute-start.2 = (bf16[256,2304]{1,0:T(8,128)(2,1)}, bf16[256,2304]{1,0:T(8,128)(2,1)}, u32[]{:S(2)}, u32[]{:S(2)}) collective-permute-start(bf16[256,2304]{1,0:T(8,128)(2,1)} %get-tuple-element.20), channel_id=1, source_target_pairs={{0,2},{2,4},{4,6},{6,0},{1,3},{3,5},{5,7},{7,1},{8,10},{10,12},{12... | collective-permute-start | bytes 3538952 | tf_op jit(solution)/shard_map/ppermute | solution.py:31
  34.5 29.8 %collective-permute-start.1 = (bf16[256,2304]{1,0:T(8,128)(2,1)}, bf16[256,2304]{1,0:T(8,128)(2,1)}, u32[]{:S(2)}, u32[]{:S(2)}) collective-permute-start(bf16[256,2304]{1,0:T(8,128)(2,1)} %get-tuple-element.21), channel_id=1, source_target_pairs={{0,6},{2,0},{4,2},{6,4},{1,7},{3,1},{5,3},{7,5},{8,14},{10,8},{12,... | collective-permute-start | bytes 3538952 | tf_op jit(solution)/shard_map/ppermute | solution.py:31
  38.2 26.1 %all-to-all-start.1 = ((bf16[8,256,128]{2,1,0:T(8,128)(2,1)}), bf16[8,256,128]{2,1,0:T(8,128)(2,1)S(1)}, u32[]{:S(2)}, u32[]{:S(2)}) async-start(bf16[8,256,128]{2,1,0:T(8,128)(2,1)} %broadcast_select_fusion), calls=%async_computation.1 | async-start | bytes 1048576 | tf_op jit(solution)/shard_map/all_to_all | solution.py:39
  46.4 31.8 %collective-permute-start.5 = (bf16[256,3072]{1,0:T(8,128)(2,1)S(1)}, bf16[256,3072]{1,0:T(8,128)(2,1)}, u32[]{:S(2)}, u32[]{:S(2)}) collective-permute-start(bf16[256,3072]{1,0:T(8,128)(2,1)S(1)} %collective-permute-done.refs_0_), channel_id=1, source_target_pairs={{0,64},{64,0},{1,65},{65,1},{2,66},{66,2},{3,67},{67,3},{4,68},{68... | collective-permute-start | bytes 4718600 | tf_op jit(solution)/shard_map/ppermute | solution.py:31
  47.6 25.5 %collective-permute-start.7 = (bf16[128,2304]{1,0:T(8,128)(2,1)}, bf16[128,2304]{1,0:T(8,128)(2,1)S(1)}, u32[]{:S(2)}, u32[]{:S(2)}) collective-permute-start(bf16[128,2304]{1,0:T(8,128)(2,1)} %get-tuple-element.22), channel_id=1, source_target_pairs={{0,56},{8,0},{16,8},{24,16},{32,24},{40,32},{48,40},{56,48},{1,57}... | collective-permute-start | bytes 1769480 | tf_op jit(solution)/shard_map/ppermute | solution.py:31
  50.3 23.9 %collective-permute-start.6 = (bf16[128,2304]{1,0:T(8,128)(2,1)}, bf16[128,2304]{1,0:T(8,128)(2,1)}, u32[]{:S(2)}, u32[]{:S(2)}) collective-permute-start(bf16[128,2304]{1,0:T(8,128)(2,1)} %get-tuple-element.23), channel_id=1, source_target_pairs={{0,8},{8,16},{16,24},{24,32},{32,40},{40,48},{48,56},{56,0},{1,9},... | collective-permute-start | bytes 1769480 | tf_op jit(solution)/shard_map/ppermute | solution.py:31
  64.3 18.7 %collective-permute-start.3 = (bf16[256,2304]{1,0:T(8,128)(2,1)}, bf16[256,2304]{1,0:T(8,128)(2,1)}, u32[]{:S(2)}, u32[]{:S(2)}) collective-permute-start(bf16[256,2304]{1,0:T(8,128)(2,1)} %collective-permute-done.2.refs_0_.refs_6_), channel_id=1, source_target_pairs={{0,64},{64,0},{1,65},{65,1},{2,66},{66,2},{3,67},{67,3},{4,68},{68... | collective-permute-start | bytes 3538952 | tf_op jit(solution)/shard_map/ppermute | solution.py:31
  64.9 18.1 %collective-permute-start.4 = (bf16[256,2304]{1,0:T(8,128)(2,1)}, bf16[256,2304]{1,0:T(8,128)(2,1)}, u32[]{:S(2)}, u32[]{:S(2)}) collective-permute-start(bf16[256,2304]{1,0:T(8,128)(2,1)} %collective-permute-done.1.refs_2_.refs_8_), channel_id=1, source_target_pairs={{0,64},{64,0},{1,65},{65,1},{2,66},{66,2},{3,67},{67,3},{4,68},{68... | collective-permute-start | bytes 3538952 | tf_op jit(solution)/shard_map/ppermute | solution.py:31
  73.1 5.1 %collective-permute-start.9 = (bf16[128,2304]{1,0:T(8,128)(2,1)S(1)}, bf16[128,2304]{1,0:T(8,128)(2,1)}, u32[]{:S(2)}, u32[]{:S(2)}) collective-permute-start(bf16[128,2304]{1,0:T(8,128)(2,1)S(1)} %collective-permute-done.7.refs_3_), channel_id=1, source_target_pairs={{0,64},{64,0},{1,65},{65,1},{2,66},{66,2},{3,67},{67,3},{4,68},{68... | collective-permute-start | bytes 1769480 | tf_op jit(solution)/shard_map/ppermute | solution.py:31
  74.2 4.0 %collective-permute-start.8 = (bf16[128,2304]{1,0:T(8,128)(2,1)}, bf16[128,2304]{1,0:T(8,128)(2,1)}, u32[]{:S(2)}, u32[]{:S(2)}) collective-permute-start(bf16[128,2304]{1,0:T(8,128)(2,1)} %collective-permute-done.6.refs_2_), channel_id=1, source_target_pairs={{0,64},{64,0},{1,65},{65,1},{2,66},{66,2},{3,67},{67,3},{4,68},{68... | collective-permute-start | bytes 1769480 | tf_op jit(solution)/shard_map/ppermute | solution.py:31
  74.6 14.3 %all-to-all-start.2 = ((bf16[16,80,128]{2,1,0:T(8,128)(2,1)}), bf16[16,80,128]{2,1,0:T(8,128)(2,1)S(1)}, u32[]{:S(2)}, u32[]{:S(2)}) async-start(bf16[16,80,128]{2,1,0:T(8,128)(2,1)} %get-tuple-element.15), calls=%async_computation.2 | async-start | bytes 655360 | tf_op jit(solution)/shard_map/all_to_all | solution.py:39
  88.8 0.8 copy-start.5
  89.6 24.9 %all-to-all-start.3 = ((bf16[8,256,128]{2,1,0:T(8,128)(2,1)}), bf16[8,256,128]{2,1,0:T(8,128)(2,1)S(1)}, u32[]{:S(2)}, u32[]{:S(2)}) async-start(bf16[8,256,128]{2,1,0:T(8,128)(2,1)} %shard_map.105), calls=%async_computation.3 | async-start | bytes 1048576 | tf_op jit(solution)/shard_map/all_to_all | solution.py:250
  143.1 19.2 %all-to-all-start.5 = ((bf16[8,256,128]{2,1,0:T(8,128)(2,1)}), bf16[8,256,128]{2,1,0:T(8,128)(2,1)S(1)}, u32[]{:S(2)}, u32[]{:S(2)}) async-start(bf16[8,256,128]{2,1,0:T(8,128)(2,1)} %shard_map.106), calls=%async_computation.5 | async-start | bytes 1048576 | tf_op jit(solution)/shard_map/all_to_all | solution.py:250
  162.6 21.6 %copy-start.3 = (f32[32,256]{1,0:T(8,128)S(1)}, f32[32,256]{1,0:T(8,128)}, u32[]{:S(2)}) copy-start(f32[32,256]{1,0:T(8,128)} %mom.1) | copy-start | bytes 98308

commit v6 on v5

--- a/solution.py
+++ b/solution.py
@@ -264,10 +264,10 @@
     _, _, odd, colour = place()
     core = c.reshape(1).astype(jnp.int32)
 
-    mine = turned(prepare(lengths, tokens, targets))
     start, moments = pack(lengths, outer_param, first_mom, second_mom)
     start = exchange(start, ("h", "yh", "yl", "x"))
-    mine, start = together(mine, start)
+    mine, start = together(prepare(lengths, tokens, targets), start)
+    mine = turned(mine)
     theirs = other_core(mine)
 
     below, above = up(mine[:, : D + WIDE]), down(mine[:, WIDE : D + 2 * WIDE])
@@ -275,7 +275,6 @@
     plane = jnp.concatenate(
         [mine[:, WIDE : WIDE + D], mine[:, D + 2 * WIDE : D + 3 * WIDE]], 1
     )
-    before, behind = shift(plane[:half], "z", 1), shift(plane[half:], "z", -1)
 
     start = start.reshape(2, 256, BLOCK)
     here = pick(start, colour // 2, 0)
@@ -285,17 +284,19 @@
     )
     weights = exchange(weights, "z").reshape(D, BLOCK)
     start = here.astype(jnp.float32)
+    plane, weights = together(plane, weights)
+    before, behind = shift(plane[:half], "z", 1), shift(plane[half:], "z", -1)
 
     moments, weights = together(moments, weights)
     moments = exchange(moments, ("c", "yh", "yl", "x"))
     moments = pick(moments.reshape(2, 8, 80, BLOCK), x, 0)
 
-    weights, above = together(weights, above)
     near = [(block, WIDE, D + 3 * WIDE) for block in (mine, theirs)]
     near += [
         (block, 0, D)
         for block in (before, behind, other_core(before), other_core(behind))
     ]
+    moments, below, above = together(moments, below, above)
     sides = [(block, WIDE, 0) for block in (below, other_core(below))]
     sides += [(block, 0, D) for block in (above, other_core(above))]
     grad = product(near, core, weights)

time: 186 us -> 187 us (level)
  waiting for transfers between devices: 69.7 us -> 58.1 us
  local copies, waits for them, and re-layouts: 4.07 us -> 10.2 us
  other arithmetic: 2.62 us -> 5.07 us
  starting transfers between devices: 40.6 us -> 42.8 us
  blocking collectives: 40 us -> 42 us
    all_to_all x3, waiting for transfers between devices: 30 us -> 13.8 us  [exchange(): return lax.all_to_all(x, axes, 0, 0, tiled=True)]
    ppermute x1, waiting for transfers between devices: 0.01 us -> 9.5 us  [turned(): return lax.ppermute(x, ('c', 'x'), TURN)]
    all_to_all x2, waiting for transfers between devices: 30.7 us -> 28 us  [among_peers(): return lax.all_to_all(x, axes, 0, 0, axis_index_groups=PEERS, tiled=True)]
    unnamed x12 -> x22, local copies, waits for them, and re-layouts: 0.77 us -> 3.26 us
    slice x0 -> x1, local copies, waits for them, and re-layouts: none -> 2.32 us  [per_device(): before, behind = (shift(plane[:half], 'z', 1), shift(plane[half:], 'z', -1))]
    ppermute x9, waiting for transfers between devices: 9.05 us -> 6.84 us  [shift(): return lax.ppermute(x, axis, [(i, (i + by) % size) for i in range(size)])]
    all_to_all x1, blocking collectives: 18.5 us -> 20.6 us  [among_peers(): return lax.all_to_all(x, axes, 0, 0, axis_index_groups=PEERS, tiled=True)]
    all_to_all x3, starting transfers between devices: 18.3 us -> 20.2 us  [exchange(): return lax.all_to_all(x, axes, 0, 0, tiled=True)]
  transfers between devices with their start and end apart: 15 -> 15, of which waited for: 6 -> 9; matrix products, arithmetic and copies ran while one was open for 2% -> 6% of each run, Pallas kernels for 7% -> 4%
where the time goes in v6:
time: 187 us; the launch traced here: 186 us
  waiting for transfers between devices  58.1 us (31%)
  starting transfers between devices  42.8 us (23%)
  blocking collectives  42 us (22%)
  Pallas kernels  26 us (14%)
  local copies, waits for them, and re-layouts  10.2 us (5%)
  other arithmetic  5.07 us (3%)
    all_to_all x2, waiting for transfers between devices, among_peers(): return lax.all_to_all(x, axes, 0, 0, axis_index_groups=PEERS, tiled=True)  28 us
    all_to_all x1, blocking collectives, exchange(): return lax.all_to_all(x, axes, 0, 0, tiled=True)  21.4 us
    all_to_all x1, blocking collectives, among_peers(): return lax.all_to_all(x, axes, 0, 0, axis_index_groups=PEERS, tiled=True)  20.6 us
    all_to_all x3, starting transfers between devices, exchange(): return lax.all_to_all(x, axes, 0, 0, tiled=True)  20.2 us
    pallas_call x3, Pallas kernels, product(): pl.pallas_call(functools.partial(product_kernel, layout, last), out_shape...  20.1 us
    all_to_all x3, waiting for transfers between devices, exchange(): return lax.all_to_all(x, axes, 0, 0, tiled=True)  13.8 us
    all_to_all x2, starting transfers between devices, among_peers(): return lax.all_to_all(x, axes, 0, 0, axis_index_groups=PEERS, tiled=True)  11 us
    ppermute x1, waiting for transfers between devices, turned(): return lax.ppermute(x, ('c', 'x'), TURN)  9.5 us
  transfers between devices with their start and end apart: 15, of which 9 were waited for; matrix products, arithmetic and copies ran while one was open for 6% of the time, Pallas kernels for 4%

profile of v6, /device:TPU:1, one launch (start us, length us, event | category | flops | bytes accessed | tf_op | source)
XLA Modules:
  0.0 185.8 jit_solution(8733959108777955698)
XLA Ops:
  0.6 0.9 copy-done
  1.5 0.9 copy-done.2
  2.4 0.8 copy-done.4
  3.2 0.7 copy-done.7
  3.9 1.7 shard_map.103
  5.6 7.6 %all-to-all-start = ((bf16[16,32,128]{2,1,0:T(8,128)(2,1)}), bf16[16,32,128]{2,1,0:T(8,128)(2,1)S(1)}, u32[]{:S(2)}, u32[]{:S(2)}) async-start(bf16[16,32,128]{2,1,0:T(8,128)(2,1)} %get-tuple-element.15), calls=%async_computation | async-start | bytes 262144 | tf_op jit(solution)/shard_map/all_to_all | solution.py:39
  13.2 3.4 %shard_map.102 = bf16[256,3072]{1,0:T(8,128)(2,1)} custom-call(s32[1,64]{1,0:T(1,128)} %lengths.3, bf16[1,256,2048]{2,1,0:T(8,128)(2,1)} %tokens.1, bf16[1,256,1024]{2,1,0:T(8,128)(2,1)} %targets.1), custom_call_target="tpu_custom_call" | custom-call | tf_op jit(solution)/shard_map/pallas_call | solution.py:93
  16.6 3.5 %all-to-all-done = bf16[16,32,128]{2,1,0:T(8,128)(2,1)S(1)} async-done(((bf16[16,32,128]{2,1,0:T(8,128)(2,1)}), bf16[16,32,128]{2,1,0:T(8,128)(2,1)S(1)}, u32[]{:S(2)}, u32[]{:S(2)}) %all-to-all-start) | async-done | bytes 131104 | tf_op jit(solution)/shard_map/all_to_all | solution.py:39
  20.0 4.2 %collective-permute-start = (bf16[256,3072]{1,0:T(8,128)(2,1)}, bf16[256,3072]{1,0:T(8,128)(2,1)S(1)}, u32[]{:S(2)}, u32[]{:S(2)}) collective-permute-start(bf16[256,3072]{1,0:T(8,128)(2,1)} %shard_map.102), channel_id=1, source_target_pairs={{0,0},{1,64},{64,1},{65,65},{2,2},{3,66},{66,3},{67,67},{4,4},{5,6... | collective-permute-start | bytes 4718600 | tf_op jit(solution)/shard_map/ppermute | solution.py:51
  24.3 0.9 broadcast_select_fusion
  25.2 8.2 %all-to-all-start.1 = ((bf16[8,256,128]{2,1,0:T(8,128)(2,1)}), bf16[8,256,128]{2,1,0:T(8,128)(2,1)S(1)}, u32[]{:S(2)}, u32[]{:S(2)}) async-start(bf16[8,256,128]{2,1,0:T(8,128)(2,1)} %broadcast_select_fusion), calls=%async_computation.1 | async-start | bytes 1048576 | tf_op jit(solution)/shard_map/all_to_all | solution.py:39
  33.4 9.5 %collective-permute-done.refs_0_ = bf16[256,3072]{1,0:T(8,128)(2,1)S(1)} collective-permute-done((bf16[256,3072]{1,0:T(8,128)(2,1)}, bf16[256,3072]{1,0:T(8,128)(2,1)S(1)}, u32[]{:S(2)}, u32[]{:S(2)}) %collective-permute-start) | collective-permute-done | bytes 1572896 | tf_op jit(solution)/shard_map/ppermute | solution.py:51
  42.9 1.6 fusion.14
  44.5 2.7 %collective-permute-start.2 = (bf16[256,2304]{1,0:T(8,128)(2,1)}, bf16[256,2304]{1,0:T(8,128)(2,1)}, u32[]{:S(2)}, u32[]{:S(2)}) collective-permute-start(bf16[256,2304]{1,0:T(8,128)(2,1)} %get-tuple-element.26), channel_id=1, source_target_pairs={{0,6},{2,0},{4,2},{6,4},{1,7},{3,1},{5,3},{7,5},{8,14},{10,8},{12,... | collective-permute-start | bytes 3538952 | tf_op jit(solution)/shard_map/ppermute | solution.py:31
  47.2 0.1 slice.36
  47.3 1.1 pad_maximum_fusion
  48.4 3.0 %all-to-all-done.1 = bf16[8,256,128]{2,1,0:T(8,128)(2,1)S(1)} async-done(((bf16[8,256,128]{2,1,0:T(8,128)(2,1)}), bf16[8,256,128]{2,1,0:T(8,128)(2,1)S(1)}, u32[]{:S(2)}, u32[]{:S(2)}) %all-to-all-start.1) | async-done | bytes 524320 | tf_op jit(solution)/shard_map/all_to_all | solution.py:39
  51.4 4.4 %all-to-all-start.2 = ((bf16[16,80,128]{2,1,0:T(8,128)(2,1)}), bf16[16,80,128]{2,1,0:T(8,128)(2,1)}, u32[]{:S(2)}, u32[]{:S(2)}) async-start(bf16[16,80,128]{2,1,0:T(8,128)(2,1)} %get-tuple-element.20), calls=%async_computation.2 | async-start | bytes 655360 | tf_op jit(solution)/shard_map/all_to_all | solution.py:39
  55.9 0.3 collective-permute-start.5
  56.2 2.3 %fusion.15 = (bf16[128,2304]{1,0:T(8,128)(2,1)}, bf16[128,2304]{1,0:T(8,128)(2,1)}) fusion(bf16[256,2304]{1,0:T(8,128)(2,1)} %pad_maximum_fusion), kind=kLoop, calls=%fused_computation.36 | loop fusion | bytes 2359296 | tf_op jit(solution)/shard_map/slice | solution.py:288
  58.5 0.2 collective-permute-start.6
  58.8 2.4 %collective-permute-start.7 = (bf16[128,2304]{1,0:T(8,128)(2,1)}, bf16[128,2304]{1,0:T(8,128)(2,1)}, u32[]{:S(2)}, u32[]{:S(2)}) collective-permute-start(bf16[128,2304]{1,0:T(8,128)(2,1)} %get-tuple-element.28), channel_id=1, source_target_pairs={{0,56},{8,0},{16,8},{24,16},{32,24},{40,32},{48,40},{56,48},{1,57}... | collective-permute-start | bytes 1769480 | tf_op jit(solution)/shard_map/ppermute | solution.py:31
  61.2 7.3 %all-to-all-done.2 = bf16[16,80,128]{2,1,0:T(8,128)(2,1)} async-done(((bf16[16,80,128]{2,1,0:T(8,128)(2,1)}), bf16[16,80,128]{2,1,0:T(8,128)(2,1)}, u32[]{:S(2)}, u32[]{:S(2)}) %all-to-all-start.2) | async-done | bytes 327712 | tf_op jit(solution)/shard_map/all_to_all | solution.py:39
  68.4 1.6 dynamic-slice_bitcast_fusion
  70.1 0.6 collective-permute-start.3
  70.7 0.1 collective-permute-start.4
  70.8 4.0 %collective-permute-done.6.refs_2_ = bf16[128,2304]{1,0:T(8,128)(2,1)} collective-permute-done((bf16[128,2304]{1,0:T(8,128)(2,1)}, bf16[128,2304]{1,0:T(8,128)(2,1)}, u32[]{:S(2)}, u32[]{:S(2)}) %collective-permute-start.6) | collective-permute-done | bytes 589856 | tf_op jit(solution)/shard_map/ppermute | solution.py:31
  74.8 1.0 collective-permute-start.8
  75.8 2.0 %collective-permute-done.8.refs_4_ = bf16[128,2304]{1,0:T(8,128)(2,1)} collective-permute-done((bf16[128,2304]{1,0:T(8,128)(2,1)}, bf16[128,2304]{1,0:T(8,128)(2,1)}, u32[]{:S(2)}, u32[]{:S(2)}) %collective-permute-start.8) | collective-permute-done | bytes 589856 | tf_op jit(solution)/shard_map/ppermute | solution.py:31
  77.8 0.8 collective-permute-done.9.refs_5_
  78.6 4.7 %shard_map.104.refs_4_ = f32[128,2048]{1,0:T(8,128)S(1)} custom-call(s32[1]{0:T(128)} %bitcast.7.core, bf16[2048,128]{1,0:T(8,128)(2,1)S(1)} %bitcast.64, bf16[256,3072]{1,0:T(8,128)(2,1)S(1)} %collective-permute-done.refs_0_, bf16[256,3072]{1,0:T(8,128)(2,1)} %collective-permute-done.5.refs_1_, bf16[128,2304]{1,0:T(8,128)(2,1)} %collective-permute-done.6.refs_2_, ...), custom_call_target="tpu_custom_call" | custom-call | flops 2147483648 | bytes 4194304 | tf_op jit(solution)/shard_map/pallas_call | solution.py:230
  83.4 5.6 %shard_map.105 = bf16[8,256,128]{2,1,0:T(8,128)(2,1)} custom-call(s32[1]{0:T(128)} %bitcast.7.core, bf16[2048,128]{1,0:T(8,128)(2,1)S(1)} %bitcast.65, bf16[256,2304]{1,0:T(8,128)(2,1)S(1)} %collective-permute-done.1.refs_0_.refs_6_, bf16[256,2304]{1,0:T(8,128)(2,1)} %collective-permute-done.3.refs_1_.refs_7_, ...), custom_call_target="tpu_custom_call" | custom-call | flops 2147483648 | bytes 4194304 | tf_op jit(solution)/shard_map/pallas_call | solution.py:230
  89.0 6.4 %all-to-all-start.3 = ((bf16[8,256,128]{2,1,0:T(8,128)(2,1)}), bf16[8,256,128]{2,1,0:T(8,128)(2,1)S(1)}, u32[]{:S(2)}, u32[]{:S(2)}) async-start(bf16[8,256,128]{2,1,0:T(8,128)(2,1)} %shard_map.105), calls=%async_computation.3 | async-start | bytes 1048576 | tf_op jit(solution)/shard_map/all_to_all | solution.py:250
  95.3 1.2 slice.34
  97.2 1.6 convert_multiply_fusion.1
  98.8 12.7 %all-to-all-done.3 = bf16[8,256,128]{2,1,0:T(8,128)(2,1)S(1)} async-done(((bf16[8,256,128]{2,1,0:T(8,128)(2,1)}), bf16[8,256,128]{2,1,0:T(8,128)(2,1)S(1)}, u32[]{:S(2)}, u32[]{:S(2)}) %all-to-all-start.3) | async-done | bytes 524320 | tf_op jit(solution)/shard_map/all_to_all | solution.py:250
  111.5 0.1 convert_reduce_fusion.1
  111.6 1.1 convert_bitcast_fusion
  112.6 0.1 broadcast_in_dim.51
  112.7 20.6 %all_to_all.35 = bf16[8,256,128]{2,1,0:T(8,128)(2,1)S(1)} all-to-all(bf16[8,256,128]{2,1,0:T(8,128)(2,1)S(1)} %broadcast_in_dim.51), channel_id=1, replica_groups={{0,12,16,28,32,44,48,60},{2,14,18,30,34,46,50,62},{4,8,20,24,36,40,52,5..., dimensions={0} | all-to-all | bytes 1048576 | tf_op jit(solution)/shard_map/all_to_all | solution.py:250
  133.3 9.8 %shard_map.106 = bf16[8,256,128]{2,1,0:T(8,128)(2,1)} custom-call(s32[1]{0:T(128)} %bitcast.7.core, bf16[2048,128]{1,0:T(8,128)(2,1)S(1)} %bitcast.66, bf16[256,3072]{1,0:T(8,128)(2,1)S(1)} %collective-permute-done.refs_0_, bf16[256,3072]{1,0:T(8,128)(2,1)} %collective-permute-done.5.refs_1_, bf16[128,2304]{1,0:T(8,128)(2,1)} %collective-permute-done.6.refs_2_, ...), custom_call_target="tpu_custom_call" | custom-call | flops 4294967296 | bytes 8388608 | tf_op jit(solution)/shard_map/pallas_call | solution.py:230
  143.2 4.6 %all-to-all-start.5 = ((bf16[8,256,128]{2,1,0:T(8,128)(2,1)}), bf16[8,256,128]{2,1,0:T(8,128)(2,1)S(1)}, u32[]{:S(2)}, u32[]{:S(2)}) async-start(bf16[8,256,128]{2,1,0:T(8,128)(2,1)} %shard_map.106), calls=%async_computation.5 | async-start | bytes 1048576 | tf_op jit(solution)/shard_map/all_to_all | solution.py:250
  147.8 15.3 %all-to-all-done.5 = bf16[8,256,128]{2,1,0:T(8,128)(2,1)S(1)} async-done(((bf16[8,256,128]{2,1,0:T(8,128)(2,1)}), bf16[8,256,128]{2,1,0:T(8,128)(2,1)S(1)}, u32[]{:S(2)}, u32[]{:S(2)}) %all-to-all-start.5) | async-done | bytes 524320 | tf_op jit(solution)/shard_map/all_to_all | solution.py:250
  163.0 0.1 convert_reduce_fusion
  163.2 0.2 fusion.2
  163.5 0.1 broadcast_in_dim.52
  163.6 21.4 %all_to_all.36.arrived = bf16[32,3,32,128]{3,2,1,0:T(8,128)(2,1)S(1)} all-to-all(bf16[32,3,32,128]{3,2,1,0:T(8,128)(2,1)S(1)} %bitcast.67), channel_id=1, replica_groups=mesh['h'=2,'c'=2,'z'=8,'yh'=2,'yl'=2,'x'=2] {'h','c','yh','yl','x'}, dimensions={0} | all-to-all | bytes 1572864 | tf_op jit(solution)/shard_map/all_to_all | solution.py:39
  185.0 0.8 shard_map.107
  (32 shorter events, 0.2 us)
Async XLA Ops:
  0.6 0.9 copy-start
  1.5 0.9 copy-start.2
  2.4 0.8 copy-start.4
  3.2 0.7 copy-start.7
  5.6 14.4 %all-to-all-start = ((bf16[16,32,128]{2,1,0:T(8,128)(2,1)}), bf16[16,32,128]{2,1,0:T(8,128)(2,1)S(1)}, u32[]{:S(2)}, u32[]{:S(2)}) async-start(bf16[16,32,128]{2,1,0:T(8,128)(2,1)} %get-tuple-element.15), calls=%async_computation | async-start | bytes 262144 | tf_op jit(solution)/shard_map/all_to_all | solution.py:39
  20.0 24.5 %copy-start.9 = (bf16[16,32,128]{2,1,0:T(8,128)(2,1)}, bf16[16,32,128]{2,1,0:T(8,128)(2,1)S(1)}, u32[]{:S(2)}) copy-start(bf16[16,32,128]{2,1,0:T(8,128)(2,1)S(1)} %all-to-all-done) | copy-start | bytes 393220
  20.0 22.9 %collective-permute-start = (bf16[256,3072]{1,0:T(8,128)(2,1)}, bf16[256,3072]{1,0:T(8,128)(2,1)S(1)}, u32[]{:S(2)}, u32[]{:S(2)}) collective-permute-start(bf16[256,3072]{1,0:T(8,128)(2,1)} %shard_map.102), channel_id=1, source_target_pairs={{0,0},{1,64},{64,1},{65,65},{2,2},{3,66},{66,3},{67,67},{4,4},{5,6... | collective-permute-start | bytes 4718600 | tf_op jit(solution)/shard_map/ppermute | solution.py:51
  25.2 26.2 %all-to-all-start.1 = ((bf16[8,256,128]{2,1,0:T(8,128)(2,1)}), bf16[8,256,128]{2,1,0:T(8,128)(2,1)S(1)}, u32[]{:S(2)}, u32[]{:S(2)}) async-start(bf16[8,256,128]{2,1,0:T(8,128)(2,1)} %broadcast_select_fusion), calls=%async_computation.1 | async-start | bytes 1048576 | tf_op jit(solution)/shard_map/all_to_all | solution.py:39
  44.5 25.6 %collective-permute-start.1 = (bf16[256,2304]{1,0:T(8,128)(2,1)}, bf16[256,2304]{1,0:T(8,128)(2,1)S(1)}, u32[]{:S(2)}, u32[]{:S(2)}) collective-permute-start(bf16[256,2304]{1,0:T(8,128)(2,1)} %get-tuple-element.27), channel_id=1, source_target_pairs={{0,2},{2,4},{4,6},{6,0},{1,3},{3,5},{5,7},{7,1},{8,10},{10,12},{12... | collective-permute-start | bytes 3538952 | tf_op jit(solution)/shard_map/ppermute | solution.py:31
  44.5 25.6 %collective-permute-start.2 = (bf16[256,2304]{1,0:T(8,128)(2,1)}, bf16[256,2304]{1,0:T(8,128)(2,1)}, u32[]{:S(2)}, u32[]{:S(2)}) collective-permute-start(bf16[256,2304]{1,0:T(8,128)(2,1)} %get-tuple-element.26), channel_id=1, source_target_pairs={{0,6},{2,0},{4,2},{6,4},{1,7},{3,1},{5,3},{7,5},{8,14},{10,8},{12,... | collective-permute-start | bytes 3538952 | tf_op jit(solution)/shard_map/ppermute | solution.py:31
  51.4 17.0 %all-to-all-start.2 = ((bf16[16,80,128]{2,1,0:T(8,128)(2,1)}), bf16[16,80,128]{2,1,0:T(8,128)(2,1)}, u32[]{:S(2)}, u32[]{:S(2)}) async-start(bf16[16,80,128]{2,1,0:T(8,128)(2,1)} %get-tuple-element.20), calls=%async_computation.2 | async-start | bytes 655360 | tf_op jit(solution)/shard_map/all_to_all | solution.py:39
  55.9 22.7 %collective-permute-start.5 = (bf16[256,3072]{1,0:T(8,128)(2,1)S(1)}, bf16[256,3072]{1,0:T(8,128)(2,1)}, u32[]{:S(2)}, u32[]{:S(2)}) collective-permute-start(bf16[256,3072]{1,0:T(8,128)(2,1)S(1)} %collective-permute-done.refs_0_), channel_id=1, source_target_pairs={{0,64},{64,0},{1,65},{65,1},{2,66},{66,2},{3,67},{67,3},{4,68},{68... | collective-permute-start | bytes 4718600 | tf_op jit(solution)/shard_map/ppermute | solution.py:31
  58.5 16.3 %collective-permute-start.6 = (bf16[128,2304]{1,0:T(8,128)(2,1)}, bf16[128,2304]{1,0:T(8,128)(2,1)}, u32[]{:S(2)}, u32[]{:S(2)}) collective-permute-start(bf16[128,2304]{1,0:T(8,128)(2,1)} %get-tuple-element.29), channel_id=1, source_target_pairs={{0,8},{8,16},{16,24},{24,32},{32,40},{40,48},{48,56},{56,0},{1,9},... | collective-permute-start | bytes 1769480 | tf_op jit(solution)/shard_map/ppermute | solution.py:31
  58.8 17.0 %collective-permute-start.7 = (bf16[128,2304]{1,0:T(8,128)(2,1)}, bf16[128,2304]{1,0:T(8,128)(2,1)}, u32[]{:S(2)}, u32[]{:S(2)}) collective-permute-start(bf16[128,2304]{1,0:T(8,128)(2,1)} %get-tuple-element.28), channel_id=1, source_target_pairs={{0,56},{8,0},{16,8},{24,16},{32,24},{40,32},{48,40},{56,48},{1,57}... | collective-permute-start | bytes 1769480 | tf_op jit(solution)/shard_map/ppermute | solution.py:31
  70.1 13.3 %collective-permute-start.3 = (bf16[256,2304]{1,0:T(8,128)(2,1)S(1)}, bf16[256,2304]{1,0:T(8,128)(2,1)}, u32[]{:S(2)}, u32[]{:S(2)}) collective-permute-start(bf16[256,2304]{1,0:T(8,128)(2,1)S(1)} %collective-permute-done.1.refs_0_.refs_6_), channel_id=1, source_target_pairs={{0,64},{64,0},{1,65},{65,1},{2,66},{66,2},{3,67},{67,3},{4,68},{68... | collective-permute-start | bytes 3538952 | tf_op jit(solution)/shard_map/ppermute | solution.py:31
  70.7 12.7 %collective-permute-start.4 = (bf16[256,2304]{1,0:T(8,128)(2,1)}, bf16[256,2304]{1,0:T(8,128)(2,1)}, u32[]{:S(2)}, u32[]{:S(2)}) collective-permute-start(bf16[256,2304]{1,0:T(8,128)(2,1)} %collective-permute-done.2.refs_2_.refs_8_), channel_id=1, source_target_pairs={{0,64},{64,0},{1,65},{65,1},{2,66},{66,2},{3,67},{67,3},{4,68},{68... | collective-permute-start | bytes 3538952 | tf_op jit(solution)/shard_map/ppermute | solution.py:31
  74.8 3.0 %collective-permute-start.8 = (bf16[128,2304]{1,0:T(8,128)(2,1)}, bf16[128,2304]{1,0:T(8,128)(2,1)}, u32[]{:S(2)}, u32[]{:S(2)}) collective-permute-start(bf16[128,2304]{1,0:T(8,128)(2,1)} %collective-permute-done.6.refs_2_), channel_id=1, source_target_pairs={{0,64},{64,0},{1,65},{65,1},{2,66},{66,2},{3,67},{67,3},{4,68},{68... | collective-permute-start | bytes 1769480 | tf_op jit(solution)/shard_map/ppermute | solution.py:31
  75.8 2.8 %collective-permute-start.9 = (bf16[128,2304]{1,0:T(8,128)(2,1)}, bf16[128,2304]{1,0:T(8,128)(2,1)}, u32[]{:S(2)}, u32[]{:S(2)}) collective-permute-start(bf16[128,2304]{1,0:T(8,128)(2,1)} %collective-permute-done.7.refs_3_), channel_id=1, source_target_pairs={{0,64},{64,0},{1,65},{65,1},{2,66},{66,2},{3,67},{67,3},{4,68},{68... | collective-permute-start | bytes 1769480 | tf_op jit(solution)/shard_map/ppermute | solution.py:31
  89.0 22.6 %all-to-all-start.3 = ((bf16[8,256,128]{2,1,0:T(8,128)(2,1)}), bf16[8,256,128]{2,1,0:T(8,128)(2,1)S(1)}, u32[]{:S(2)}, u32[]{:S(2)}) async-start(bf16[8,256,128]{2,1,0:T(8,128)(2,1)} %shard_map.105), calls=%async_computation.3 | async-start | bytes 1048576 | tf_op jit(solution)/shard_map/all_to_all | solution.py:250
  143.1 20.0 %copy-start.8 = (f32[8,32,128]{2,1,0:T(8,128)S(1)}, f32[8,32,128]{2,1,0:T(8,128)}, u32[]{:S(2)}) copy-start(f32[8,32,128]{2,1,0:T(8,128)} %get-tuple-element.31) | copy-start | bytes 393220
  143.1 20.0 %copy-start.10 = (bf16[16,32,128]{2,1,0:T(8,128)(2,1)S(1)}, bf16[16,32,128]{2,1,0:T(8,128)(2,1)}, u32[]{:S(2)}) copy-start(bf16[16,32,128]{2,1,0:T(8,128)(2,1)} %copy-done.9) | copy-start | bytes 393220
  143.2 19.9 %all-to-all-start.5 = ((bf16[8,256,128]{2,1,0:T(8,128)(2,1)}), bf16[8,256,128]{2,1,0:T(8,128)(2,1)S(1)}, u32[]{:S(2)}, u32[]{:S(2)}) async-start(bf16[8,256,128]{2,1,0:T(8,128)(2,1)} %shard_map.106), calls=%async_computation.5 | async-start | bytes 1048576 | tf_op jit(solution)/shard_map/all_to_all | solution.py:250
  163.4 21.6 %copy-start.1 = (f32[1,32,1024]{2,1,0:T(8,128)S(1)}, f32[1,32,1024]{2,1,0:T(8,128)}, u32[]{:S(2)}) copy-start(f32[1,32,1024]{2,1,0:T(8,128)} %first.3) | copy-start | bytes 393220
  163.4 21.6 %copy-start.3 = (f32[1,32,1024]{2,1,0:T(8,128)S(1)}, f32[1,32,1024]{2,1,0:T(8,128)}, u32[]{:S(2)}) copy-start(f32[1,32,1024]{2,1,0:T(8,128)} %second.3) | copy-start | bytes 393220
  163.4 21.6 %copy-start.5 = (f32[32,256]{1,0:T(8,128)S(1)}, f32[32,256]{1,0:T(8,128)}, u32[]{:S(2)}) copy-start(f32[32,256]{1,0:T(8,128)} %param.17) | copy-start | bytes 98308
  163.4 21.6 %copy-start.6 = (f32[32,256]{1,0:T(8,128)S(1)}, f32[32,256]{1,0:T(8,128)}, u32[]{:S(2)}) copy-start(f32[32,256]{1,0:T(8,128)} %mom.1) | copy-start | bytes 98308

commit v7 on v6

--- a/solution.py
+++ b/solution.py
@@ -105,33 +105,41 @@
     )(lengths, tokens, targets)
 
 
-def pack_kernel(lengths, param, first, second, weights, moments):
-    _, _, odd, _ = place()
+def pack_kernel(param, weights):
+    for slot in range(16):
+        yl = slot // 2 % 2
+        half = slice(yl * BLOCK, (yl + 1) * BLOCK)
+        weights[slot] = param[:, half].astype(jnp.bfloat16)
+
+
+def pack(param):
+    whole = pl.BlockSpec(memory_space=pltpu.VMEM)
+    return pl.pallas_call(
+        pack_kernel,
+        out_shape=jax.ShapeDtypeStruct((16, 32, BLOCK), jnp.bfloat16),
+        in_specs=[whole],
+        out_specs=whole,
+        compiler_params=pltpu.CompilerParams(vmem_limit_bytes=60 * 2**20),
+    )(param)
+
+
+def pack_moments_kernel(lengths, first, second, moments):
     count = lax.fori_loop(0, lengths.shape[1], lambda i, t: t + lengths[0, i], 0)
     count = (count // 128).astype(jnp.float32)
-    for slot in range(16):
-        core, yh, yl = slot // 8, slot // 4 % 2, slot // 2 % 2
-        half = slice(yl * BLOCK, (yl + 1) * BLOCK)
-        weights[slot] = param[:, half].astype(jnp.bfloat16)
-        column = lax.rem(yh + odd, 2) * (2 * WIDE) + core * WIDE + yl * BLOCK
-        columns = pl.ds(pl.multiple_of(column, BLOCK), BLOCK)
-        moments[slot, 0:32] = first[0, :, columns].astype(jnp.bfloat16)
-        moments[slot, 32:64] = second[0, :, columns].astype(jnp.bfloat16)
-        moments[slot, 64:80] = jnp.full((16, BLOCK), count).astype(jnp.bfloat16)
-
-
-def pack(lengths, param, first, second):
+    moments[0:32] = first[0].astype(jnp.bfloat16)
+    moments[32:64] = second[0].astype(jnp.bfloat16)
+    moments[64:80] = jnp.full((16, 8 * BLOCK), count).astype(jnp.bfloat16)
+
+
+def pack_moments(lengths, first, second):
     whole = pl.BlockSpec(memory_space=pltpu.VMEM)
     return pl.pallas_call(
-        pack_kernel,
-        out_shape=[
-            jax.ShapeDtypeStruct((16, 32, BLOCK), jnp.bfloat16),
-            jax.ShapeDtypeStruct((16, 80, BLOCK), jnp.bfloat16),
-        ],
-        in_specs=[pl.BlockSpec(memory_space=pltpu.SMEM), whole, whole, whole],
-        out_specs=[whole, whole],
+        pack_moments_kernel,
+        out_shape=jax.ShapeDtypeStruct((80, 8 * BLOCK), jnp.bfloat16),
+        in_specs=[pl.BlockSpec(memory_space=pltpu.SMEM), whole, whole],
+        out_specs=whole,
         compiler_params=pltpu.CompilerParams(vmem_limit_bytes=16 * 2**20),
-    )(lengths, param, first, second)
+    )(lengths, first, second)
 
 
 def finish_kernel(
@@ -264,8 +272,7 @@
     _, _, odd, colour = place()
     core = c.reshape(1).astype(jnp.int32)
 
-    start, moments = pack(lengths, outer_param, first_mom, second_mom)
-    start = exchange(start, ("h", "yh", "yl", "x"))
+    start = exchange(pack(outer_param), ("h", "yh", "yl", "x"))
     mine, start = together(prepare(lengths, tokens, targets), start)
     mine = turned(mine)
     theirs = other_core(mine)
@@ -287,16 +294,16 @@
     plane, weights = together(plane, weights)
     before, behind = shift(plane[:half], "z", 1), shift(plane[half:], "z", -1)
 
-    moments, weights = together(moments, weights)
-    moments = exchange(moments, ("c", "yh", "yl", "x"))
-    moments = pick(moments.reshape(2, 8, 80, BLOCK), x, 0)
+    moments, start = together(pack_moments(lengths, first_mom, second_mom), start)
+    moments = lax.all_gather(turned(moments), ("yh", "yl", "c"), axis=0, tiled=True)
+    column = colour // 2 * (2 * WIDE) + c * WIDE + colour % 2 * BLOCK
+    moments = lax.dynamic_slice_in_dim(moments, column, BLOCK, 1).reshape(8, 80, BLOCK)
 
     near = [(block, WIDE, D + 3 * WIDE) for block in (mine, theirs)]
     near += [
         (block, 0, D)
         for block in (before, behind, other_core(before), other_core(behind))
     ]
-    moments, below, above = together(moments, below, above)
     sides = [(block, WIDE, 0) for block in (below, other_core(below))]
     sides += [(block, 0, D) for block in (above, other_core(above))]
     grad = product(near, core, weights)

time: 187 us -> 197 us (1.053)
  blocking collectives: 42 us -> 61.6 us
  between operations: 1.61 us -> 15.1 us
  waiting for transfers between devices: 58.1 us -> 47.5 us
  starting transfers between devices: 42.8 us -> 35.6 us
  local copies, waits for them, and re-layouts: 10.2 us -> 5.37 us
    all_to_all x1 -> x2, blocking collectives: 20.6 us -> 40.6 us  [among_peers(): return lax.all_to_all(x, axes, 0, 0, axis_index_groups=PEERS, tiled=True)]
    all_to_all x2 -> x1, waiting for transfers between devices: 28 us -> 13.2 us  [among_peers(): return lax.all_to_all(x, axes, 0, 0, axis_index_groups=PEERS, tiled=True)]
    ppermute x9, waiting for transfers between devices: 6.84 us -> 19.8 us  [shift(): return lax.ppermute(x, axis, [(i, (i + by) % size) for i in range(size)])]
    all_to_all x3 -> x2, waiting for transfers between devices: 13.8 us -> 6.81 us  [exchange(): return lax.all_to_all(x, axes, 0, 0, tiled=True)]
    all_to_all x3 -> x2, starting transfers between devices: 20.2 us -> 15.8 us  [exchange(): return lax.all_to_all(x, axes, 0, 0, tiled=True)]
    all_to_all x2 -> x1, starting transfers between devices: 11 us -> 6.91 us  [among_peers(): return lax.all_to_all(x, axes, 0, 0, axis_index_groups=PEERS, tiled=True)]
    unnamed x22 -> x18, local copies, waits for them, and re-layouts: 3.26 us -> 0.72 us
    ppermute x1 -> x2, starting transfers between devices: 4.17 us -> 6.07 us  [turned(): return lax.ppermute(x, ('c', 'x'), TURN)]
  transfers between devices with their start and end apart: 15 -> 15, of which waited for: 9 -> 7; matrix products, arithmetic and copies ran while one was open for 6% -> 4% of each run, Pallas kernels for 4% -> 7%
where the time goes in v7:
time: 197 us; the launch traced here: 196 us
  blocking collectives  61.6 us (31%)
  waiting for transfers between devices  47.5 us (24%)
  starting transfers between devices  35.6 us (18%)
  Pallas kernels  25.8 us (13%)
  between operations  15.1 us (8%)
  local copies, waits for them, and re-layouts  5.37 us (3%)
  other arithmetic  5.02 us (3%)
    all_to_all x2, blocking collectives, among_peers(): return lax.all_to_all(x, axes, 0, 0, axis_index_groups=PEERS, tiled=True)  40.6 us
    all_to_all x1, blocking collectives, exchange(): return lax.all_to_all(x, axes, 0, 0, tiled=True)  21 us
    ppermute x9, waiting for transfers between devices, shift(): return lax.ppermute(x, axis, [(i, (i + by) % size) for i in range(size)])  19.8 us
    pallas_call x3, Pallas kernels, product(): pl.pallas_call(functools.partial(product_kernel, layout, last), out_shape...  19.2 us
    all_to_all x2, starting transfers between devices, exchange(): return lax.all_to_all(x, axes, 0, 0, tiled=True)  15.8 us
    all_to_all x1, waiting for transfers between devices, among_peers(): return lax.all_to_all(x, axes, 0, 0, axis_index_groups=PEERS, tiled=True)  13.2 us
    ppermute x2, waiting for transfers between devices, turned(): return lax.ppermute(x, ('c', 'x'), TURN)  7.66 us
    all_to_all x1, starting transfers between devices, among_peers(): return lax.all_to_all(x, axes, 0, 0, axis_index_groups=PEERS, tiled=True)  6.91 us
  transfers between devices with their start and end apart: 15, of which 7 were waited for; matrix products, arithmetic and copies ran while one was open for 4% of the time, Pallas kernels for 7%

profile of v7, /device:TPU:1, one launch (start us, length us, event | category | flops | bytes accessed | tf_op | source)
XLA Modules:
  0.0 196.0 jit_solution(6156049600860406772)
XLA Ops:
  7.2 1.4 shard_map.104
  8.6 7.6 %all-to-all-start = ((bf16[16,32,128]{2,1,0:T(8,128)(2,1)}), bf16[16,32,128]{2,1,0:T(8,128)(2,1)S(1)}, u32[]{:S(2)}, u32[]{:S(2)}) async-start(bf16[16,32,128]{2,1,0:T(8,128)(2,1)} %shard_map.104), calls=%async_computation | async-start | bytes 262144 | tf_op jit(solution)/shard_map/all_to_all | solution.py:39
  16.2 3.5 %shard_map.103 = bf16[256,3072]{1,0:T(8,128)(2,1)} custom-call(s32[1,64]{1,0:T(1,128)} %lengths.3, bf16[1,256,2048]{2,1,0:T(8,128)(2,1)} %tokens.1, bf16[1,256,1024]{2,1,0:T(8,128)(2,1)} %targets.1), custom_call_target="tpu_custom_call" | custom-call | tf_op jit(solution)/shard_map/pallas_call | solution.py:93
  19.7 3.3 %all-to-all-done = bf16[16,32,128]{2,1,0:T(8,128)(2,1)S(1)} async-done(((bf16[16,32,128]{2,1,0:T(8,128)(2,1)}), bf16[16,32,128]{2,1,0:T(8,128)(2,1)S(1)}, u32[]{:S(2)}, u32[]{:S(2)}) %all-to-all-start) | async-done | bytes 131104 | tf_op jit(solution)/shard_map/all_to_all | solution.py:39
  23.0 4.2 %collective-permute-start.1 = (bf16[256,3072]{1,0:T(8,128)(2,1)}, bf16[256,3072]{1,0:T(8,128)(2,1)S(1)}, u32[]{:S(2)}, u32[]{:S(2)}) collective-permute-start(bf16[256,3072]{1,0:T(8,128)(2,1)} %shard_map.103), channel_id=1, source_target_pairs={{0,0},{1,64},{64,1},{65,65},{2,2},{3,66},{66,3},{67,67},{4,4},{5,6... | collective-permute-start | bytes 4718600 | tf_op jit(solution)/shard_map/ppermute | solution.py:51
  27.3 0.9 shard_map.102
  28.2 0.7 fusion.12
  28.9 1.9 collective-permute-start
  30.8 1.0 broadcast_select_fusion
  31.8 8.2 %all-to-all-start.1 = ((bf16[8,256,128]{2,1,0:T(8,128)(2,1)}), bf16[8,256,128]{2,1,0:T(8,128)(2,1)S(1)}, u32[]{:S(2)}, u32[]{:S(2)}) async-start(bf16[8,256,128]{2,1,0:T(8,128)(2,1)} %broadcast_select_fusion), calls=%async_computation.1 | async-start | bytes 1048576 | tf_op jit(solution)/shard_map/all_to_all | solution.py:39
  39.9 0.0 all-gather.2.cloned.1.call-start
  40.0 7.7 %collective-permute-done = bf16[80,1024]{1,0:T(8,128)(2,1)S(1)} collective-permute-done((bf16[80,1024]{1,0:T(8,128)(2,1)S(1)}, bf16[80,1024]{1,0:T(8,128)(2,1)S(1)}, u32[]{:S(2)}, u32[]{:S(2)}) %collective-permute-start) | collective-permute-done | bytes 163872 | tf_op jit(solution)/shard_map/ppermute | solution.py:51
  47.7 0.7 copy-done.8
  48.3 0.0 all-gather.2.cloned.1.call-update
  48.4 1.6 fusion.13
  50.0 2.7 %collective-permute-start.4 = (bf16[256,2304]{1,0:T(8,128)(2,1)}, bf16[256,2304]{1,0:T(8,128)(2,1)}, u32[]{:S(2)}, u32[]{:S(2)}) collective-permute-start(bf16[256,2304]{1,0:T(8,128)(2,1)} %get-tuple-element.18), channel_id=1, source_target_pairs={{0,6},{2,0},{4,2},{6,4},{1,7},{3,1},{5,3},{7,5},{8,14},{10,8},{12,... | collective-permute-start | bytes 3538952 | tf_op jit(solution)/shard_map/ppermute | solution.py:31
  52.7 0.1 slice.37
  52.7 1.1 pad_maximum_fusion
  53.9 3.5 %all-to-all-done.1 = bf16[8,256,128]{2,1,0:T(8,128)(2,1)S(1)} async-done(((bf16[8,256,128]{2,1,0:T(8,128)(2,1)}), bf16[8,256,128]{2,1,0:T(8,128)(2,1)S(1)}, u32[]{:S(2)}, u32[]{:S(2)}) %all-to-all-start.1) | async-done | bytes 524320 | tf_op jit(solution)/shard_map/all_to_all | solution.py:39
  57.3 0.4 collective-permute-start.6
  57.7 1.3 fusion.14
  59.1 0.1 collective-permute-start.7
  59.2 2.7 %collective-permute-start.8 = (bf16[128,2304]{1,0:T(8,128)(2,1)S(1)}, bf16[128,2304]{1,0:T(8,128)(2,1)}, u32[]{:S(2)}, u32[]{:S(2)}) collective-permute-start(bf16[128,2304]{1,0:T(8,128)(2,1)S(1)} %get-tuple-element.20), channel_id=1, source_target_pairs={{0,56},{8,0},{16,8},{24,16},{32,24},{40,32},{48,40},{56,48},{1,57}... | collective-permute-start | bytes 1769480 | tf_op jit(solution)/shard_map/ppermute | solution.py:31
  61.8 14.3 %collective-permute-done.2.refs_0_.refs_6_ = bf16[256,2304]{1,0:T(8,128)(2,1)S(1)} collective-permute-done((bf16[256,2304]{1,0:T(8,128)(2,1)}, bf16[256,2304]{1,0:T(8,128)(2,1)S(1)}, u32[]{:S(2)}, u32[]{:S(2)}) %collective-permute-start.2) | collective-permute-done | bytes 1179680 | tf_op jit(solution)/shard_map/ppermute | solution.py:31
  76.1 0.5 collective-permute-start.5
  76.6 0.1 collective-permute-start.9
  76.7 0.4 collective-permute-start.10
  77.1 4.7 %collective-permute-done.9.refs_4_ = bf16[128,2304]{1,0:T(8,128)(2,1)} collective-permute-done((bf16[128,2304]{1,0:T(8,128)(2,1)}, bf16[128,2304]{1,0:T(8,128)(2,1)}, u32[]{:S(2)}, u32[]{:S(2)}) %collective-permute-start.9) | collective-permute-done | bytes 589856 | tf_op jit(solution)/shard_map/ppermute | solution.py:31
  81.8 0.8 collective-permute-done.10.refs_5_
  82.7 4.7 %shard_map.105.refs_4_ = f32[128,2048]{1,0:T(8,128)S(1)} custom-call(s32[1]{0:T(128)} %bitcast.4.core, bf16[2048,128]{1,0:T(8,128)(2,1)S(1)} %bitcast.29, bf16[256,3072]{1,0:T(8,128)(2,1)S(1)} %collective-permute-done.1.refs_0_, bf16[256,3072]{1,0:T(8,128)(2,1)} %collective-permute-done.6.refs_1_, bf16[128,2304]{1,0:T(8,128)(2,1)} %collective-permute-done.7.refs_2_, ...), custom_call_target="tpu_custom_call" | custom-call | flops 2147483648 | bytes 4194304 | tf_op jit(solution)/shard_map/pallas_call | solution.py:238
  87.4 5.6 %shard_map.106 = bf16[8,256,128]{2,1,0:T(8,128)(2,1)} custom-call(s32[1]{0:T(128)} %bitcast.4.core, bf16[2048,128]{1,0:T(8,128)(2,1)S(1)} %bitcast.30, bf16[256,2304]{1,0:T(8,128)(2,1)S(1)} %collective-permute-done.2.refs_0_.refs_6_, bf16[256,2304]{1,0:T(8,128)(2,1)} %collective-permute-done.3.refs_1_.refs_7_, ...), custom_call_target="tpu_custom_call" | custom-call | flops 2147483648 | bytes 4194304 | tf_op jit(solution)/shard_map/pallas_call | solution.py:238
  93.0 6.9 %all-to-all-start.2 = ((bf16[8,256,128]{2,1,0:T(8,128)(2,1)}), bf16[8,256,128]{2,1,0:T(8,128)(2,1)S(1)}, u32[]{:S(2)}, u32[]{:S(2)}) async-start(bf16[8,256,128]{2,1,0:T(8,128)(2,1)} %shard_map.106), calls=%async_computation.2 | async-start | bytes 1048576 | tf_op jit(solution)/shard_map/all_to_all | solution.py:258
  99.9 0.0 all-gather.2.cloned.1.call-done
  99.9 0.9 constant_dynamic-slice_fusion
  100.9 0.5 slice.41
  102.1 0.7 convert_multiply_fusion
  102.8 13.2 %all-to-all-done.2 = bf16[8,256,128]{2,1,0:T(8,128)(2,1)S(1)} async-done(((bf16[8,256,128]{2,1,0:T(8,128)(2,1)}), bf16[8,256,128]{2,1,0:T(8,128)(2,1)S(1)}, u32[]{:S(2)}, u32[]{:S(2)}) %all-to-all-start.2) | async-done | bytes 524320 | tf_op jit(solution)/shard_map/all_to_all | solution.py:258
  116.0 0.1 convert_reduce_fusion.1
  116.0 1.1 fusion.10
  117.2 0.1 broadcast_in_dim.45
  117.3 20.9 %all_to_all.30 = bf16[8,256,128]{2,1,0:T(8,128)(2,1)S(1)} all-to-all(bf16[8,256,128]{2,1,0:T(8,128)(2,1)S(1)} %broadcast_in_dim.45), channel_id=1, replica_groups={{0,12,16,28,32,44,48,60},{2,14,18,30,34,46,50,62},{4,8,20,24,36,40,52,5..., dimensions={0} | all-to-all | bytes 1048576 | tf_op jit(solution)/shard_map/all_to_all | solution.py:258
  138.2 9.0 %shard_map.107 = bf16[8,256,128]{2,1,0:T(8,128)(2,1)S(1)} custom-call(s32[1]{0:T(128)} %bitcast.4.core, bf16[2048,128]{1,0:T(8,128)(2,1)S(1)} %bitcast.31, bf16[256,3072]{1,0:T(8,128)(2,1)S(1)} %collective-permute-done.1.refs_0_, bf16[256,3072]{1,0:T(8,128)(2,1)} %collective-permute-done.6.refs_1_, bf16[128,2304]{1,0:T(8,128)(2,1)} %collective-permute-done.7.refs_2_, ...), custom_call_target="tpu_custom_call" | custom-call | flops 4294967296 | bytes 8388608 | tf_op jit(solution)/shard_map/pallas_call | solution.py:238
  147.2 19.7 %all_to_all.31 = bf16[8,256,128]{2,1,0:T(8,128)(2,1)S(1)} all-to-all(bf16[8,256,128]{2,1,0:T(8,128)(2,1)S(1)} %shard_map.107), channel_id=1, replica_groups={{0,12,16,28,32,44,48,60},{2,14,18,30,34,46,50,62},{4,8,20,24,36,40,52,5..., dimensions={0} | all-to-all | bytes 1048576 | tf_op jit(solution)/shard_map/all_to_all | solution.py:258
  166.9 0.1 convert_reduce_fusion
  167.0 0.2 fusion.9
  167.2 0.1 broadcast_in_dim.46
  167.4 21.0 %all_to_all.32.arrived = bf16[32,3,32,128]{3,2,1,0:T(8,128)(2,1)S(1)} all-to-all(bf16[32,3,32,128]{3,2,1,0:T(8,128)(2,1)S(1)} %bitcast.32), channel_id=1, replica_groups=mesh['h'=2,'c'=2,'z'=8,'yh'=2,'yl'=2,'x'=2] {'h','c','yh','yl','x'}, dimensions={0} | all-to-all | bytes 1572864 | tf_op jit(solution)/shard_map/all_to_all | solution.py:39
  188.4 0.8 shard_map.108
  (29 shorter events, 0.1 us)
Async XLA Ops:
  8.6 14.4 %all-to-all-start = ((bf16[16,32,128]{2,1,0:T(8,128)(2,1)}), bf16[16,32,128]{2,1,0:T(8,128)(2,1)S(1)}, u32[]{:S(2)}, u32[]{:S(2)}) async-start(bf16[16,32,128]{2,1,0:T(8,128)(2,1)} %shard_map.104), calls=%async_computation | async-start | bytes 262144 | tf_op jit(solution)/shard_map/all_to_all | solution.py:39
  16.2 11.1 %copy-start = (f32[1,32,1024]{2,1,0:T(8,128)S(1)}, f32[1,32,1024]{2,1,0:T(8,128)}, u32[]{:S(2)}) copy-start(f32[1,32,1024]{2,1,0:T(8,128)} %first.3) | copy-start | bytes 393220
  16.2 11.1 %copy-start.1 = (f32[1,32,1024]{2,1,0:T(8,128)S(1)}, f32[1,32,1024]{2,1,0:T(8,128)}, u32[]{:S(2)}) copy-start(f32[1,32,1024]{2,1,0:T(8,128)} %second.3) | copy-start | bytes 393220
  16.2 11.1 %copy-start.4 = (s32[1,64]{1,0:T(1,128)S(1)}, s32[1,64]{1,0:T(1,128)}, u32[]{:S(2)}) copy-start(s32[1,64]{1,0:T(1,128)} %lengths.3) | copy-start | bytes 772
  23.0 25.3 %collective-permute-start.1 = (bf16[256,3072]{1,0:T(8,128)(2,1)}, bf16[256,3072]{1,0:T(8,128)(2,1)S(1)}, u32[]{:S(2)}, u32[]{:S(2)}) collective-permute-start(bf16[256,3072]{1,0:T(8,128)(2,1)} %shard_map.103), channel_id=1, source_target_pairs={{0,0},{1,64},{64,1},{65,65},{2,2},{3,66},{66,3},{67,67},{4,4},{5,6... | collective-permute-start | bytes 4718600 | tf_op jit(solution)/shard_map/ppermute | solution.py:51
  28.9 18.8 %collective-permute-start = (bf16[80,1024]{1,0:T(8,128)(2,1)S(1)}, bf16[80,1024]{1,0:T(8,128)(2,1)S(1)}, u32[]{:S(2)}, u32[]{:S(2)}) collective-permute-start(bf16[80,1024]{1,0:T(8,128)(2,1)S(1)} %shard_map.102), channel_id=1, source_target_pairs={{0,0},{1,64},{64,1},{65,65},{2,2},{3,66},{66,3},{67,67},{4,4},{5,6... | collective-permute-start | bytes 491528 | tf_op jit(solution)/shard_map/ppermute | solution.py:51
  31.8 25.6 %all-to-all-start.1 = ((bf16[8,256,128]{2,1,0:T(8,128)(2,1)}), bf16[8,256,128]{2,1,0:T(8,128)(2,1)S(1)}, u32[]{:S(2)}, u32[]{:S(2)}) async-start(bf16[8,256,128]{2,1,0:T(8,128)(2,1)} %broadcast_select_fusion), calls=%async_computation.1 | async-start | bytes 1048576 | tf_op jit(solution)/shard_map/all_to_all | solution.py:39
  39.9 60.0 %all-gather.2.cloned.1.call-start = ((), (), s32[]{:S(2)}) async-start(), calls=%async_computation.6 | async-start | bytes 1474560 | tf_op jit(solution)/shard_map/all_gather | solution.py:298
  47.7 0.7 copy-start.8
  50.0 26.1 %collective-permute-start.2 = (bf16[256,2304]{1,0:T(8,128)(2,1)}, bf16[256,2304]{1,0:T(8,128)(2,1)S(1)}, u32[]{:S(2)}, u32[]{:S(2)}) collective-permute-start(bf16[256,2304]{1,0:T(8,128)(2,1)} %get-tuple-element.19), channel_id=1, source_target_pairs={{0,2},{2,4},{4,6},{6,0},{1,3},{3,5},{5,7},{7,1},{8,10},{10,12},{12... | collective-permute-start | bytes 3538952 | tf_op jit(solution)/shard_map/ppermute | solution.py:31
  50.0 26.1 %collective-permute-start.4 = (bf16[256,2304]{1,0:T(8,128)(2,1)}, bf16[256,2304]{1,0:T(8,128)(2,1)}, u32[]{:S(2)}, u32[]{:S(2)}) collective-permute-start(bf16[256,2304]{1,0:T(8,128)(2,1)} %get-tuple-element.18), channel_id=1, source_target_pairs={{0,6},{2,0},{4,2},{6,4},{1,7},{3,1},{5,3},{7,5},{8,14},{10,8},{12,... | collective-permute-start | bytes 3538952 | tf_op jit(solution)/shard_map/ppermute | solution.py:31
  57.3 25.3 %collective-permute-start.6 = (bf16[256,3072]{1,0:T(8,128)(2,1)S(1)}, bf16[256,3072]{1,0:T(8,128)(2,1)}, u32[]{:S(2)}, u32[]{:S(2)}) collective-permute-start(bf16[256,3072]{1,0:T(8,128)(2,1)S(1)} %collective-permute-done.1.refs_0_), channel_id=1, source_target_pairs={{0,64},{64,0},{1,65},{65,1},{2,66},{66,2},{3,67},{67,3},{4,68},{68... | collective-permute-start | bytes 4718600 | tf_op jit(solution)/shard_map/ppermute | solution.py:31
  59.1 17.6 %collective-permute-start.7 = (bf16[128,2304]{1,0:T(8,128)(2,1)S(1)}, bf16[128,2304]{1,0:T(8,128)(2,1)}, u32[]{:S(2)}, u32[]{:S(2)}) collective-permute-start(bf16[128,2304]{1,0:T(8,128)(2,1)S(1)} %get-tuple-element.21), channel_id=1, source_target_pairs={{0,8},{8,16},{16,24},{24,32},{32,40},{40,48},{48,56},{56,0},{1,9},... | collective-permute-start | bytes 1769480 | tf_op jit(solution)/shard_map/ppermute | solution.py:31
  59.2 17.6 %collective-permute-start.8 = (bf16[128,2304]{1,0:T(8,128)(2,1)S(1)}, bf16[128,2304]{1,0:T(8,128)(2,1)}, u32[]{:S(2)}, u32[]{:S(2)}) collective-permute-start(bf16[128,2304]{1,0:T(8,128)(2,1)S(1)} %get-tuple-element.20), channel_id=1, source_target_pairs={{0,56},{8,0},{16,8},{24,16},{32,24},{40,32},{48,40},{56,48},{1,57}... | collective-permute-start | bytes 1769480 | tf_op jit(solution)/shard_map/ppermute | solution.py:31
  76.1 11.3 %collective-permute-start.3 = (bf16[256,2304]{1,0:T(8,128)(2,1)S(1)}, bf16[256,2304]{1,0:T(8,128)(2,1)}, u32[]{:S(2)}, u32[]{:S(2)}) collective-permute-start(bf16[256,2304]{1,0:T(8,128)(2,1)S(1)} %collective-permute-done.2.refs_0_.refs_6_), channel_id=1, source_target_pairs={{0,64},{64,0},{1,65},{65,1},{2,66},{66,2},{3,67},{67,3},{4,68},{68... | collective-permute-start | bytes 3538952 | tf_op jit(solution)/shard_map/ppermute | solution.py:31
  76.1 11.3 %collective-permute-start.5 = (bf16[256,2304]{1,0:T(8,128)(2,1)}, bf16[256,2304]{1,0:T(8,128)(2,1)}, u32[]{:S(2)}, u32[]{:S(2)}) collective-permute-start(bf16[256,2304]{1,0:T(8,128)(2,1)} %collective-permute-done.4.refs_2_.refs_8_), channel_id=1, source_target_pairs={{0,64},{64,0},{1,65},{65,1},{2,66},{66,2},{3,67},{67,3},{4,68},{68... | collective-permute-start | bytes 3538952 | tf_op jit(solution)/shard_map/ppermute | solution.py:31
  76.6 5.2 %collective-permute-start.9 = (bf16[128,2304]{1,0:T(8,128)(2,1)}, bf16[128,2304]{1,0:T(8,128)(2,1)}, u32[]{:S(2)}, u32[]{:S(2)}) collective-permute-start(bf16[128,2304]{1,0:T(8,128)(2,1)} %collective-permute-done.7.refs_2_), channel_id=1, source_target_pairs={{0,64},{64,0},{1,65},{65,1},{2,66},{66,2},{3,67},{67,3},{4,68},{68... | collective-permute-start | bytes 1769480 | tf_op jit(solution)/shard_map/ppermute | solution.py:31
  76.7 6.0 %collective-permute-start.10 = (bf16[128,2304]{1,0:T(8,128)(2,1)}, bf16[128,2304]{1,0:T(8,128)(2,1)}, u32[]{:S(2)}, u32[]{:S(2)}) collective-permute-start(bf16[128,2304]{1,0:T(8,128)(2,1)} %collective-permute-done.8.refs_3_), channel_id=1, source_target_pairs={{0,64},{64,0},{1,65},{65,1},{2,66},{66,2},{3,67},{67,3},{4,68},{68... | collective-permute-start | bytes 1769480 | tf_op jit(solution)/shard_map/ppermute | solution.py:31
  93.0 23.0 %all-to-all-start.2 = ((bf16[8,256,128]{2,1,0:T(8,128)(2,1)}), bf16[8,256,128]{2,1,0:T(8,128)(2,1)S(1)}, u32[]{:S(2)}, u32[]{:S(2)}) async-start(bf16[8,256,128]{2,1,0:T(8,128)(2,1)} %shard_map.106), calls=%async_computation.2 | async-start | bytes 1048576 | tf_op jit(solution)/shard_map/all_to_all | solution.py:258
  147.1 19.8 %copy-start.5 = (f32[256,128]{1,0:T(8,128)S(1)}, f32[256,128]{1,0:T(8,128)}, u32[]{:S(2)}) copy-start(f32[256,128]{1,0:T(8,128)} %get-tuple-element.11) | copy-start | bytes 393220
  147.1 19.8 %copy-start.6 = (f32[8,32,128]{2,1,0:T(8,128)S(1)}, f32[8,32,128]{2,1,0:T(8,128)}, u32[]{:S(2)}) copy-start(f32[8,32,128]{2,1,0:T(8,128)} %get-tuple-element.22) | copy-start | bytes 393220
  147.1 19.8 %copy-start.7 = (f32[8,32,128]{2,1,0:T(8,128)S(1)}, f32[8,32,128]{2,1,0:T(8,128)}, u32[]{:S(2)}) copy-start(f32[8,32,128]{2,1,0:T(8,128)} %get-tuple-element.23) | copy-start | bytes 393220
  167.2 21.2 %copy-start.2 = (f32[32,256]{1,0:T(8,128)S(1)}, f32[32,256]{1,0:T(8,128)}, u32[]{:S(2)}) copy-start(f32[32,256]{1,0:T(8,128)} %param.17) | copy-start | bytes 98308
  167.2 21.2 %copy-start.3 = (f32[32,256]{1,0:T(8,128)S(1)}, f32[32,256]{1,0:T(8,128)}, u32[]{:S(2)}) copy-start(f32[32,256]{1,0:T(8,128)} %mom.1) | copy-start | bytes 98308
Sparse Core Ops, SparseCore 0:
  48.5 27.5 all-gather.1

commit v8 on v7

--- a/solution.py
+++ b/solution.py
@@ -65,16 +65,17 @@
     return z, y, odd, lax.rem(y + 2 * odd, 4)
 
 
-def prepare_kernel(lengths, tokens, targets, out, inputs, goals, sems):
+def prepare_kernel(first, lengths, tokens, targets, out, inputs, goals, sems):
+    here = pl.ds(first, out.shape[0])
     copies = [
-        pltpu.make_async_copy(tokens.at[0], inputs, sems.at[0]),
-        pltpu.make_async_copy(targets.at[0], goals, sems.at[1]),
+        pltpu.make_async_copy(tokens.at[0, here], inputs, sems.at[0]),
+        pltpu.make_async_copy(targets.at[0, here], goals, sems.at[1]),
     ]
     for copy in copies:
         copy.start()
     z, y, _, colour = place()
     length = lengths[0, (z * 4 + y) * 2 + lax.axis_index("x")]
-    valid = lax.broadcasted_iota(jnp.int32, inputs.shape, 0) < length
+    valid = lax.broadcasted_iota(jnp.int32, inputs.shape, 0) + first < length
     copies[0].wait()
     out[:, WIDE : WIDE + D] = jnp.where(valid, inputs[...], jnp.zeros_like(inputs))
     copies[1].wait()
@@ -88,10 +89,10 @@
             ]
 
 
-def prepare(lengths, tokens, targets):
-    rows = tokens.shape[1]
-    return pl.pallas_call(
-        prepare_kernel,
+def prepare(first, lengths, tokens, targets):
+    rows = tokens.shape[1] // 2
+    return pl.pallas_call(
+        functools.partial(prepare_kernel, first),
         out_shape=jax.ShapeDtypeStruct((rows, D + 4 * WIDE), jnp.bfloat16),
         in_specs=[pl.BlockSpec(memory_space=pltpu.SMEM)]
         + [pl.BlockSpec(memory_space=pl.ANY)] * 2,
@@ -124,18 +125,23 @@
 
 
 def pack_moments_kernel(lengths, first, second, moments):
+    _, _, odd, _ = place()
     count = lax.fori_loop(0, lengths.shape[1], lambda i, t: t + lengths[0, i], 0)
     count = (count // 128).astype(jnp.float32)
-    moments[0:32] = first[0].astype(jnp.bfloat16)
-    moments[32:64] = second[0].astype(jnp.bfloat16)
-    moments[64:80] = jnp.full((16, 8 * BLOCK), count).astype(jnp.bfloat16)
+    for slot in range(16):
+        core, yh, yl = slot // 8, slot // 4 % 2, slot // 2 % 2
+        column = lax.rem(yh + odd, 2) * (2 * WIDE) + core * WIDE + yl * BLOCK
+        columns = pl.ds(pl.multiple_of(column, BLOCK), BLOCK)
+        moments[slot, 0:32] = first[0, :, columns].astype(jnp.bfloat16)
+        moments[slot, 32:64] = second[0, :, columns].astype(jnp.bfloat16)
+        moments[slot, 64:80] = jnp.full((16, BLOCK), count).astype(jnp.bfloat16)
 
 
 def pack_moments(lengths, first, second):
     whole = pl.BlockSpec(memory_space=pltpu.VMEM)
     return pl.pallas_call(
         pack_moments_kernel,
-        out_shape=jax.ShapeDtypeStruct((80, 8 * BLOCK), jnp.bfloat16),
+        out_shape=jax.ShapeDtypeStruct((16, 80, BLOCK), jnp.bfloat16),
         in_specs=[pl.BlockSpec(memory_space=pltpu.SMEM), whole, whole],
         out_specs=whole,
         compiler_params=pltpu.CompilerParams(vmem_limit_bytes=16 * 2**20),
@@ -272,16 +278,20 @@
     _, _, odd, colour = place()
     core = c.reshape(1).astype(jnp.int32)
 
+    half = tokens.shape[1] // 2
+    mine_a = turned(prepare(0, lengths, tokens, targets))
     start = exchange(pack(outer_param), ("h", "yh", "yl", "x"))
-    mine, start = together(prepare(lengths, tokens, targets), start)
-    mine = turned(mine)
-    theirs = other_core(mine)
-
-    below, above = up(mine[:, : D + WIDE]), down(mine[:, WIDE : D + 2 * WIDE])
-    half = mine.shape[0] // 2
-    plane = jnp.concatenate(
-        [mine[:, WIDE : WIDE + D], mine[:, D + 2 * WIDE : D + 3 * WIDE]], 1
-    )
+    mine_b, start = together(prepare(half, lengths, tokens, targets), start)
+    mine_b = turned(mine_b)
+
+    def both(*columns):
+        return jnp.concatenate([mine_a[:, slice(*columns)], mine_b[:, slice(*columns)]], 0)
+
+    below, above = up(both(0, D + WIDE)), down(both(WIDE, D + 2 * WIDE))
+
+    def plane_of(mine):
+        wanted = mine[:, D + 2 * WIDE : D + 3 * WIDE]
+        return jnp.concatenate([mine[:, WIDE : WIDE + D], wanted], 1)
 
     start = start.reshape(2, 256, BLOCK)
     here = pick(start, colour // 2, 0)
@@ -291,15 +301,17 @@
     )
     weights = exchange(weights, "z").reshape(D, BLOCK)
     start = here.astype(jnp.float32)
-    plane, weights = together(plane, weights)
-    before, behind = shift(plane[:half], "z", 1), shift(plane[half:], "z", -1)
-
-    moments, start = together(pack_moments(lengths, first_mom, second_mom), start)
-    moments = lax.all_gather(turned(moments), ("yh", "yl", "c"), axis=0, tiled=True)
-    column = colour // 2 * (2 * WIDE) + c * WIDE + colour % 2 * BLOCK
-    moments = lax.dynamic_slice_in_dim(moments, column, BLOCK, 1).reshape(8, 80, BLOCK)
-
-    near = [(block, WIDE, D + 3 * WIDE) for block in (mine, theirs)]
+    mine_a, mine_b, weights = together(mine_a, mine_b, weights)
+    before, behind = plane_of(mine_a), plane_of(mine_b)
+    before, behind = shift(before, "z", 1), shift(behind, "z", -1)
+
+    moments, weights = together(pack_moments(lengths, first_mom, second_mom), weights)
+    moments = exchange(moments, ("c", "yh", "yl", "x"))
+    moments = pick(moments.reshape(2, 8, 80, BLOCK), x, 0)
+    moments, before, behind = together(moments, before, behind)
+
+    near = [(block, WIDE, D + 3 * WIDE) for block in (mine_a, mine_b)]
+    near += [(other_core(block), WIDE, D + 3 * WIDE) for block in (mine_a, mine_b)]
     near += [
         (block, 0, D)
         for block in (before, behind, other_core(before), other_core(behind))

time: 197 us -> 186 us (0.944)
  blocking collectives: 61.6 us -> 43 us
  between operations: 15.1 us -> 1.71 us
  starting transfers between devices: 35.6 us -> 45.6 us
  waiting for transfers between devices: 47.5 us -> 53.8 us
  Pallas kernels: 25.8 us -> 29.8 us
  other arithmetic: 5.02 us -> 8.05 us
  local copies, waits for them, and re-layouts: 5.37 us -> 3.28 us
    all_to_all x2 -> x1, blocking collectives: 40.6 us -> 20.9 us  [among_peers(): return lax.all_to_all(x, axes, 0, 0, axis_index_groups=PEERS, tiled=True)]
    all_to_all x1 -> x2, waiting for transfers between devices: 13.2 us -> 27 us  [among_peers(): return lax.all_to_all(x, axes, 0, 0, axis_index_groups=PEERS, tiled=True)]
    ppermute x9 -> x10, waiting for transfers between devices: 19.8 us -> 8.75 us  [shift(): return lax.ppermute(x, axis, [(i, (i + by) % size) for i in range(size)])]
    all_to_all x2 -> x3, waiting for transfers between devices: 6.81 us -> 16.3 us  [exchange(): return lax.all_to_all(x, axes, 0, 0, tiled=True)]
    ppermute x2, waiting for transfers between devices: 7.66 us -> 1.84 us  [turned(): return lax.ppermute(x, ('c', 'x'), TURN)]
    all_to_all x1 -> x2, starting transfers between devices: 6.91 us -> 10.9 us  [among_peers(): return lax.all_to_all(x, axes, 0, 0, axis_index_groups=PEERS, tiled=True)]
    all_to_all x2 -> x3, starting transfers between devices: 15.8 us -> 19.3 us  [exchange(): return lax.all_to_all(x, axes, 0, 0, tiled=True)]
    pallas_call x2 -> x3, Pallas kernels: 4.37 us -> 7.23 us  [the longest x2 5.51 us: prepare(): pl.pallas_call(functools.partial(prepare_kernel, first), out_shape=jax.Sh...]
  transfers between devices with their start and end apart: 15 -> 17, of which waited for: 7 -> 10; matrix products, arithmetic and copies ran while one was open for 4% -> 5% of each run, Pallas kernels for 7% -> 6%
where the time goes in v8:
time: 186 us; the launch traced here: 185 us
  waiting for transfers between devices  53.8 us (29%)
  starting transfers between devices  45.6 us (25%)
  blocking collectives  43 us (23%)
  Pallas kernels  29.8 us (16%)
  other arithmetic  8.05 us (4%)
  local copies, waits for them, and re-layouts  3.28 us (2%)
    all_to_all x2, waiting for transfers between devices, among_peers(): return lax.all_to_all(x, axes, 0, 0, axis_index_groups=PEERS, tiled=True)  27 us
    all_to_all x1, blocking collectives, exchange(): return lax.all_to_all(x, axes, 0, 0, tiled=True)  22 us
    all_to_all x1, blocking collectives, among_peers(): return lax.all_to_all(x, axes, 0, 0, axis_index_groups=PEERS, tiled=True)  20.9 us
    pallas_call x3, Pallas kernels, product(): pl.pallas_call(functools.partial(product_kernel, layout, last), out_shape...  20.4 us
    all_to_all x3, starting transfers between devices, exchange(): return lax.all_to_all(x, axes, 0, 0, tiled=True)  19.3 us
    all_to_all x3, waiting for transfers between devices, exchange(): return lax.all_to_all(x, axes, 0, 0, tiled=True)  16.3 us
    all_to_all x2, starting transfers between devices, among_peers(): return lax.all_to_all(x, axes, 0, 0, axis_index_groups=PEERS, tiled=True)  10.9 us
    ppermute x10, waiting for transfers between devices, shift(): return lax.ppermute(x, axis, [(i, (i + by) % size) for i in range(size)])  8.75 us
  transfers between devices with their start and end apart: 17, of which 10 were waited for; matrix products, arithmetic and copies ran while one was open for 5% of the time, Pallas kernels for 6%

profile of v8, /device:TPU:1, one launch (start us, length us, event | category | flops | bytes accessed | tf_op | source)
XLA Modules:
  0.0 185.3 jit_solution(12568468496990903193)
XLA Ops:
  0.6 2.8 %shard_map.105 = bf16[128,3072]{1,0:T(8,128)(2,1)} custom-call(s32[1,64]{1,0:T(1,128)} %lengths.5, bf16[1,256,2048]{2,1,0:T(8,128)(2,1)} %tokens.3, bf16[1,256,1024]{2,1,0:T(8,128)(2,1)} %targets.3), custom_call_target="tpu_custom_call" | custom-call | tf_op jit(solution)/shard_map/pallas_call | solution.py:94
  3.4 4.5 %collective-permute-start = (bf16[128,3072]{1,0:T(8,128)(2,1)}, bf16[128,3072]{1,0:T(8,128)(2,1)S(1)}, u32[]{:S(2)}, u32[]{:S(2)}) collective-permute-start(bf16[128,3072]{1,0:T(8,128)(2,1)} %shard_map.105), channel_id=1, source_target_pairs={{0,0},{1,64},{64,1},{65,65},{2,2},{3,66},{66,3},{67,67},{4,4},{5,6... | collective-permute-start | bytes 2359304 | tf_op jit(solution)/shard_map/ppermute | solution.py:51
  7.9 1.4 shard_map.103
  9.3 6.5 %all-to-all-start = ((bf16[16,32,128]{2,1,0:T(8,128)(2,1)}), bf16[16,32,128]{2,1,0:T(8,128)(2,1)S(1)}, u32[]{:S(2)}, u32[]{:S(2)}) async-start(bf16[16,32,128]{2,1,0:T(8,128)(2,1)} %shard_map.103), calls=%async_computation | async-start | bytes 262144 | tf_op jit(solution)/shard_map/all_to_all | solution.py:39
  15.9 2.7 %shard_map.102 = bf16[128,3072]{1,0:T(8,128)(2,1)} custom-call(s32[1,64]{1,0:T(1,128)} %lengths.5, bf16[1,256,2048]{2,1,0:T(8,128)(2,1)} %tokens.3, bf16[1,256,1024]{2,1,0:T(8,128)(2,1)} %targets.3), custom_call_target="tpu_custom_call" | custom-call | tf_op jit(solution)/shard_map/pallas_call | solution.py:94
  18.6 5.2 %all-to-all-done = bf16[16,32,128]{2,1,0:T(8,128)(2,1)S(1)} async-done(((bf16[16,32,128]{2,1,0:T(8,128)(2,1)}), bf16[16,32,128]{2,1,0:T(8,128)(2,1)S(1)}, u32[]{:S(2)}, u32[]{:S(2)}) %all-to-all-start) | async-done | bytes 131104 | tf_op jit(solution)/shard_map/all_to_all | solution.py:39
  23.8 2.4 %collective-permute-start.1 = (bf16[128,3072]{1,0:T(8,128)(2,1)}, bf16[128,3072]{1,0:T(8,128)(2,1)S(1)}, u32[]{:S(2)}, u32[]{:S(2)}) collective-permute-start(bf16[128,3072]{1,0:T(8,128)(2,1)} %shard_map.102), channel_id=1, source_target_pairs={{0,0},{1,64},{64,1},{65,65},{2,2},{3,66},{66,3},{67,67},{4,4},{5,6... | collective-permute-start | bytes 2359304 | tf_op jit(solution)/shard_map/ppermute | solution.py:51
  26.3 0.9 broadcast_select_fusion
  27.2 8.2 %all-to-all-start.1 = ((bf16[8,256,128]{2,1,0:T(8,128)(2,1)}), bf16[8,256,128]{2,1,0:T(8,128)(2,1)S(1)}, u32[]{:S(2)}, u32[]{:S(2)}) async-start(bf16[8,256,128]{2,1,0:T(8,128)(2,1)} %broadcast_select_fusion), calls=%async_computation.1 | async-start | bytes 1048576 | tf_op jit(solution)/shard_map/all_to_all | solution.py:39
  35.4 0.1 fusion.14
  35.5 1.8 collective-permute-done.1.refs_1_
  37.3 0.1 fusion.15
  37.4 1.2 pad_maximum_fusion
  38.6 1.1 pad_maximum_fusion.1
  39.7 2.7 %collective-permute-start.6 = (bf16[256,2304]{1,0:T(8,128)(2,1)}, bf16[256,2304]{1,0:T(8,128)(2,1)}, u32[]{:S(2)}, u32[]{:S(2)}) collective-permute-start(bf16[256,2304]{1,0:T(8,128)(2,1)} %pad_maximum_fusion.1), channel_id=1, source_target_pairs={{0,6},{2,0},{4,2},{6,4},{1,7},{3,1},{5,3},{7,5},{8,14},{10,8},{12,... | collective-permute-start | bytes 3538952 | tf_op jit(solution)/shard_map/ppermute | solution.py:31
  42.3 11.1 %all-to-all-done.1 = bf16[8,256,128]{2,1,0:T(8,128)(2,1)S(1)} async-done(((bf16[8,256,128]{2,1,0:T(8,128)(2,1)}), bf16[8,256,128]{2,1,0:T(8,128)(2,1)S(1)}, u32[]{:S(2)}, u32[]{:S(2)}) %all-to-all-start.1) | async-done | bytes 524320 | tf_op jit(solution)/shard_map/all_to_all | solution.py:39
  53.6 0.5 collective-permute-start.8
  54.1 0.8 pad_maximum_fusion.2
  54.9 0.2 collective-permute-start.2
  55.2 0.9 pad_maximum_fusion.3
  56.0 2.5 %collective-permute-start.3 = (bf16[128,2304]{1,0:T(8,128)(2,1)}, bf16[128,2304]{1,0:T(8,128)(2,1)S(1)}, u32[]{:S(2)}, u32[]{:S(2)}) collective-permute-start(bf16[128,2304]{1,0:T(8,128)(2,1)} %pad_maximum_fusion.3), channel_id=1, source_target_pairs={{0,56},{8,0},{16,8},{24,16},{32,24},{40,32},{48,40},{56,48},{1,57}... | collective-permute-start | bytes 1769480 | tf_op jit(solution)/shard_map/ppermute | solution.py:31
  58.5 1.7 shard_map.104
  60.2 4.6 %all-to-all-start.2 = ((bf16[16,80,128]{2,1,0:T(8,128)(2,1)}), bf16[16,80,128]{2,1,0:T(8,128)(2,1)}, u32[]{:S(2)}, u32[]{:S(2)}) async-start(bf16[16,80,128]{2,1,0:T(8,128)(2,1)} %shard_map.104), calls=%async_computation.2 | async-start | bytes 655360 | tf_op jit(solution)/shard_map/all_to_all | solution.py:39
  64.8 1.7 collective-permute-done.4.refs_0_.refs_8_
  66.5 3.3 %collective-permute-done.6.refs_2_.refs_10_ = bf16[256,2304]{1,0:T(8,128)(2,1)} collective-permute-done((bf16[256,2304]{1,0:T(8,128)(2,1)}, bf16[256,2304]{1,0:T(8,128)(2,1)}, u32[]{:S(2)}, u32[]{:S(2)}) %collective-permute-start.6) | collective-permute-done | bytes 1179680 | tf_op jit(solution)/shard_map/ppermute | solution.py:31
  69.8 1.5 collective-permute-done.2.refs_4_
  71.2 0.9 collective-permute-start.9
  72.1 1.6 dynamic-slice_bitcast_fusion
  73.7 1.5 collective-permute-start.10
  75.2 0.3 collective-permute-start.11
  75.5 1.5 collective-permute-done.10.refs_6_
  77.0 0.8 collective-permute-done.11.refs_7_
  77.8 4.7 %shard_map.106.refs_4_ = f32[128,2048]{1,0:T(8,128)S(1)} custom-call(s32[1]{0:T(128)} %bitcast.7.core, bf16[2048,128]{1,0:T(8,128)(2,1)S(1)} %bitcast.64, bf16[128,3072]{1,0:T(8,128)(2,1)S(1)} %collective-permute-done.refs_0_, bf16[128,3072]{1,0:T(8,128)(2,1)S(1)} %copy-done.1, bf16[128,3072]{1,0:T(8,128)(2,1)} %collective-permute-done.8.refs_2_, ...), custom_call_target="tpu_custom_call" | custom-call | flops 2147483648 | bytes 4194304 | tf_op jit(solution)/shard_map/pallas_call | solution.py:244
  82.6 5.8 %shard_map.107 = bf16[8,256,128]{2,1,0:T(8,128)(2,1)} custom-call(s32[1]{0:T(128)} %bitcast.7.core, bf16[2048,128]{1,0:T(8,128)(2,1)S(1)} %bitcast.65, bf16[256,2304]{1,0:T(8,128)(2,1)} %collective-permute-done.4.refs_0_.refs_8_, bf16[256,2304]{1,0:T(8,128)(2,1)} %collective-permute-done.5.refs_1_.refs_9_, ...), custom_call_target="tpu_custom_call" | custom-call | flops 2147483648 | bytes 4194304 | tf_op jit(solution)/shard_map/pallas_call | solution.py:244
  88.4 5.9 %all-to-all-start.3 = ((bf16[8,256,128]{2,1,0:T(8,128)(2,1)}), bf16[8,256,128]{2,1,0:T(8,128)(2,1)S(1)}, u32[]{:S(2)}, u32[]{:S(2)}) async-start(bf16[8,256,128]{2,1,0:T(8,128)(2,1)} %shard_map.107), calls=%async_computation.3 | async-start | bytes 1048576 | tf_op jit(solution)/shard_map/all_to_all | solution.py:264
  94.4 1.2 slice.42
  96.3 1.6 convert_multiply_fusion.1
  97.8 12.6 %all-to-all-done.3 = bf16[8,256,128]{2,1,0:T(8,128)(2,1)S(1)} async-done(((bf16[8,256,128]{2,1,0:T(8,128)(2,1)}), bf16[8,256,128]{2,1,0:T(8,128)(2,1)S(1)}, u32[]{:S(2)}, u32[]{:S(2)}) %all-to-all-start.3) | async-done | bytes 524320 | tf_op jit(solution)/shard_map/all_to_all | solution.py:264
  110.6 1.2 convert_bitcast_fusion
  111.7 0.1 broadcast_in_dim.51
  111.8 20.9 %all_to_all.35 = bf16[8,256,128]{2,1,0:T(8,128)(2,1)S(1)} all-to-all(bf16[8,256,128]{2,1,0:T(8,128)(2,1)S(1)} %broadcast_in_dim.51), channel_id=1, replica_groups={{0,12,16,28,32,44,48,60},{2,14,18,30,34,46,50,62},{4,8,20,24,36,40,52,5..., dimensions={0} | all-to-all | bytes 1048576 | tf_op jit(solution)/shard_map/all_to_all | solution.py:264
  132.8 9.8 %shard_map.108 = bf16[8,256,128]{2,1,0:T(8,128)(2,1)} custom-call(s32[1]{0:T(128)} %bitcast.7.core, bf16[2048,128]{1,0:T(8,128)(2,1)S(1)} %bitcast.66, bf16[128,3072]{1,0:T(8,128)(2,1)S(1)} %collective-permute-done.refs_0_, bf16[128,3072]{1,0:T(8,128)(2,1)S(1)} %copy-done.1, bf16[128,3072]{1,0:T(8,128)(2,1)} %collective-permute-done.8.refs_2_, ...), custom_call_target="tpu_custom_call" | custom-call | flops 4294967296 | bytes 8388608 | tf_op jit(solution)/shard_map/pallas_call | solution.py:244
  142.6 5.0 %all-to-all-start.5 = ((bf16[8,256,128]{2,1,0:T(8,128)(2,1)}), bf16[8,256,128]{2,1,0:T(8,128)(2,1)S(1)}, u32[]{:S(2)}, u32[]{:S(2)}) async-start(bf16[8,256,128]{2,1,0:T(8,128)(2,1)} %shard_map.108), calls=%async_computation.5 | async-start | bytes 1048576 | tf_op jit(solution)/shard_map/all_to_all | solution.py:264
  147.6 14.3 %all-to-all-done.5 = bf16[8,256,128]{2,1,0:T(8,128)(2,1)S(1)} async-done(((bf16[8,256,128]{2,1,0:T(8,128)(2,1)}), bf16[8,256,128]{2,1,0:T(8,128)(2,1)S(1)}, u32[]{:S(2)}, u32[]{:S(2)}) %all-to-all-start.5) | async-done | bytes 524320 | tf_op jit(solution)/shard_map/all_to_all | solution.py:264
  162.0 0.2 fusion.2
  162.3 0.1 broadcast_in_dim.52
  162.4 22.0 %all_to_all.36.arrived = bf16[32,3,32,128]{3,2,1,0:T(8,128)(2,1)S(1)} all-to-all(bf16[32,3,32,128]{3,2,1,0:T(8,128)(2,1)S(1)} %bitcast.67), channel_id=1, replica_groups=mesh['h'=2,'c'=2,'z'=8,'yh'=2,'yl'=2,'x'=2] {'h','c','yh','yl','x'}, dimensions={0} | all-to-all | bytes 1572864 | tf_op jit(solution)/shard_map/all_to_all | solution.py:39
  184.5 0.8 shard_map.109
  (49 shorter events, 0.4 us)
Async XLA Ops:
  3.4 32.0 %collective-permute-start = (bf16[128,3072]{1,0:T(8,128)(2,1)}, bf16[128,3072]{1,0:T(8,128)(2,1)S(1)}, u32[]{:S(2)}, u32[]{:S(2)}) collective-permute-start(bf16[128,3072]{1,0:T(8,128)(2,1)} %shard_map.105), channel_id=1, source_target_pairs={{0,0},{1,64},{64,1},{65,65},{2,2},{3,66},{66,3},{67,67},{4,4},{5,6... | collective-permute-start | bytes 2359304 | tf_op jit(solution)/shard_map/ppermute | solution.py:51
  9.3 14.4 %all-to-all-start = ((bf16[16,32,128]{2,1,0:T(8,128)(2,1)}), bf16[16,32,128]{2,1,0:T(8,128)(2,1)S(1)}, u32[]{:S(2)}, u32[]{:S(2)}) async-start(bf16[16,32,128]{2,1,0:T(8,128)(2,1)} %shard_map.103), calls=%async_computation | async-start | bytes 262144 | tf_op jit(solution)/shard_map/all_to_all | solution.py:39
  23.8 11.6 %copy-start.11 = (bf16[16,32,128]{2,1,0:T(8,128)(2,1)}, bf16[16,32,128]{2,1,0:T(8,128)(2,1)S(1)}, u32[]{:S(2)}) copy-start(bf16[16,32,128]{2,1,0:T(8,128)(2,1)S(1)} %all-to-all-done) | copy-start | bytes 393220
  23.8 13.5 %collective-permute-start.1 = (bf16[128,3072]{1,0:T(8,128)(2,1)}, bf16[128,3072]{1,0:T(8,128)(2,1)S(1)}, u32[]{:S(2)}, u32[]{:S(2)}) collective-permute-start(bf16[128,3072]{1,0:T(8,128)(2,1)} %shard_map.102), channel_id=1, source_target_pairs={{0,0},{1,64},{64,1},{65,65},{2,2},{3,66},{66,3},{67,67},{4,4},{5,6... | collective-permute-start | bytes 2359304 | tf_op jit(solution)/shard_map/ppermute | solution.py:51
  27.2 26.3 %all-to-all-start.1 = ((bf16[8,256,128]{2,1,0:T(8,128)(2,1)}), bf16[8,256,128]{2,1,0:T(8,128)(2,1)S(1)}, u32[]{:S(2)}, u32[]{:S(2)}) async-start(bf16[8,256,128]{2,1,0:T(8,128)(2,1)} %broadcast_select_fusion), calls=%async_computation.1 | async-start | bytes 1048576 | tf_op jit(solution)/shard_map/all_to_all | solution.py:39
  37.3 16.2 %copy-start = (bf16[128,3072]{1,0:T(8,128)(2,1)}, bf16[128,3072]{1,0:T(8,128)(2,1)S(1)}, u32[]{:S(2)}) copy-start(bf16[128,3072]{1,0:T(8,128)(2,1)S(1)} %collective-permute-done.1.refs_1_) | copy-start | bytes 2359300
  38.6 27.9 %collective-permute-start.4 = (bf16[256,2304]{1,0:T(8,128)(2,1)}, bf16[256,2304]{1,0:T(8,128)(2,1)}, u32[]{:S(2)}, u32[]{:S(2)}) collective-permute-start(bf16[256,2304]{1,0:T(8,128)(2,1)} %pad_maximum_fusion), channel_id=1, source_target_pairs={{0,2},{2,4},{4,6},{6,0},{1,3},{3,5},{5,7},{7,1},{8,10},{10,12},{12... | collective-permute-start | bytes 3538952 | tf_op jit(solution)/shard_map/ppermute | solution.py:31
  39.7 30.1 %collective-permute-start.6 = (bf16[256,2304]{1,0:T(8,128)(2,1)}, bf16[256,2304]{1,0:T(8,128)(2,1)}, u32[]{:S(2)}, u32[]{:S(2)}) collective-permute-start(bf16[256,2304]{1,0:T(8,128)(2,1)} %pad_maximum_fusion.1), channel_id=1, source_target_pairs={{0,6},{2,0},{4,2},{6,4},{1,7},{3,1},{5,3},{7,5},{8,14},{10,8},{12,... | collective-permute-start | bytes 3538952 | tf_op jit(solution)/shard_map/ppermute | solution.py:31
  53.5 1.7 slice-start
  53.5 1.6 slice-start.1
  53.5 5.0 %copy-start.2 = (f32[1,32,1024]{2,1,0:T(8,128)S(1)}, f32[1,32,1024]{2,1,0:T(8,128)}, u32[]{:S(2)}) copy-start(f32[1,32,1024]{2,1,0:T(8,128)} %first.3) | copy-start | bytes 393220
  53.5 4.9 %copy-start.3 = (f32[1,32,1024]{2,1,0:T(8,128)S(1)}, f32[1,32,1024]{2,1,0:T(8,128)}, u32[]{:S(2)}) copy-start(f32[1,32,1024]{2,1,0:T(8,128)} %second.3) | copy-start | bytes 393220
  53.5 4.9 %copy-start.6 = (s32[1,64]{1,0:T(1,128)S(1)}, s32[1,64]{1,0:T(1,128)}, u32[]{:S(2)}) copy-start(s32[1,64]{1,0:T(1,128)} %lengths.5) | copy-start | bytes 772
  53.6 21.7 %collective-permute-start.8 = (bf16[128,3072]{1,0:T(8,128)(2,1)S(1)}, bf16[128,3072]{1,0:T(8,128)(2,1)}, u32[]{:S(2)}, u32[]{:S(2)}) collective-permute-start(bf16[128,3072]{1,0:T(8,128)(2,1)S(1)} %collective-permute-done.refs_0_), channel_id=1, source_target_pairs={{0,64},{64,0},{1,65},{65,1},{2,66},{66,2},{3,67},{67,3},{4,68},{68... | collective-permute-start | bytes 2359304 | tf_op jit(solution)/shard_map/ppermute | solution.py:31
  54.9 16.3 %copy-start.1 = (bf16[128,3072]{1,0:T(8,128)(2,1)S(1)}, bf16[128,3072]{1,0:T(8,128)(2,1)}, u32[]{:S(2)}) copy-start(bf16[128,3072]{1,0:T(8,128)(2,1)} %copy-done) | copy-start | bytes 2359300
  54.9 16.3 %collective-permute-start.2 = (bf16[128,2304]{1,0:T(8,128)(2,1)}, bf16[128,2304]{1,0:T(8,128)(2,1)S(1)}, u32[]{:S(2)}, u32[]{:S(2)}) collective-permute-start(bf16[128,2304]{1,0:T(8,128)(2,1)} %pad_maximum_fusion.2), channel_id=1, source_target_pairs={{0,8},{8,16},{16,24},{24,32},{32,40},{40,48},{48,56},{56,0},{1,9},... | collective-permute-start | bytes 1769480 | tf_op jit(solution)/shard_map/ppermute | solution.py:31
  56.0 17.7 %collective-permute-start.3 = (bf16[128,2304]{1,0:T(8,128)(2,1)}, bf16[128,2304]{1,0:T(8,128)(2,1)S(1)}, u32[]{:S(2)}, u32[]{:S(2)}) collective-permute-start(bf16[128,2304]{1,0:T(8,128)(2,1)} %pad_maximum_fusion.3), channel_id=1, source_target_pairs={{0,56},{8,0},{16,8},{24,16},{32,24},{40,32},{48,40},{56,48},{1,57}... | collective-permute-start | bytes 1769480 | tf_op jit(solution)/shard_map/ppermute | solution.py:31
  60.2 11.9 %all-to-all-start.2 = ((bf16[16,80,128]{2,1,0:T(8,128)(2,1)}), bf16[16,80,128]{2,1,0:T(8,128)(2,1)}, u32[]{:S(2)}, u32[]{:S(2)}) async-start(bf16[16,80,128]{2,1,0:T(8,128)(2,1)} %shard_map.104), calls=%async_computation.2 | async-start | bytes 655360 | tf_op jit(solution)/shard_map/all_to_all | solution.py:39
  66.5 16.1 %collective-permute-start.5 = (bf16[256,2304]{1,0:T(8,128)(2,1)}, bf16[256,2304]{1,0:T(8,128)(2,1)}, u32[]{:S(2)}, u32[]{:S(2)}) collective-permute-start(bf16[256,2304]{1,0:T(8,128)(2,1)} %collective-permute-done.4.refs_0_.refs_8_), channel_id=1, source_target_pairs={{0,64},{64,0},{1,65},{65,1},{2,66},{66,2},{3,67},{67,3},{4,68},{68... | collective-permute-start | bytes 3538952 | tf_op jit(solution)/shard_map/ppermute | solution.py:31
  69.8 12.8 %collective-permute-start.7 = (bf16[256,2304]{1,0:T(8,128)(2,1)}, bf16[256,2304]{1,0:T(8,128)(2,1)}, u32[]{:S(2)}, u32[]{:S(2)}) collective-permute-start(bf16[256,2304]{1,0:T(8,128)(2,1)} %collective-permute-done.6.refs_2_.refs_10_), channel_id=1, source_target_pairs={{0,64},{64,0},{1,65},{65,1},{2,66},{66,2},{3,67},{67,3},{4,68},{68... | collective-permute-start | bytes 3538952 | tf_op jit(solution)/shard_map/ppermute | solution.py:31
  71.2 4.3 %collective-permute-start.9 = (bf16[128,3072]{1,0:T(8,128)(2,1)S(1)}, bf16[128,3072]{1,0:T(8,128)(2,1)}, u32[]{:S(2)}, u32[]{:S(2)}) collective-permute-start(bf16[128,3072]{1,0:T(8,128)(2,1)S(1)} %copy-done.1), channel_id=1, source_target_pairs={{0,64},{64,0},{1,65},{65,1},{2,66},{66,2},{3,67},{67,3},{4,68},{68... | collective-permute-start | bytes 2359304 | tf_op jit(solution)/shard_map/ppermute | solution.py:31
  73.7 3.3 %collective-permute-start.10 = (bf16[128,2304]{1,0:T(8,128)(2,1)S(1)}, bf16[128,2304]{1,0:T(8,128)(2,1)}, u32[]{:S(2)}, u32[]{:S(2)}) collective-permute-start(bf16[128,2304]{1,0:T(8,128)(2,1)S(1)} %collective-permute-done.2.refs_4_), channel_id=1, source_target_pairs={{0,64},{64,0},{1,65},{65,1},{2,66},{66,2},{3,67},{67,3},{4,68},{68... | collective-permute-start | bytes 1769480 | tf_op jit(solution)/shard_map/ppermute | solution.py:31
  75.2 2.6 %collective-permute-start.11 = (bf16[128,2304]{1,0:T(8,128)(2,1)S(1)}, bf16[128,2304]{1,0:T(8,128)(2,1)}, u32[]{:S(2)}, u32[]{:S(2)}) collective-permute-start(bf16[128,2304]{1,0:T(8,128)(2,1)S(1)} %collective-permute-done.3.refs_5_), channel_id=1, source_target_pairs={{0,64},{64,0},{1,65},{65,1},{2,66},{66,2},{3,67},{67,3},{4,68},{68... | collective-permute-start | bytes 1769480 | tf_op jit(solution)/shard_map/ppermute | solution.py:31
  88.4 22.0 %all-to-all-start.3 = ((bf16[8,256,128]{2,1,0:T(8,128)(2,1)}), bf16[8,256,128]{2,1,0:T(8,128)(2,1)S(1)}, u32[]{:S(2)}, u32[]{:S(2)}) async-start(bf16[8,256,128]{2,1,0:T(8,128)(2,1)} %shard_map.107), calls=%async_computation.3 | async-start | bytes 1048576 | tf_op jit(solution)/shard_map/all_to_all | solution.py:264
  110.5 1.2 copy-start.7
  132.8 14.8 %copy-start.8 = (f32[256,128]{1,0:T(8,128)S(1)}, f32[256,128]{1,0:T(8,128)}, u32[]{:S(2)}) copy-start(f32[256,128]{1,0:T(8,128)} %copy-done.7) | copy-start | bytes 393220
  142.6 19.4 %copy-start.9 = (f32[8,32,128]{2,1,0:T(8,128)S(1)}, f32[8,32,128]{2,1,0:T(8,128)}, u32[]{:S(2)}) copy-start(f32[8,32,128]{2,1,0:T(8,128)} %get-tuple-element.28) | copy-start | bytes 393220
  142.6 19.4 %copy-start.10 = (f32[8,32,128]{2,1,0:T(8,128)S(1)}, f32[8,32,128]{2,1,0:T(8,128)}, u32[]{:S(2)}) copy-start(f32[8,32,128]{2,1,0:T(8,128)} %get-tuple-element.29) | copy-start | bytes 393220
  142.6 19.4 %copy-start.12 = (bf16[16,32,128]{2,1,0:T(8,128)(2,1)S(1)}, bf16[16,32,128]{2,1,0:T(8,128)(2,1)}, u32[]{:S(2)}) copy-start(bf16[16,32,128]{2,1,0:T(8,128)(2,1)} %copy-done.11) | copy-start | bytes 393220
  142.6 19.3 %all-to-all-start.5 = ((bf16[8,256,128]{2,1,0:T(8,128)(2,1)}), bf16[8,256,128]{2,1,0:T(8,128)(2,1)S(1)}, u32[]{:S(2)}, u32[]{:S(2)}) async-start(bf16[8,256,128]{2,1,0:T(8,128)(2,1)} %shard_map.108), calls=%async_computation.5 | async-start | bytes 1048576 | tf_op jit(solution)/shard_map/all_to_all | solution.py:264
  162.3 22.2 %copy-start.4 = (f32[32,256]{1,0:T(8,128)S(1)}, f32[32,256]{1,0:T(8,128)}, u32[]{:S(2)}) copy-start(f32[32,256]{1,0:T(8,128)} %param.17) | copy-start | bytes 98308
  162.3 22.2 %copy-start.5 = (f32[32,256]{1,0:T(8,128)S(1)}, f32[32,256]{1,0:T(8,128)}, u32[]{:S(2)}) copy-start(f32[32,256]{1,0:T(8,128)} %mom.1) | copy-start | bytes 98308

commit v9 on v8

--- a/solution.py
+++ b/solution.py
@@ -281,8 +281,7 @@
     half = tokens.shape[1] // 2
     mine_a = turned(prepare(0, lengths, tokens, targets))
     start = exchange(pack(outer_param), ("h", "yh", "yl", "x"))
-    mine_b, start = together(prepare(half, lengths, tokens, targets), start)
-    mine_b = turned(mine_b)
+    mine_b = turned(prepare(half, lengths, tokens, targets))
 
     def both(*columns):
         return jnp.concatenate([mine_a[:, slice(*columns)], mine_b[:, slice(*columns)]], 0)

time: 186 us -> 185 us (level)
  waiting for transfers between devices: 53.8 us -> 48.3 us
  starting transfers between devices: 45.6 us -> 49 us
    ppermute x10, starting transfers between devices: 8.54 us -> 11.5 us  [shift(): return lax.ppermute(x, axis, [(i, (i + by) % size) for i in range(size)])]
    ppermute x10, waiting for transfers between devices: 8.75 us -> 5.87 us  [shift(): return lax.ppermute(x, axis, [(i, (i + by) % size) for i in range(size)])]
  transfers between devices with their start and end apart: 17 -> 17, of which waited for: 10 -> 8; matrix products, arithmetic and copies ran while one was open for 5% -> 5% of each run, Pallas kernels for 6% -> 6%
where the time goes in v9:
time: 185 us; the launch traced here: 184 us
  starting transfers between devices  49 us (26%)
  waiting for transfers between devices  48.3 us (26%)
  blocking collectives  43.4 us (23%)
  Pallas kernels  29.8 us (16%)
  other arithmetic  8.03 us (4%)
  local copies, waits for them, and re-layouts  3.27 us (2%)
    all_to_all x2, waiting for transfers between devices, among_peers(): return lax.all_to_all(x, axes, 0, 0, axis_index_groups=PEERS, tiled=True)  27.3 us
    all_to_all x1, blocking collectives, among_peers(): return lax.all_to_all(x, axes, 0, 0, axis_index_groups=PEERS, tiled=True)  22 us
    all_to_all x1, blocking collectives, exchange(): return lax.all_to_all(x, axes, 0, 0, tiled=True)  21.4 us
    pallas_call x3, Pallas kernels, product(): pl.pallas_call(functools.partial(product_kernel, layout, last), out_shape...  20.4 us
    all_to_all x3, starting transfers between devices, exchange(): return lax.all_to_all(x, axes, 0, 0, tiled=True)  19.2 us
    all_to_all x3, waiting for transfers between devices, exchange(): return lax.all_to_all(x, axes, 0, 0, tiled=True)  15.1 us
    ppermute x10, starting transfers between devices, shift(): return lax.ppermute(x, axis, [(i, (i + by) % size) for i in range(size)])  11.5 us
    all_to_all x2, starting transfers between devices, among_peers(): return lax.all_to_all(x, axes, 0, 0, axis_index_groups=PEERS, tiled=True)  10.9 us
  transfers between devices with their start and end apart: 17, of which 8 were waited for; matrix products, arithmetic and copies ran while one was open for 5% of the time, Pallas kernels for 6%

profile of v9, /device:TPU:1, one launch (start us, length us, event | category | flops | bytes accessed | tf_op | source)
XLA Modules:
  0.0 183.5 jit_solution(15124080000466134867)
XLA Ops:
  0.6 2.8 %shard_map.104 = bf16[128,3072]{1,0:T(8,128)(2,1)} custom-call(s32[1,64]{1,0:T(1,128)} %lengths.5, bf16[1,256,2048]{2,1,0:T(8,128)(2,1)} %tokens.3, bf16[1,256,1024]{2,1,0:T(8,128)(2,1)} %targets.3), custom_call_target="tpu_custom_call" | custom-call | tf_op jit(solution)/shard_map/pallas_call | solution.py:94
  3.4 4.5 %collective-permute-start = (bf16[128,3072]{1,0:T(8,128)(2,1)}, bf16[128,3072]{1,0:T(8,128)(2,1)S(1)}, u32[]{:S(2)}, u32[]{:S(2)}) collective-permute-start(bf16[128,3072]{1,0:T(8,128)(2,1)} %shard_map.104), channel_id=1, source_target_pairs={{0,0},{1,64},{64,1},{65,65},{2,2},{3,66},{66,3},{67,67},{4,4},{5,6... | collective-permute-start | bytes 2359304 | tf_op jit(solution)/shard_map/ppermute | solution.py:51
  7.9 1.4 shard_map.102
  9.3 6.5 %all-to-all-start = ((bf16[16,32,128]{2,1,0:T(8,128)(2,1)}), bf16[16,32,128]{2,1,0:T(8,128)(2,1)S(1)}, u32[]{:S(2)}, u32[]{:S(2)}) async-start(bf16[16,32,128]{2,1,0:T(8,128)(2,1)} %shard_map.102), calls=%async_computation | async-start | bytes 262144 | tf_op jit(solution)/shard_map/all_to_all | solution.py:39
  15.8 2.7 %shard_map.105 = bf16[128,3072]{1,0:T(8,128)(2,1)} custom-call(s32[1,64]{1,0:T(1,128)} %lengths.5, bf16[1,256,2048]{2,1,0:T(8,128)(2,1)} %tokens.3, bf16[1,256,1024]{2,1,0:T(8,128)(2,1)} %targets.3), custom_call_target="tpu_custom_call" | custom-call | tf_op jit(solution)/shard_map/pallas_call | solution.py:94
  18.6 2.9 %collective-permute-start.1 = (bf16[128,3072]{1,0:T(8,128)(2,1)}, bf16[128,3072]{1,0:T(8,128)(2,1)S(1)}, u32[]{:S(2)}, u32[]{:S(2)}) collective-permute-start(bf16[128,3072]{1,0:T(8,128)(2,1)} %shard_map.105), channel_id=1, source_target_pairs={{0,0},{1,64},{64,1},{65,65},{2,2},{3,66},{66,3},{67,67},{4,4},{5,6... | collective-permute-start | bytes 2359304 | tf_op jit(solution)/shard_map/ppermute | solution.py:51
  21.5 2.2 %all-to-all-done = bf16[16,32,128]{2,1,0:T(8,128)(2,1)S(1)} async-done(((bf16[16,32,128]{2,1,0:T(8,128)(2,1)}), bf16[16,32,128]{2,1,0:T(8,128)(2,1)S(1)}, u32[]{:S(2)}, u32[]{:S(2)}) %all-to-all-start) | async-done | bytes 131104 | tf_op jit(solution)/shard_map/all_to_all | solution.py:39
  23.8 0.9 broadcast_select_fusion
  24.7 8.2 %all-to-all-start.1 = ((bf16[8,256,128]{2,1,0:T(8,128)(2,1)}), bf16[8,256,128]{2,1,0:T(8,128)(2,1)S(1)}, u32[]{:S(2)}, u32[]{:S(2)}) async-start(bf16[8,256,128]{2,1,0:T(8,128)(2,1)} %broadcast_select_fusion), calls=%async_computation.1 | async-start | bytes 1048576 | tf_op jit(solution)/shard_map/all_to_all | solution.py:39
  32.9 0.1 fusion.14
  33.0 0.1 fusion.15
  33.1 1.2 pad_maximum_fusion
  34.3 0.4 collective-permute-start.4
  34.7 1.1 pad_maximum_fusion.1
  35.8 2.3 %collective-permute-start.6 = (bf16[256,2304]{1,0:T(8,128)(2,1)}, bf16[256,2304]{1,0:T(8,128)(2,1)}, u32[]{:S(2)}, u32[]{:S(2)}) collective-permute-start(bf16[256,2304]{1,0:T(8,128)(2,1)} %pad_maximum_fusion.1), channel_id=1, source_target_pairs={{0,6},{2,0},{4,2},{6,4},{1,7},{3,1},{5,3},{7,5},{8,14},{10,8},{12,... | collective-permute-start | bytes 3538952 | tf_op jit(solution)/shard_map/ppermute | solution.py:31
  38.1 12.8 %all-to-all-done.1 = bf16[8,256,128]{2,1,0:T(8,128)(2,1)S(1)} async-done(((bf16[8,256,128]{2,1,0:T(8,128)(2,1)}), bf16[8,256,128]{2,1,0:T(8,128)(2,1)S(1)}, u32[]{:S(2)}, u32[]{:S(2)}) %all-to-all-start.1) | async-done | bytes 524320 | tf_op jit(solution)/shard_map/all_to_all | solution.py:39
  51.0 0.6 collective-permute-start.8
  51.6 0.8 pad_maximum_fusion.2
  52.4 0.3 collective-permute-start.2
  52.7 0.9 pad_maximum_fusion.3
  53.6 2.4 %collective-permute-start.3 = (bf16[128,2304]{1,0:T(8,128)(2,1)}, bf16[128,2304]{1,0:T(8,128)(2,1)S(1)}, u32[]{:S(2)}, u32[]{:S(2)}) collective-permute-start(bf16[128,2304]{1,0:T(8,128)(2,1)} %pad_maximum_fusion.3), channel_id=1, source_target_pairs={{0,56},{8,0},{16,8},{24,16},{32,24},{40,32},{48,40},{56,48},{1,57}... | collective-permute-start | bytes 1769480 | tf_op jit(solution)/shard_map/ppermute | solution.py:31
  56.0 1.7 shard_map.103
  57.7 4.6 %all-to-all-start.2 = ((bf16[16,80,128]{2,1,0:T(8,128)(2,1)}), bf16[16,80,128]{2,1,0:T(8,128)(2,1)}, u32[]{:S(2)}, u32[]{:S(2)}) async-start(bf16[16,80,128]{2,1,0:T(8,128)(2,1)} %shard_map.103), calls=%async_computation.2 | async-start | bytes 655360 | tf_op jit(solution)/shard_map/all_to_all | solution.py:39
  62.2 0.5 collective-permute-done.4.refs_0_.refs_8_
  62.8 1.4 collective-permute-start.5
  64.2 1.7 collective-permute-start.7
  65.9 3.0 %collective-permute-done.2.refs_4_ = bf16[128,2304]{1,0:T(8,128)(2,1)S(1)} collective-permute-done((bf16[128,2304]{1,0:T(8,128)(2,1)}, bf16[128,2304]{1,0:T(8,128)(2,1)S(1)}, u32[]{:S(2)}, u32[]{:S(2)}) %collective-permute-start.2) | collective-permute-done | bytes 589856 | tf_op jit(solution)/shard_map/ppermute | solution.py:31
  68.9 0.7 collective-permute-start.9
  69.6 1.6 dynamic-slice_bitcast_fusion
  71.2 1.5 collective-permute-start.10
  72.7 0.3 collective-permute-start.11
  72.9 1.5 collective-permute-done.10.refs_6_
  74.4 0.8 collective-permute-done.11.refs_7_
  75.3 4.7 %shard_map.106.refs_4_ = f32[128,2048]{1,0:T(8,128)S(1)} custom-call(s32[1]{0:T(128)} %bitcast.7.core, bf16[2048,128]{1,0:T(8,128)(2,1)S(1)} %bitcast.64, bf16[128,3072]{1,0:T(8,128)(2,1)S(1)} %collective-permute-done.refs_0_, bf16[128,3072]{1,0:T(8,128)(2,1)S(1)} %copy-done.1, bf16[128,3072]{1,0:T(8,128)(2,1)} %collective-permute-done.8.refs_2_, ...), custom_call_target="tpu_custom_call" | custom-call | flops 2147483648 | bytes 4194304 | tf_op jit(solution)/shard_map/pallas_call | solution.py:244
  80.0 5.8 %shard_map.107 = bf16[8,256,128]{2,1,0:T(8,128)(2,1)} custom-call(s32[1]{0:T(128)} %bitcast.7.core, bf16[2048,128]{1,0:T(8,128)(2,1)S(1)} %bitcast.65, bf16[256,2304]{1,0:T(8,128)(2,1)} %collective-permute-done.4.refs_0_.refs_8_, bf16[256,2304]{1,0:T(8,128)(2,1)} %collective-permute-done.5.refs_1_.refs_9_, ...), custom_call_target="tpu_custom_call" | custom-call | flops 2147483648 | bytes 4194304 | tf_op jit(solution)/shard_map/pallas_call | solution.py:244
  85.9 6.5 %all-to-all-start.3 = ((bf16[8,256,128]{2,1,0:T(8,128)(2,1)}), bf16[8,256,128]{2,1,0:T(8,128)(2,1)S(1)}, u32[]{:S(2)}, u32[]{:S(2)}) async-start(bf16[8,256,128]{2,1,0:T(8,128)(2,1)} %shard_map.107), calls=%async_computation.3 | async-start | bytes 1048576 | tf_op jit(solution)/shard_map/all_to_all | solution.py:264
  92.4 1.2 slice.42
  94.3 1.6 convert_multiply_fusion.1
  95.9 12.2 %all-to-all-done.3 = bf16[8,256,128]{2,1,0:T(8,128)(2,1)S(1)} async-done(((bf16[8,256,128]{2,1,0:T(8,128)(2,1)}), bf16[8,256,128]{2,1,0:T(8,128)(2,1)S(1)}, u32[]{:S(2)}, u32[]{:S(2)}) %all-to-all-start.3) | async-done | bytes 524320 | tf_op jit(solution)/shard_map/all_to_all | solution.py:264
  108.1 1.2 convert_bitcast_fusion
  109.3 22.0 %all_to_all.35 = bf16[8,256,128]{2,1,0:T(8,128)(2,1)S(1)} all-to-all(bf16[8,256,128]{2,1,0:T(8,128)(2,1)S(1)} %broadcast_in_dim.51), channel_id=1, replica_groups={{0,12,16,28,32,44,48,60},{2,14,18,30,34,46,50,62},{4,8,20,24,36,40,52,5..., dimensions={0} | all-to-all | bytes 1048576 | tf_op jit(solution)/shard_map/all_to_all | solution.py:264
  131.3 9.8 %shard_map.108 = bf16[8,256,128]{2,1,0:T(8,128)(2,1)} custom-call(s32[1]{0:T(128)} %bitcast.7.core, bf16[2048,128]{1,0:T(8,128)(2,1)S(1)} %bitcast.66, bf16[128,3072]{1,0:T(8,128)(2,1)S(1)} %collective-permute-done.refs_0_, bf16[128,3072]{1,0:T(8,128)(2,1)S(1)} %copy-done.1, bf16[128,3072]{1,0:T(8,128)(2,1)} %collective-permute-done.8.refs_2_, ...), custom_call_target="tpu_custom_call" | custom-call | flops 4294967296 | bytes 8388608 | tf_op jit(solution)/shard_map/pallas_call | solution.py:244
  141.2 4.4 %all-to-all-start.5 = ((bf16[8,256,128]{2,1,0:T(8,128)(2,1)}), bf16[8,256,128]{2,1,0:T(8,128)(2,1)S(1)}, u32[]{:S(2)}, u32[]{:S(2)}) async-start(bf16[8,256,128]{2,1,0:T(8,128)(2,1)} %shard_map.108), calls=%async_computation.5 | async-start | bytes 1048576 | tf_op jit(solution)/shard_map/all_to_all | solution.py:264
  145.6 15.2 %all-to-all-done.5 = bf16[8,256,128]{2,1,0:T(8,128)(2,1)S(1)} async-done(((bf16[8,256,128]{2,1,0:T(8,128)(2,1)}), bf16[8,256,128]{2,1,0:T(8,128)(2,1)S(1)}, u32[]{:S(2)}, u32[]{:S(2)}) %all-to-all-start.5) | async-done | bytes 524320 | tf_op jit(solution)/shard_map/all_to_all | solution.py:264
  160.9 0.2 fusion.2
  161.2 0.1 broadcast_in_dim.52
  161.3 21.4 %all_to_all.36.arrived = bf16[32,3,32,128]{3,2,1,0:T(8,128)(2,1)S(1)} all-to-all(bf16[32,3,32,128]{3,2,1,0:T(8,128)(2,1)S(1)} %bitcast.67), channel_id=1, replica_groups=mesh['h'=2,'c'=2,'z'=8,'yh'=2,'yl'=2,'x'=2] {'h','c','yh','yl','x'}, dimensions={0} | all-to-all | bytes 1572864 | tf_op jit(solution)/shard_map/all_to_all | solution.py:39
  182.7 0.8 shard_map.109
  (49 shorter events, 0.4 us)
Async XLA Ops:
  3.4 29.5 %collective-permute-start = (bf16[128,3072]{1,0:T(8,128)(2,1)}, bf16[128,3072]{1,0:T(8,128)(2,1)S(1)}, u32[]{:S(2)}, u32[]{:S(2)}) collective-permute-start(bf16[128,3072]{1,0:T(8,128)(2,1)} %shard_map.104), channel_id=1, source_target_pairs={{0,0},{1,64},{64,1},{65,65},{2,2},{3,66},{66,3},{67,67},{4,4},{5,6... | collective-permute-start | bytes 2359304 | tf_op jit(solution)/shard_map/ppermute | solution.py:51
  9.3 14.4 %all-to-all-start = ((bf16[16,32,128]{2,1,0:T(8,128)(2,1)}), bf16[16,32,128]{2,1,0:T(8,128)(2,1)S(1)}, u32[]{:S(2)}, u32[]{:S(2)}) async-start(bf16[16,32,128]{2,1,0:T(8,128)(2,1)} %shard_map.102), calls=%async_computation | async-start | bytes 262144 | tf_op jit(solution)/shard_map/all_to_all | solution.py:39
  18.6 14.4 %collective-permute-start.1 = (bf16[128,3072]{1,0:T(8,128)(2,1)}, bf16[128,3072]{1,0:T(8,128)(2,1)S(1)}, u32[]{:S(2)}, u32[]{:S(2)}) collective-permute-start(bf16[128,3072]{1,0:T(8,128)(2,1)} %shard_map.105), channel_id=1, source_target_pairs={{0,0},{1,64},{64,1},{65,65},{2,2},{3,66},{66,3},{67,67},{4,4},{5,6... | collective-permute-start | bytes 2359304 | tf_op jit(solution)/shard_map/ppermute | solution.py:51
  23.8 9.1 %copy-start.11 = (bf16[16,32,128]{2,1,0:T(8,128)(2,1)}, bf16[16,32,128]{2,1,0:T(8,128)(2,1)S(1)}, u32[]{:S(2)}) copy-start(bf16[16,32,128]{2,1,0:T(8,128)(2,1)S(1)} %all-to-all-done) | copy-start | bytes 393220
  24.7 26.1 %all-to-all-start.1 = ((bf16[8,256,128]{2,1,0:T(8,128)(2,1)}), bf16[8,256,128]{2,1,0:T(8,128)(2,1)S(1)}, u32[]{:S(2)}, u32[]{:S(2)}) async-start(bf16[8,256,128]{2,1,0:T(8,128)(2,1)} %broadcast_select_fusion), calls=%async_computation.1 | async-start | bytes 1048576 | tf_op jit(solution)/shard_map/all_to_all | solution.py:39
  33.0 17.9 %copy-start = (bf16[128,3072]{1,0:T(8,128)(2,1)}, bf16[128,3072]{1,0:T(8,128)(2,1)S(1)}, u32[]{:S(2)}) copy-start(bf16[128,3072]{1,0:T(8,128)(2,1)S(1)} %collective-permute-done.1.refs_1_) | copy-start | bytes 2359300
  34.3 28.5 %collective-permute-start.4 = (bf16[256,2304]{1,0:T(8,128)(2,1)}, bf16[256,2304]{1,0:T(8,128)(2,1)}, u32[]{:S(2)}, u32[]{:S(2)}) collective-permute-start(bf16[256,2304]{1,0:T(8,128)(2,1)} %pad_maximum_fusion), channel_id=1, source_target_pairs={{0,2},{2,4},{4,6},{6,0},{1,3},{3,5},{5,7},{7,1},{8,10},{10,12},{12... | collective-permute-start | bytes 3538952 | tf_op jit(solution)/shard_map/ppermute | solution.py:31
  35.8 28.4 %collective-permute-start.6 = (bf16[256,2304]{1,0:T(8,128)(2,1)}, bf16[256,2304]{1,0:T(8,128)(2,1)}, u32[]{:S(2)}, u32[]{:S(2)}) collective-permute-start(bf16[256,2304]{1,0:T(8,128)(2,1)} %pad_maximum_fusion.1), channel_id=1, source_target_pairs={{0,6},{2,0},{4,2},{6,4},{1,7},{3,1},{5,3},{7,5},{8,14},{10,8},{12,... | collective-permute-start | bytes 3538952 | tf_op jit(solution)/shard_map/ppermute | solution.py:31
  50.9 1.8 slice-start
  50.9 1.8 slice-start.1
  51.0 5.0 %copy-start.2 = (f32[1,32,1024]{2,1,0:T(8,128)S(1)}, f32[1,32,1024]{2,1,0:T(8,128)}, u32[]{:S(2)}) copy-start(f32[1,32,1024]{2,1,0:T(8,128)} %first.3) | copy-start | bytes 393220
  51.0 5.0 %copy-start.3 = (f32[1,32,1024]{2,1,0:T(8,128)S(1)}, f32[1,32,1024]{2,1,0:T(8,128)}, u32[]{:S(2)}) copy-start(f32[1,32,1024]{2,1,0:T(8,128)} %second.3) | copy-start | bytes 393220
  51.0 5.0 %copy-start.6 = (s32[1,64]{1,0:T(1,128)S(1)}, s32[1,64]{1,0:T(1,128)}, u32[]{:S(2)}) copy-start(s32[1,64]{1,0:T(1,128)} %lengths.5) | copy-start | bytes 772
  51.0 21.7 %collective-permute-start.8 = (bf16[128,3072]{1,0:T(8,128)(2,1)S(1)}, bf16[128,3072]{1,0:T(8,128)(2,1)}, u32[]{:S(2)}, u32[]{:S(2)}) collective-permute-start(bf16[128,3072]{1,0:T(8,128)(2,1)S(1)} %collective-permute-done.refs_0_), channel_id=1, source_target_pairs={{0,64},{64,0},{1,65},{65,1},{2,66},{66,2},{3,67},{67,3},{4,68},{68... | collective-permute-start | bytes 2359304 | tf_op jit(solution)/shard_map/ppermute | solution.py:31
  52.4 16.5 %copy-start.1 = (bf16[128,3072]{1,0:T(8,128)(2,1)S(1)}, bf16[128,3072]{1,0:T(8,128)(2,1)}, u32[]{:S(2)}) copy-start(bf16[128,3072]{1,0:T(8,128)(2,1)} %copy-done) | copy-start | bytes 2359300
  52.4 16.5 %collective-permute-start.2 = (bf16[128,2304]{1,0:T(8,128)(2,1)}, bf16[128,2304]{1,0:T(8,128)(2,1)S(1)}, u32[]{:S(2)}, u32[]{:S(2)}) collective-permute-start(bf16[128,2304]{1,0:T(8,128)(2,1)} %pad_maximum_fusion.2), channel_id=1, source_target_pairs={{0,8},{8,16},{16,24},{24,32},{32,40},{40,48},{48,56},{56,0},{1,9},... | collective-permute-start | bytes 1769480 | tf_op jit(solution)/shard_map/ppermute | solution.py:31
  53.6 17.6 %collective-permute-start.3 = (bf16[128,2304]{1,0:T(8,128)(2,1)}, bf16[128,2304]{1,0:T(8,128)(2,1)S(1)}, u32[]{:S(2)}, u32[]{:S(2)}) collective-permute-start(bf16[128,2304]{1,0:T(8,128)(2,1)} %pad_maximum_fusion.3), channel_id=1, source_target_pairs={{0,56},{8,0},{16,8},{24,16},{32,24},{40,32},{48,40},{56,48},{1,57}... | collective-permute-start | bytes 1769480 | tf_op jit(solution)/shard_map/ppermute | solution.py:31
  57.7 11.9 %all-to-all-start.2 = ((bf16[16,80,128]{2,1,0:T(8,128)(2,1)}), bf16[16,80,128]{2,1,0:T(8,128)(2,1)}, u32[]{:S(2)}, u32[]{:S(2)}) async-start(bf16[16,80,128]{2,1,0:T(8,128)(2,1)} %shard_map.103), calls=%async_computation.2 | async-start | bytes 655360 | tf_op jit(solution)/shard_map/all_to_all | solution.py:39
  62.8 17.2 %collective-permute-start.5 = (bf16[256,2304]{1,0:T(8,128)(2,1)}, bf16[256,2304]{1,0:T(8,128)(2,1)}, u32[]{:S(2)}, u32[]{:S(2)}) collective-permute-start(bf16[256,2304]{1,0:T(8,128)(2,1)} %collective-permute-done.4.refs_0_.refs_8_), channel_id=1, source_target_pairs={{0,64},{64,0},{1,65},{65,1},{2,66},{66,2},{3,67},{67,3},{4,68},{68... | collective-permute-start | bytes 3538952 | tf_op jit(solution)/shard_map/ppermute | solution.py:31
  64.2 15.8 %collective-permute-start.7 = (bf16[256,2304]{1,0:T(8,128)(2,1)}, bf16[256,2304]{1,0:T(8,128)(2,1)}, u32[]{:S(2)}, u32[]{:S(2)}) collective-permute-start(bf16[256,2304]{1,0:T(8,128)(2,1)} %collective-permute-done.6.refs_2_.refs_10_), channel_id=1, source_target_pairs={{0,64},{64,0},{1,65},{65,1},{2,66},{66,2},{3,67},{67,3},{4,68},{68... | collective-permute-start | bytes 3538952 | tf_op jit(solution)/shard_map/ppermute | solution.py:31
  68.9 4.0 %collective-permute-start.9 = (bf16[128,3072]{1,0:T(8,128)(2,1)S(1)}, bf16[128,3072]{1,0:T(8,128)(2,1)}, u32[]{:S(2)}, u32[]{:S(2)}) collective-permute-start(bf16[128,3072]{1,0:T(8,128)(2,1)S(1)} %copy-done.1), channel_id=1, source_target_pairs={{0,64},{64,0},{1,65},{65,1},{2,66},{66,2},{3,67},{67,3},{4,68},{68... | collective-permute-start | bytes 2359304 | tf_op jit(solution)/shard_map/ppermute | solution.py:31
  71.2 3.2 %collective-permute-start.10 = (bf16[128,2304]{1,0:T(8,128)(2,1)S(1)}, bf16[128,2304]{1,0:T(8,128)(2,1)}, u32[]{:S(2)}, u32[]{:S(2)}) collective-permute-start(bf16[128,2304]{1,0:T(8,128)(2,1)S(1)} %collective-permute-done.2.refs_4_), channel_id=1, source_target_pairs={{0,64},{64,0},{1,65},{65,1},{2,66},{66,2},{3,67},{67,3},{4,68},{68... | collective-permute-start | bytes 1769480 | tf_op jit(solution)/shard_map/ppermute | solution.py:31
  72.7 2.6 %collective-permute-start.11 = (bf16[128,2304]{1,0:T(8,128)(2,1)S(1)}, bf16[128,2304]{1,0:T(8,128)(2,1)}, u32[]{:S(2)}, u32[]{:S(2)}) collective-permute-start(bf16[128,2304]{1,0:T(8,128)(2,1)S(1)} %collective-permute-done.3.refs_5_), channel_id=1, source_target_pairs={{0,64},{64,0},{1,65},{65,1},{2,66},{66,2},{3,67},{67,3},{4,68},{68... | collective-permute-start | bytes 1769480 | tf_op jit(solution)/shard_map/ppermute | solution.py:31
  85.9 22.1 %all-to-all-start.3 = ((bf16[8,256,128]{2,1,0:T(8,128)(2,1)}), bf16[8,256,128]{2,1,0:T(8,128)(2,1)S(1)}, u32[]{:S(2)}, u32[]{:S(2)}) async-start(bf16[8,256,128]{2,1,0:T(8,128)(2,1)} %shard_map.107), calls=%async_computation.3 | async-start | bytes 1048576 | tf_op jit(solution)/shard_map/all_to_all | solution.py:264
  108.1 1.2 copy-start.7
  131.3 14.2 %copy-start.8 = (f32[256,128]{1,0:T(8,128)S(1)}, f32[256,128]{1,0:T(8,128)}, u32[]{:S(2)}) copy-start(f32[256,128]{1,0:T(8,128)} %copy-done.7) | copy-start | bytes 393220
  141.2 19.7 %copy-start.9 = (f32[8,32,128]{2,1,0:T(8,128)S(1)}, f32[8,32,128]{2,1,0:T(8,128)}, u32[]{:S(2)}) copy-start(f32[8,32,128]{2,1,0:T(8,128)} %get-tuple-element.24) | copy-start | bytes 393220
  141.2 19.7 %copy-start.10 = (f32[8,32,128]{2,1,0:T(8,128)S(1)}, f32[8,32,128]{2,1,0:T(8,128)}, u32[]{:S(2)}) copy-start(f32[8,32,128]{2,1,0:T(8,128)} %get-tuple-element.25) | copy-start | bytes 393220
  141.2 19.7 %copy-start.12 = (bf16[16,32,128]{2,1,0:T(8,128)(2,1)S(1)}, bf16[16,32,128]{2,1,0:T(8,128)(2,1)}, u32[]{:S(2)}) copy-start(bf16[16,32,128]{2,1,0:T(8,128)(2,1)} %copy-done.11) | copy-start | bytes 393220
  141.2 19.6 %all-to-all-start.5 = ((bf16[8,256,128]{2,1,0:T(8,128)(2,1)}), bf16[8,256,128]{2,1,0:T(8,128)(2,1)S(1)}, u32[]{:S(2)}, u32[]{:S(2)}) async-start(bf16[8,256,128]{2,1,0:T(8,128)(2,1)} %shard_map.108), calls=%async_computation.5 | async-start | bytes 1048576 | tf_op jit(solution)/shard_map/all_to_all | solution.py:264
  161.1 21.6 %copy-start.4 = (f32[32,256]{1,0:T(8,128)S(1)}, f32[32,256]{1,0:T(8,128)}, u32[]{:S(2)}) copy-start(f32[32,256]{1,0:T(8,128)} %param.17) | copy-start | bytes 98308
  161.2 21.6 %copy-start.5 = (f32[32,256]{1,0:T(8,128)S(1)}, f32[32,256]{1,0:T(8,128)}, u32[]{:S(2)}) copy-start(f32[32,256]{1,0:T(8,128)} %mom.1) | copy-start | bytes 98308

commit v10 on v9

--- a/solution.py
+++ b/solution.py
@@ -306,8 +306,8 @@
 
     moments, weights = together(pack_moments(lengths, first_mom, second_mom), weights)
     moments = exchange(moments, ("c", "yh", "yl", "x"))
+    moments, above = together(moments, above)
     moments = pick(moments.reshape(2, 8, 80, BLOCK), x, 0)
-    moments, before, behind = together(moments, before, behind)
 
     near = [(block, WIDE, D + 3 * WIDE) for block in (mine_a, mine_b)]
     near += [(other_core(block), WIDE, D + 3 * WIDE) for block in (mine_a, mine_b)]

time: 185 us -> 188 us (1.016)
  waiting for transfers between devices: 48.3 us -> 57.3 us
  starting transfers between devices: 49 us -> 40.7 us
    all_to_all x3, waiting for transfers between devices: 15.1 us -> 21.6 us  [exchange(): return lax.all_to_all(x, axes, 0, 0, tiled=True)]
    ppermute x10, starting transfers between devices: 11.5 us -> 6.08 us  [shift(): return lax.ppermute(x, axis, [(i, (i + by) % size) for i in range(size)])]
    ppermute x10, waiting for transfers between devices: 5.87 us -> 8.95 us  [shift(): return lax.ppermute(x, axis, [(i, (i + by) % size) for i in range(size)])]
    all_to_all x2, starting transfers between devices: 10.9 us -> 8.43 us  [among_peers(): return lax.all_to_all(x, axes, 0, 0, axis_index_groups=PEERS, tiled=True)]
  transfers between devices with their start and end apart: 17 -> 17, of which waited for: 8 -> 9; matrix products, arithmetic and copies ran while one was open for 5% -> 6% of each run, Pallas kernels for 6% -> 6%
where the time goes in v10:
time: 188 us; the launch traced here: 187 us
  waiting for transfers between devices  57.3 us (30%)
  blocking collectives  44.1 us (23%)
  starting transfers between devices  40.7 us (22%)
  Pallas kernels  29.8 us (16%)
  other arithmetic  8.27 us (4%)
  local copies, waits for them, and re-layouts  4.84 us (3%)
    all_to_all x2, waiting for transfers between devices, among_peers(): return lax.all_to_all(x, axes, 0, 0, axis_index_groups=PEERS, tiled=True)  26.8 us
    all_to_all x1, blocking collectives, among_peers(): return lax.all_to_all(x, axes, 0, 0, axis_index_groups=PEERS, tiled=True)  22.1 us
    all_to_all x1, blocking collectives, exchange(): return lax.all_to_all(x, axes, 0, 0, tiled=True)  21.9 us
    all_to_all x3, waiting for transfers between devices, exchange(): return lax.all_to_all(x, axes, 0, 0, tiled=True)  21.6 us
    pallas_call x3, Pallas kernels, product(): pl.pallas_call(functools.partial(product_kernel, layout, last), out_shape...  20.4 us
    all_to_all x3, starting transfers between devices, exchange(): return lax.all_to_all(x, axes, 0, 0, tiled=True)  18.7 us
    ppermute x10, waiting for transfers between devices, shift(): return lax.ppermute(x, axis, [(i, (i + by) % size) for i in range(size)])  8.95 us
    all_to_all x2, starting transfers between devices, among_peers(): return lax.all_to_all(x, axes, 0, 0, axis_index_groups=PEERS, tiled=True)  8.43 us
  transfers between devices with their start and end apart: 17, of which 9 were waited for; matrix products, arithmetic and copies ran while one was open for 6% of the time, Pallas kernels for 6%

profile of v10, /device:TPU:1, one launch (start us, length us, event | category | flops | bytes accessed | tf_op | source)
XLA Modules:
  0.0 186.7 jit_solution(11360989201386082618)
XLA Ops:
  0.6 2.8 %shard_map.105 = bf16[128,3072]{1,0:T(8,128)(2,1)} custom-call(s32[1,64]{1,0:T(1,128)} %lengths.5, bf16[1,256,2048]{2,1,0:T(8,128)(2,1)} %tokens.3, bf16[1,256,1024]{2,1,0:T(8,128)(2,1)} %targets.3), custom_call_target="tpu_custom_call" | custom-call | tf_op jit(solution)/shard_map/pallas_call | solution.py:94
  3.4 4.5 %collective-permute-start.1 = (bf16[128,3072]{1,0:T(8,128)(2,1)}, bf16[128,3072]{1,0:T(8,128)(2,1)S(1)}, u32[]{:S(2)}, u32[]{:S(2)}) collective-permute-start(bf16[128,3072]{1,0:T(8,128)(2,1)} %shard_map.105), channel_id=1, source_target_pairs={{0,0},{1,64},{64,1},{65,65},{2,2},{3,66},{66,3},{67,67},{4,4},{5,6... | collective-permute-start | bytes 2359304 | tf_op jit(solution)/shard_map/ppermute | solution.py:51
  7.9 1.4 shard_map.102
  9.3 6.5 %all-to-all-start = ((bf16[16,32,128]{2,1,0:T(8,128)(2,1)}), bf16[16,32,128]{2,1,0:T(8,128)(2,1)S(1)}, u32[]{:S(2)}, u32[]{:S(2)}) async-start(bf16[16,32,128]{2,1,0:T(8,128)(2,1)} %shard_map.102), calls=%async_computation | async-start | bytes 262144 | tf_op jit(solution)/shard_map/all_to_all | solution.py:39
  15.8 2.8 %shard_map.104 = bf16[128,3072]{1,0:T(8,128)(2,1)} custom-call(s32[1,64]{1,0:T(1,128)} %lengths.5, bf16[1,256,2048]{2,1,0:T(8,128)(2,1)} %tokens.3, bf16[1,256,1024]{2,1,0:T(8,128)(2,1)} %targets.3), custom_call_target="tpu_custom_call" | custom-call | tf_op jit(solution)/shard_map/pallas_call | solution.py:94
  18.6 2.9 %collective-permute-start = (bf16[128,3072]{1,0:T(8,128)(2,1)}, bf16[128,3072]{1,0:T(8,128)(2,1)S(1)}, u32[]{:S(2)}, u32[]{:S(2)}) collective-permute-start(bf16[128,3072]{1,0:T(8,128)(2,1)} %shard_map.104), channel_id=1, source_target_pairs={{0,0},{1,64},{64,1},{65,65},{2,2},{3,66},{66,3},{67,67},{4,4},{5,6... | collective-permute-start | bytes 2359304 | tf_op jit(solution)/shard_map/ppermute | solution.py:51
  21.6 2.2 %all-to-all-done = bf16[16,32,128]{2,1,0:T(8,128)(2,1)S(1)} async-done(((bf16[16,32,128]{2,1,0:T(8,128)(2,1)}), bf16[16,32,128]{2,1,0:T(8,128)(2,1)S(1)}, u32[]{:S(2)}, u32[]{:S(2)}) %all-to-all-start) | async-done | bytes 131104 | tf_op jit(solution)/shard_map/all_to_all | solution.py:39
  23.8 0.9 broadcast_select_fusion
  24.7 8.2 %all-to-all-start.1 = ((bf16[8,256,128]{2,1,0:T(8,128)(2,1)}), bf16[8,256,128]{2,1,0:T(8,128)(2,1)S(1)}, u32[]{:S(2)}, u32[]{:S(2)}) async-start(bf16[8,256,128]{2,1,0:T(8,128)(2,1)} %broadcast_select_fusion), calls=%async_computation.1 | async-start | bytes 1048576 | tf_op jit(solution)/shard_map/all_to_all | solution.py:39
  33.1 1.1 pad_maximum_fusion
  34.2 1.7 collective-permute-start.2
  35.9 1.1 pad_maximum_fusion.1
  37.0 1.7 shard_map.103
  38.7 12.1 %all-to-all-done.1 = bf16[8,256,128]{2,1,0:T(8,128)(2,1)S(1)} async-done(((bf16[8,256,128]{2,1,0:T(8,128)(2,1)}), bf16[8,256,128]{2,1,0:T(8,128)(2,1)S(1)}, u32[]{:S(2)}, u32[]{:S(2)}) %all-to-all-start.1) | async-done | bytes 524320 | tf_op jit(solution)/shard_map/all_to_all | solution.py:39
  50.8 0.6 slice.39
  51.5 0.8 slice.38
  52.3 0.6 slice.41
  52.9 0.9 slice.40
  53.8 0.5 collective-permute-start.6
  54.3 4.1 %all-to-all-start.2 = ((bf16[16,80,128]{2,1,0:T(8,128)(2,1)}), bf16[16,80,128]{2,1,0:T(8,128)(2,1)}, u32[]{:S(2)}, u32[]{:S(2)}) async-start(bf16[16,80,128]{2,1,0:T(8,128)(2,1)} %shard_map.103), calls=%async_computation.2 | async-start | bytes 655360 | tf_op jit(solution)/shard_map/all_to_all | solution.py:39
  58.4 2.0 %pad_maximum_fusion.3 = bf16[128,2304]{1,0:T(8,128)(2,1)} fusion(bf16[128,256]{1,0:T(8,128)(2,1)} %slice.41, bf16[128,2048]{1,0:T(8,128)(2,1)} %slice.40), kind=kLoop, calls=%fused_computation.5 | loop fusion | flops 1179648 | bytes 1179648 | tf_op jit(solution)/shard_map/concatenate | solution.py:293
  60.4 0.9 pad_maximum_fusion.2
  61.3 1.5 collective-permute-start.8
  62.8 7.3 %all-to-all-done.2 = bf16[16,80,128]{2,1,0:T(8,128)(2,1)} async-done(((bf16[16,80,128]{2,1,0:T(8,128)(2,1)}), bf16[16,80,128]{2,1,0:T(8,128)(2,1)}, u32[]{:S(2)}, u32[]{:S(2)}) %all-to-all-start.2) | async-done | bytes 327712 | tf_op jit(solution)/shard_map/all_to_all | solution.py:39
  70.0 0.2 collective-permute-start.4
  70.3 0.3 collective-permute-start.5
  70.5 5.0 %collective-permute-done.9.refs_5_ = bf16[128,2304]{1,0:T(8,128)(2,1)} collective-permute-done((bf16[128,2304]{1,0:T(8,128)(2,1)}, bf16[128,2304]{1,0:T(8,128)(2,1)}, u32[]{:S(2)}, u32[]{:S(2)}) %collective-permute-start.9) | collective-permute-done | bytes 589856 | tf_op jit(solution)/shard_map/ppermute | solution.py:31
  75.5 0.9 collective-permute-start.7
  76.5 1.1 collective-permute-done.8.refs_4_
  77.6 0.9 collective-permute-start.11
  78.6 2.0 %collective-permute-done.11.refs_7_ = bf16[128,2304]{1,0:T(8,128)(2,1)} collective-permute-done((bf16[128,2304]{1,0:T(8,128)(2,1)}, bf16[128,2304]{1,0:T(8,128)(2,1)}, u32[]{:S(2)}, u32[]{:S(2)}) %collective-permute-start.11) | collective-permute-done | bytes 589856 | tf_op jit(solution)/shard_map/ppermute | solution.py:31
  80.5 0.8 collective-permute-done.10.refs_6_
  81.4 4.7 %shard_map.106.refs_4_ = f32[128,2048]{1,0:T(8,128)S(1)} custom-call(s32[1]{0:T(128)} %bitcast.7.core, bf16[2048,128]{1,0:T(8,128)(2,1)S(1)} %bitcast.64, bf16[128,3072]{1,0:T(8,128)(2,1)S(1)} %collective-permute-done.refs_0_, bf16[128,3072]{1,0:T(8,128)(2,1)S(1)} %collective-permute-done.1.refs_1_, bf16[128,3072]{1,0:T(8,128)(2,1)} %collective-permute-done.6.refs_2_, ...), custom_call_target="tpu_custom_call" | custom-call | flops 2147483648 | bytes 4194304 | tf_op jit(solution)/shard_map/pallas_call | solution.py:244
  86.2 5.8 %shard_map.107 = bf16[8,256,128]{2,1,0:T(8,128)(2,1)} custom-call(s32[1]{0:T(128)} %bitcast.7.core, bf16[2048,128]{1,0:T(8,128)(2,1)S(1)} %bitcast.65, bf16[256,2304]{1,0:T(8,128)(2,1)} %collective-permute-done.3.refs_0_.refs_8_, bf16[256,2304]{1,0:T(8,128)(2,1)} %collective-permute-done.4.refs_1_.refs_9_, ...), custom_call_target="tpu_custom_call" | custom-call | flops 2147483648 | bytes 4194304 | tf_op jit(solution)/shard_map/pallas_call | solution.py:244
  92.0 4.0 %all-to-all-start.3 = ((bf16[8,256,128]{2,1,0:T(8,128)(2,1)}), bf16[8,256,128]{2,1,0:T(8,128)(2,1)S(1)}, u32[]{:S(2)}, u32[]{:S(2)}) async-start(bf16[8,256,128]{2,1,0:T(8,128)(2,1)} %shard_map.107), calls=%async_computation.3 | async-start | bytes 1048576 | tf_op jit(solution)/shard_map/all_to_all | solution.py:264
  96.0 0.9 dynamic-slice_bitcast_fusion
  97.0 0.5 slice.49
  98.2 0.7 convert_multiply_fusion.1
  98.9 12.3 %all-to-all-done.3 = bf16[8,256,128]{2,1,0:T(8,128)(2,1)S(1)} async-done(((bf16[8,256,128]{2,1,0:T(8,128)(2,1)}), bf16[8,256,128]{2,1,0:T(8,128)(2,1)S(1)}, u32[]{:S(2)}, u32[]{:S(2)}) %all-to-all-start.3) | async-done | bytes 524320 | tf_op jit(solution)/shard_map/all_to_all | solution.py:264
  111.3 1.2 convert_bitcast_fusion
  112.6 22.1 %all_to_all.35 = bf16[8,256,128]{2,1,0:T(8,128)(2,1)S(1)} all-to-all(bf16[8,256,128]{2,1,0:T(8,128)(2,1)S(1)} %broadcast_in_dim.51), channel_id=1, replica_groups={{0,12,16,28,32,44,48,60},{2,14,18,30,34,46,50,62},{4,8,20,24,36,40,52,5..., dimensions={0} | all-to-all | bytes 1048576 | tf_op jit(solution)/shard_map/all_to_all | solution.py:264
  134.7 9.8 %shard_map.108 = bf16[8,256,128]{2,1,0:T(8,128)(2,1)} custom-call(s32[1]{0:T(128)} %bitcast.7.core, bf16[2048,128]{1,0:T(8,128)(2,1)S(1)} %bitcast.66, bf16[128,3072]{1,0:T(8,128)(2,1)S(1)} %collective-permute-done.refs_0_, bf16[128,3072]{1,0:T(8,128)(2,1)S(1)} %collective-permute-done.1.refs_1_, bf16[128,3072]{1,0:T(8,128)(2,1)} %collective-permute-done.6.refs_2_, ...), custom_call_target="tpu_custom_call" | custom-call | flops 4294967296 | bytes 8388608 | tf_op jit(solution)/shard_map/pallas_call | solution.py:244
  144.6 4.4 %all-to-all-start.5 = ((bf16[8,256,128]{2,1,0:T(8,128)(2,1)}), bf16[8,256,128]{2,1,0:T(8,128)(2,1)S(1)}, u32[]{:S(2)}, u32[]{:S(2)}) async-start(bf16[8,256,128]{2,1,0:T(8,128)(2,1)} %shard_map.108), calls=%async_computation.5 | async-start | bytes 1048576 | tf_op jit(solution)/shard_map/all_to_all | solution.py:264
  149.0 14.4 %all-to-all-done.5 = bf16[8,256,128]{2,1,0:T(8,128)(2,1)S(1)} async-done(((bf16[8,256,128]{2,1,0:T(8,128)(2,1)}), bf16[8,256,128]{2,1,0:T(8,128)(2,1)S(1)}, u32[]{:S(2)}, u32[]{:S(2)}) %all-to-all-start.5) | async-done | bytes 524320 | tf_op jit(solution)/shard_map/all_to_all | solution.py:264
  163.5 0.2 fusion.2
  163.8 0.1 broadcast_in_dim.52
  163.9 21.9 %all_to_all.36.arrived = bf16[32,3,32,128]{3,2,1,0:T(8,128)(2,1)S(1)} all-to-all(bf16[32,3,32,128]{3,2,1,0:T(8,128)(2,1)S(1)} %bitcast.67), channel_id=1, replica_groups=mesh['h'=2,'c'=2,'z'=8,'yh'=2,'yl'=2,'x'=2] {'h','c','yh','yl','x'}, dimensions={0} | all-to-all | bytes 1572864 | tf_op jit(solution)/shard_map/all_to_all | solution.py:39
  185.9 0.8 shard_map.109
  (47 shorter events, 0.5 us)
Async XLA Ops:
  3.4 29.5 %collective-permute-start.1 = (bf16[128,3072]{1,0:T(8,128)(2,1)}, bf16[128,3072]{1,0:T(8,128)(2,1)S(1)}, u32[]{:S(2)}, u32[]{:S(2)}) collective-permute-start(bf16[128,3072]{1,0:T(8,128)(2,1)} %shard_map.105), channel_id=1, source_target_pairs={{0,0},{1,64},{64,1},{65,65},{2,2},{3,66},{66,3},{67,67},{4,4},{5,6... | collective-permute-start | bytes 2359304 | tf_op jit(solution)/shard_map/ppermute | solution.py:51
  9.3 14.4 %all-to-all-start = ((bf16[16,32,128]{2,1,0:T(8,128)(2,1)}), bf16[16,32,128]{2,1,0:T(8,128)(2,1)S(1)}, u32[]{:S(2)}, u32[]{:S(2)}) async-start(bf16[16,32,128]{2,1,0:T(8,128)(2,1)} %shard_map.102), calls=%async_computation | async-start | bytes 262144 | tf_op jit(solution)/shard_map/all_to_all | solution.py:39
  18.6 14.4 %collective-permute-start = (bf16[128,3072]{1,0:T(8,128)(2,1)}, bf16[128,3072]{1,0:T(8,128)(2,1)S(1)}, u32[]{:S(2)}, u32[]{:S(2)}) collective-permute-start(bf16[128,3072]{1,0:T(8,128)(2,1)} %shard_map.104), channel_id=1, source_target_pairs={{0,0},{1,64},{64,1},{65,65},{2,2},{3,66},{66,3},{67,67},{4,4},{5,6... | collective-permute-start | bytes 2359304 | tf_op jit(solution)/shard_map/ppermute | solution.py:51
  23.8 9.1 %copy-start.10 = (bf16[16,32,128]{2,1,0:T(8,128)(2,1)}, bf16[16,32,128]{2,1,0:T(8,128)(2,1)S(1)}, u32[]{:S(2)}) copy-start(bf16[16,32,128]{2,1,0:T(8,128)(2,1)S(1)} %all-to-all-done) | copy-start | bytes 393220
  24.7 26.1 %all-to-all-start.1 = ((bf16[8,256,128]{2,1,0:T(8,128)(2,1)}), bf16[8,256,128]{2,1,0:T(8,128)(2,1)S(1)}, u32[]{:S(2)}, u32[]{:S(2)}) async-start(bf16[8,256,128]{2,1,0:T(8,128)(2,1)} %broadcast_select_fusion), calls=%async_computation.1 | async-start | bytes 1048576 | tf_op jit(solution)/shard_map/all_to_all | solution.py:39
  34.2 35.9 %collective-permute-start.2 = (bf16[256,2304]{1,0:T(8,128)(2,1)}, bf16[256,2304]{1,0:T(8,128)(2,1)S(1)}, u32[]{:S(2)}, u32[]{:S(2)}) collective-permute-start(bf16[256,2304]{1,0:T(8,128)(2,1)} %pad_maximum_fusion), channel_id=1, source_target_pairs={{0,6},{2,0},{4,2},{6,4},{1,7},{3,1},{5,3},{7,5},{8,14},{10,8},{12,... | collective-permute-start | bytes 3538952 | tf_op jit(solution)/shard_map/ppermute | solution.py:31
  35.9 1.1 copy-start
  35.9 1.1 copy-start.1
  35.9 1.1 copy-start.4
  37.0 33.0 %collective-permute-start.3 = (bf16[256,2304]{1,0:T(8,128)(2,1)}, bf16[256,2304]{1,0:T(8,128)(2,1)}, u32[]{:S(2)}, u32[]{:S(2)}) collective-permute-start(bf16[256,2304]{1,0:T(8,128)(2,1)} %pad_maximum_fusion.1), channel_id=1, source_target_pairs={{0,2},{2,4},{4,6},{6,0},{1,3},{3,5},{5,7},{7,1},{8,10},{10,12},{12... | collective-permute-start | bytes 3538952 | tf_op jit(solution)/shard_map/ppermute | solution.py:31
  53.8 24.8 %collective-permute-start.6 = (bf16[128,3072]{1,0:T(8,128)(2,1)S(1)}, bf16[128,3072]{1,0:T(8,128)(2,1)}, u32[]{:S(2)}, u32[]{:S(2)}) collective-permute-start(bf16[128,3072]{1,0:T(8,128)(2,1)S(1)} %collective-permute-done.refs_0_), channel_id=1, source_target_pairs={{0,64},{64,0},{1,65},{65,1},{2,66},{66,2},{3,67},{67,3},{4,68},{68... | collective-permute-start | bytes 2359304 | tf_op jit(solution)/shard_map/ppermute | solution.py:31
  54.3 15.7 %all-to-all-start.2 = ((bf16[16,80,128]{2,1,0:T(8,128)(2,1)}), bf16[16,80,128]{2,1,0:T(8,128)(2,1)}, u32[]{:S(2)}, u32[]{:S(2)}) async-start(bf16[16,80,128]{2,1,0:T(8,128)(2,1)} %shard_map.103), calls=%async_computation.2 | async-start | bytes 655360 | tf_op jit(solution)/shard_map/all_to_all | solution.py:39
  58.4 2.0 %copy-start.7 = (bf16[128,2048]{1,0:T(8,128)(2,1)S(1)}, bf16[128,2048]{1,0:T(8,128)(2,1)}, u32[]{:S(2)}) copy-start(bf16[128,2048]{1,0:T(8,128)(2,1)} %slice.38) | copy-start | bytes 1572868
  58.4 2.0 %copy-start.12 = (bf16[128,256]{1,0:T(8,128)(2,1)S(1)}, bf16[128,256]{1,0:T(8,128)(2,1)}, u32[]{:S(2)}) copy-start(bf16[128,256]{1,0:T(8,128)(2,1)} %slice.39) | copy-start | bytes 196612
  60.4 15.1 %collective-permute-start.9 = (bf16[128,2304]{1,0:T(8,128)(2,1)}, bf16[128,2304]{1,0:T(8,128)(2,1)}, u32[]{:S(2)}, u32[]{:S(2)}) collective-permute-start(bf16[128,2304]{1,0:T(8,128)(2,1)} %pad_maximum_fusion.3), channel_id=1, source_target_pairs={{0,56},{8,0},{16,8},{24,16},{32,24},{40,32},{48,40},{56,48},{1,57}... | collective-permute-start | bytes 1769480 | tf_op jit(solution)/shard_map/ppermute | solution.py:31
  61.3 16.3 %collective-permute-start.8 = (bf16[128,2304]{1,0:T(8,128)(2,1)}, bf16[128,2304]{1,0:T(8,128)(2,1)}, u32[]{:S(2)}, u32[]{:S(2)}) collective-permute-start(bf16[128,2304]{1,0:T(8,128)(2,1)} %pad_maximum_fusion.2), channel_id=1, source_target_pairs={{0,8},{8,16},{16,24},{24,32},{32,40},{40,48},{48,56},{56,0},{1,9},... | collective-permute-start | bytes 1769480 | tf_op jit(solution)/shard_map/ppermute | solution.py:31
  70.0 16.1 %collective-permute-start.4 = (bf16[256,2304]{1,0:T(8,128)(2,1)}, bf16[256,2304]{1,0:T(8,128)(2,1)}, u32[]{:S(2)}, u32[]{:S(2)}) collective-permute-start(bf16[256,2304]{1,0:T(8,128)(2,1)} %collective-permute-done.3.refs_0_.refs_8_), channel_id=1, source_target_pairs={{0,64},{64,0},{1,65},{65,1},{2,66},{66,2},{3,67},{67,3},{4,68},{68... | collective-permute-start | bytes 3538952 | tf_op jit(solution)/shard_map/ppermute | solution.py:31
  70.3 15.9 %collective-permute-start.5 = (bf16[256,2304]{1,0:T(8,128)(2,1)S(1)}, bf16[256,2304]{1,0:T(8,128)(2,1)}, u32[]{:S(2)}, u32[]{:S(2)}) collective-permute-start(bf16[256,2304]{1,0:T(8,128)(2,1)S(1)} %collective-permute-done.2.refs_2_.refs_10_), channel_id=1, source_target_pairs={{0,64},{64,0},{1,65},{65,1},{2,66},{66,2},{3,67},{67,3},{4,68},{68... | collective-permute-start | bytes 3538952 | tf_op jit(solution)/shard_map/ppermute | solution.py:31
  75.5 3.1 %collective-permute-start.7 = (bf16[128,3072]{1,0:T(8,128)(2,1)S(1)}, bf16[128,3072]{1,0:T(8,128)(2,1)}, u32[]{:S(2)}, u32[]{:S(2)}) collective-permute-start(bf16[128,3072]{1,0:T(8,128)(2,1)S(1)} %collective-permute-done.1.refs_1_), channel_id=1, source_target_pairs={{0,64},{64,0},{1,65},{65,1},{2,66},{66,2},{3,67},{67,3},{4,68},{68... | collective-permute-start | bytes 2359304 | tf_op jit(solution)/shard_map/ppermute | solution.py:31
  77.6 2.9 %collective-permute-start.11 = (bf16[128,2304]{1,0:T(8,128)(2,1)}, bf16[128,2304]{1,0:T(8,128)(2,1)}, u32[]{:S(2)}, u32[]{:S(2)}) collective-permute-start(bf16[128,2304]{1,0:T(8,128)(2,1)} %collective-permute-done.9.refs_5_), channel_id=1, source_target_pairs={{0,64},{64,0},{1,65},{65,1},{2,66},{66,2},{3,67},{67,3},{4,68},{68... | collective-permute-start | bytes 1769480 | tf_op jit(solution)/shard_map/ppermute | solution.py:31
  78.6 2.8 %collective-permute-start.10 = (bf16[128,2304]{1,0:T(8,128)(2,1)}, bf16[128,2304]{1,0:T(8,128)(2,1)}, u32[]{:S(2)}, u32[]{:S(2)}) collective-permute-start(bf16[128,2304]{1,0:T(8,128)(2,1)} %collective-permute-done.8.refs_4_), channel_id=1, source_target_pairs={{0,64},{64,0},{1,65},{65,1},{2,66},{66,2},{3,67},{67,3},{4,68},{68... | collective-permute-start | bytes 1769480 | tf_op jit(solution)/shard_map/ppermute | solution.py:31
  92.0 19.3 %all-to-all-start.3 = ((bf16[8,256,128]{2,1,0:T(8,128)(2,1)}), bf16[8,256,128]{2,1,0:T(8,128)(2,1)S(1)}, u32[]{:S(2)}, u32[]{:S(2)}) async-start(bf16[8,256,128]{2,1,0:T(8,128)(2,1)} %shard_map.107), calls=%async_computation.3 | async-start | bytes 1048576 | tf_op jit(solution)/shard_map/all_to_all | solution.py:264
  111.3 1.2 copy-start.5
  134.7 14.3 %copy-start.6 = (f32[256,128]{1,0:T(8,128)S(1)}, f32[256,128]{1,0:T(8,128)}, u32[]{:S(2)}) copy-start(f32[256,128]{1,0:T(8,128)} %copy-done.5) | copy-start | bytes 393220
  144.5 19.0 %copy-start.8 = (f32[8,32,128]{2,1,0:T(8,128)S(1)}, f32[8,32,128]{2,1,0:T(8,128)}, u32[]{:S(2)}) copy-start(f32[8,32,128]{2,1,0:T(8,128)} %get-tuple-element.22) | copy-start | bytes 393220
  144.5 19.0 %copy-start.9 = (f32[8,32,128]{2,1,0:T(8,128)S(1)}, f32[8,32,128]{2,1,0:T(8,128)}, u32[]{:S(2)}) copy-start(f32[8,32,128]{2,1,0:T(8,128)} %get-tuple-element.23) | copy-start | bytes 393220
  144.6 19.0 %copy-start.11 = (bf16[16,32,128]{2,1,0:T(8,128)(2,1)S(1)}, bf16[16,32,128]{2,1,0:T(8,128)(2,1)}, u32[]{:S(2)}) copy-start(bf16[16,32,128]{2,1,0:T(8,128)(2,1)} %copy-done.10) | copy-start | bytes 393220
  144.6 18.8 %all-to-all-start.5 = ((bf16[8,256,128]{2,1,0:T(8,128)(2,1)}), bf16[8,256,128]{2,1,0:T(8,128)(2,1)S(1)}, u32[]{:S(2)}, u32[]{:S(2)}) async-start(bf16[8,256,128]{2,1,0:T(8,128)(2,1)} %shard_map.108), calls=%async_computation.5 | async-start | bytes 1048576 | tf_op jit(solution)/shard_map/all_to_all | solution.py:264
  163.8 22.1 %copy-start.2 = (f32[32,256]{1,0:T(8,128)S(1)}, f32[32,256]{1,0:T(8,128)}, u32[]{:S(2)}) copy-start(f32[32,256]{1,0:T(8,128)} %param.17) | copy-start | bytes 98308
  163.8 22.1 %copy-start.3 = (f32[32,256]{1,0:T(8,128)S(1)}, f32[32,256]{1,0:T(8,128)}, u32[]{:S(2)}) copy-start(f32[32,256]{1,0:T(8,128)} %mom.1) | copy-start | bytes 98308

commit v11 on v10

--- a/solution.py
+++ b/solution.py
@@ -306,11 +306,11 @@
 
     moments, weights = together(pack_moments(lengths, first_mom, second_mom), weights)
     moments = exchange(moments, ("c", "yh", "yl", "x"))
-    moments, above = together(moments, above)
+    moments, held = together(moments, mine_b)
     moments = pick(moments.reshape(2, 8, 80, BLOCK), x, 0)
 
     near = [(block, WIDE, D + 3 * WIDE) for block in (mine_a, mine_b)]
-    near += [(other_core(block), WIDE, D + 3 * WIDE) for block in (mine_a, mine_b)]
+    near += [(other_core(block), WIDE, D + 3 * WIDE) for block in (mine_a, held)]
     near += [
         (block, 0, D)
         for block in (before, behind, other_core(before), other_core(behind))

time: 188 us -> 184 us (0.979)
  starting transfers between devices: 40.7 us -> 49.1 us
  waiting for transfers between devices: 57.3 us -> 50.4 us
  local copies, waits for them, and re-layouts: 4.84 us -> 1.92 us
    ppermute x10, waiting for transfers between devices: 8.95 us -> 3.75 us  [shift(): return lax.ppermute(x, axis, [(i, (i + by) % size) for i in range(size)])]
    ppermute x10, starting transfers between devices: 6.08 us -> 11.1 us  [shift(): return lax.ppermute(x, axis, [(i, (i + by) % size) for i in range(size)])]
    all_to_all x2, starting transfers between devices: 8.43 us -> 11.3 us  [among_peers(): return lax.all_to_all(x, axes, 0, 0, axis_index_groups=PEERS, tiled=True)]
    all_to_all x3, waiting for transfers between devices: 21.6 us -> 18.7 us  [exchange(): return lax.all_to_all(x, axes, 0, 0, tiled=True)]
  transfers between devices with their start and end apart: 17 -> 17, of which waited for: 9 -> 9; matrix products, arithmetic and copies ran while one was open for 6% -> 4% of each run, Pallas kernels for 6% -> 6%
where the time goes in v11:
time: 184 us; the launch traced here: 183 us
  waiting for transfers between devices  50.4 us (27%)
  starting transfers between devices  49.1 us (27%)
  blocking collectives  43.4 us (24%)
  Pallas kernels  29.8 us (16%)
  other arithmetic  7.1 us (4%)
  local copies, waits for them, and re-layouts  1.92 us (1%)
    all_to_all x2, waiting for transfers between devices, among_peers(): return lax.all_to_all(x, axes, 0, 0, axis_index_groups=PEERS, tiled=True)  27.9 us
    all_to_all x1, blocking collectives, among_peers(): return lax.all_to_all(x, axes, 0, 0, axis_index_groups=PEERS, tiled=True)  22 us
    all_to_all x1, blocking collectives, exchange(): return lax.all_to_all(x, axes, 0, 0, tiled=True)  21.4 us
    pallas_call x3, Pallas kernels, product(): pl.pallas_call(functools.partial(product_kernel, layout, last), out_shape...  20.4 us
    all_to_all x3, starting transfers between devices, exchange(): return lax.all_to_all(x, axes, 0, 0, tiled=True)  19.2 us
    all_to_all x3, waiting for transfers between devices, exchange(): return lax.all_to_all(x, axes, 0, 0, tiled=True)  18.7 us
    all_to_all x2, starting transfers between devices, among_peers(): return lax.all_to_all(x, axes, 0, 0, axis_index_groups=PEERS, tiled=True)  11.3 us
    ppermute x10, starting transfers between devices, shift(): return lax.ppermute(x, axis, [(i, (i + by) % size) for i in range(size)])  11.1 us
  transfers between devices with their start and end apart: 17, of which 9 were waited for; matrix products, arithmetic and copies ran while one was open for 4% of the time, Pallas kernels for 6%

profile of v11, /device:TPU:1, one launch (start us, length us, event | category | flops | bytes accessed | tf_op | source)
XLA Modules:
  0.0 183.4 jit_solution(8730831861597427362)
XLA Ops:
  0.6 2.8 %shard_map.105 = bf16[128,3072]{1,0:T(8,128)(2,1)} custom-call(s32[1,64]{1,0:T(1,128)} %lengths.5, bf16[1,256,2048]{2,1,0:T(8,128)(2,1)} %tokens.3, bf16[1,256,1024]{2,1,0:T(8,128)(2,1)} %targets.3), custom_call_target="tpu_custom_call" | custom-call | tf_op jit(solution)/shard_map/pallas_call | solution.py:94
  3.4 4.5 %collective-permute-start.1 = (bf16[128,3072]{1,0:T(8,128)(2,1)}, bf16[128,3072]{1,0:T(8,128)(2,1)S(1)}, u32[]{:S(2)}, u32[]{:S(2)}) collective-permute-start(bf16[128,3072]{1,0:T(8,128)(2,1)} %shard_map.105), channel_id=1, source_target_pairs={{0,0},{1,64},{64,1},{65,65},{2,2},{3,66},{66,3},{67,67},{4,4},{5,6... | collective-permute-start | bytes 2359304 | tf_op jit(solution)/shard_map/ppermute | solution.py:51
  7.9 1.4 shard_map.102
  9.3 6.5 %all-to-all-start = ((bf16[16,32,128]{2,1,0:T(8,128)(2,1)}), bf16[16,32,128]{2,1,0:T(8,128)(2,1)S(1)}, u32[]{:S(2)}, u32[]{:S(2)}) async-start(bf16[16,32,128]{2,1,0:T(8,128)(2,1)} %shard_map.102), calls=%async_computation | async-start | bytes 262144 | tf_op jit(solution)/shard_map/all_to_all | solution.py:39
  15.8 2.7 %shard_map.104 = bf16[128,3072]{1,0:T(8,128)(2,1)} custom-call(s32[1,64]{1,0:T(1,128)} %lengths.5, bf16[1,256,2048]{2,1,0:T(8,128)(2,1)} %tokens.3, bf16[1,256,1024]{2,1,0:T(8,128)(2,1)} %targets.3), custom_call_target="tpu_custom_call" | custom-call | tf_op jit(solution)/shard_map/pallas_call | solution.py:94
  18.6 2.9 %collective-permute-start = (bf16[128,3072]{1,0:T(8,128)(2,1)}, bf16[128,3072]{1,0:T(8,128)(2,1)S(1)}, u32[]{:S(2)}, u32[]{:S(2)}) collective-permute-start(bf16[128,3072]{1,0:T(8,128)(2,1)} %shard_map.104), channel_id=1, source_target_pairs={{0,0},{1,64},{64,1},{65,65},{2,2},{3,66},{66,3},{67,67},{4,4},{5,6... | collective-permute-start | bytes 2359304 | tf_op jit(solution)/shard_map/ppermute | solution.py:51
  21.5 2.2 %all-to-all-done = bf16[16,32,128]{2,1,0:T(8,128)(2,1)S(1)} async-done(((bf16[16,32,128]{2,1,0:T(8,128)(2,1)}), bf16[16,32,128]{2,1,0:T(8,128)(2,1)S(1)}, u32[]{:S(2)}, u32[]{:S(2)}) %all-to-all-start) | async-done | bytes 131104 | tf_op jit(solution)/shard_map/all_to_all | solution.py:39
  23.8 0.9 broadcast_select_fusion
  24.7 8.2 %all-to-all-start.1 = ((bf16[8,256,128]{2,1,0:T(8,128)(2,1)}), bf16[8,256,128]{2,1,0:T(8,128)(2,1)S(1)}, u32[]{:S(2)}, u32[]{:S(2)}) async-start(bf16[8,256,128]{2,1,0:T(8,128)(2,1)} %broadcast_select_fusion), calls=%async_computation.1 | async-start | bytes 1048576 | tf_op jit(solution)/shard_map/all_to_all | solution.py:39
  32.9 0.1 fusion.15
  33.1 1.1 pad_maximum_fusion
  34.2 0.4 collective-permute-start.2
  34.6 1.1 pad_maximum_fusion.1
  35.7 2.3 %collective-permute-start.4 = (bf16[256,2304]{1,0:T(8,128)(2,1)}, bf16[256,2304]{1,0:T(8,128)(2,1)}, u32[]{:S(2)}, u32[]{:S(2)}) collective-permute-start(bf16[256,2304]{1,0:T(8,128)(2,1)} %pad_maximum_fusion.1), channel_id=1, source_target_pairs={{0,6},{2,0},{4,2},{6,4},{1,7},{3,1},{5,3},{7,5},{8,14},{10,8},{12,... | collective-permute-start | bytes 3538952 | tf_op jit(solution)/shard_map/ppermute | solution.py:31
  38.0 12.9 %all-to-all-done.1 = bf16[8,256,128]{2,1,0:T(8,128)(2,1)S(1)} async-done(((bf16[8,256,128]{2,1,0:T(8,128)(2,1)}), bf16[8,256,128]{2,1,0:T(8,128)(2,1)S(1)}, u32[]{:S(2)}, u32[]{:S(2)}) %all-to-all-start.1) | async-done | bytes 524320 | tf_op jit(solution)/shard_map/all_to_all | solution.py:39
  51.0 0.6 collective-permute-start.6
  51.5 0.8 pad_maximum_fusion.2
  52.4 0.3 collective-permute-start.8
  52.7 0.9 pad_maximum_fusion.3
  53.5 2.4 %collective-permute-start.9 = (bf16[128,2304]{1,0:T(8,128)(2,1)}, bf16[128,2304]{1,0:T(8,128)(2,1)S(1)}, u32[]{:S(2)}, u32[]{:S(2)}) collective-permute-start(bf16[128,2304]{1,0:T(8,128)(2,1)} %pad_maximum_fusion.3), channel_id=1, source_target_pairs={{0,56},{8,0},{16,8},{24,16},{32,24},{40,32},{48,40},{56,48},{1,57}... | collective-permute-start | bytes 1769480 | tf_op jit(solution)/shard_map/ppermute | solution.py:31
  55.9 1.7 shard_map.103
  57.6 4.6 %all-to-all-start.2 = ((bf16[16,80,128]{2,1,0:T(8,128)(2,1)}), bf16[16,80,128]{2,1,0:T(8,128)(2,1)}, u32[]{:S(2)}, u32[]{:S(2)}) async-start(bf16[16,80,128]{2,1,0:T(8,128)(2,1)} %shard_map.103), calls=%async_computation.2 | async-start | bytes 655360 | tf_op jit(solution)/shard_map/all_to_all | solution.py:39
  62.2 0.5 collective-permute-done.2.refs_0_.refs_8_
  62.7 1.4 collective-permute-start.3
  64.1 1.7 collective-permute-start.5
  65.8 3.6 %all-to-all-done.2 = bf16[16,80,128]{2,1,0:T(8,128)(2,1)} async-done(((bf16[16,80,128]{2,1,0:T(8,128)(2,1)}), bf16[16,80,128]{2,1,0:T(8,128)(2,1)}, u32[]{:S(2)}, u32[]{:S(2)}) %all-to-all-start.2) | async-done | bytes 327712 | tf_op jit(solution)/shard_map/all_to_all | solution.py:39
  69.4 1.6 collective-permute-start.7
  71.0 0.1 collective-permute-start.10
  71.1 0.4 collective-permute-start.11
  71.5 1.5 collective-permute-done.7.refs_3_
  73.1 0.8 collective-permute-done.10.refs_6_
  73.9 0.8 collective-permute-done.11.refs_7_
  74.7 4.7 %shard_map.106.refs_4_ = f32[128,2048]{1,0:T(8,128)S(1)} custom-call(s32[1]{0:T(128)} %bitcast.7.core, bf16[2048,128]{1,0:T(8,128)(2,1)S(1)} %bitcast.64, bf16[128,3072]{1,0:T(8,128)(2,1)S(1)} %collective-permute-done.refs_0_, bf16[128,3072]{1,0:T(8,128)(2,1)S(1)} %copy-done.1, bf16[128,3072]{1,0:T(8,128)(2,1)} %collective-permute-done.6.refs_2_, ...), custom_call_target="tpu_custom_call" | custom-call | flops 2147483648 | bytes 4194304 | tf_op jit(solution)/shard_map/pallas_call | solution.py:244
  79.5 5.8 %shard_map.107 = bf16[8,256,128]{2,1,0:T(8,128)(2,1)} custom-call(s32[1]{0:T(128)} %bitcast.7.core, bf16[2048,128]{1,0:T(8,128)(2,1)S(1)} %bitcast.65, bf16[256,2304]{1,0:T(8,128)(2,1)} %collective-permute-done.2.refs_0_.refs_8_, bf16[256,2304]{1,0:T(8,128)(2,1)} %collective-permute-done.3.refs_1_.refs_9_, ...), custom_call_target="tpu_custom_call" | custom-call | flops 2147483648 | bytes 4194304 | tf_op jit(solution)/shard_map/pallas_call | solution.py:244
  85.3 7.0 %all-to-all-start.3 = ((bf16[8,256,128]{2,1,0:T(8,128)(2,1)}), bf16[8,256,128]{2,1,0:T(8,128)(2,1)S(1)}, u32[]{:S(2)}, u32[]{:S(2)}) async-start(bf16[8,256,128]{2,1,0:T(8,128)(2,1)} %shard_map.107), calls=%async_computation.3 | async-start | bytes 1048576 | tf_op jit(solution)/shard_map/all_to_all | solution.py:264
  92.3 0.9 dynamic-slice_bitcast_fusion
  93.3 0.5 slice.49
  94.5 0.7 convert_multiply_fusion.1
  95.2 12.8 %all-to-all-done.3 = bf16[8,256,128]{2,1,0:T(8,128)(2,1)S(1)} async-done(((bf16[8,256,128]{2,1,0:T(8,128)(2,1)}), bf16[8,256,128]{2,1,0:T(8,128)(2,1)S(1)}, u32[]{:S(2)}, u32[]{:S(2)}) %all-to-all-start.3) | async-done | bytes 524320 | tf_op jit(solution)/shard_map/all_to_all | solution.py:264
  108.0 1.2 convert_bitcast_fusion
  109.3 22.0 %all_to_all.35 = bf16[8,256,128]{2,1,0:T(8,128)(2,1)S(1)} all-to-all(bf16[8,256,128]{2,1,0:T(8,128)(2,1)S(1)} %broadcast_in_dim.51), channel_id=1, replica_groups={{0,12,16,28,32,44,48,60},{2,14,18,30,34,46,50,62},{4,8,20,24,36,40,52,5..., dimensions={0} | all-to-all | bytes 1048576 | tf_op jit(solution)/shard_map/all_to_all | solution.py:264
  131.3 9.8 %shard_map.108 = bf16[8,256,128]{2,1,0:T(8,128)(2,1)} custom-call(s32[1]{0:T(128)} %bitcast.7.core, bf16[2048,128]{1,0:T(8,128)(2,1)S(1)} %bitcast.66, bf16[128,3072]{1,0:T(8,128)(2,1)S(1)} %collective-permute-done.refs_0_, bf16[128,3072]{1,0:T(8,128)(2,1)S(1)} %copy-done.1, bf16[128,3072]{1,0:T(8,128)(2,1)} %collective-permute-done.6.refs_2_, ...), custom_call_target="tpu_custom_call" | custom-call | flops 4294967296 | bytes 8388608 | tf_op jit(solution)/shard_map/pallas_call | solution.py:244
  141.2 4.4 %all-to-all-start.5 = ((bf16[8,256,128]{2,1,0:T(8,128)(2,1)}), bf16[8,256,128]{2,1,0:T(8,128)(2,1)S(1)}, u32[]{:S(2)}, u32[]{:S(2)}) async-start(bf16[8,256,128]{2,1,0:T(8,128)(2,1)} %shard_map.108), calls=%async_computation.5 | async-start | bytes 1048576 | tf_op jit(solution)/shard_map/all_to_all | solution.py:264
  145.5 15.2 %all-to-all-done.5 = bf16[8,256,128]{2,1,0:T(8,128)(2,1)S(1)} async-done(((bf16[8,256,128]{2,1,0:T(8,128)(2,1)}), bf16[8,256,128]{2,1,0:T(8,128)(2,1)S(1)}, u32[]{:S(2)}, u32[]{:S(2)}) %all-to-all-start.5) | async-done | bytes 524320 | tf_op jit(solution)/shard_map/all_to_all | solution.py:264
  160.8 0.2 fusion.2
  161.1 0.1 broadcast_in_dim.52
  161.2 21.4 %all_to_all.36.arrived = bf16[32,3,32,128]{3,2,1,0:T(8,128)(2,1)S(1)} all-to-all(bf16[32,3,32,128]{3,2,1,0:T(8,128)(2,1)S(1)} %bitcast.67), channel_id=1, replica_groups=mesh['h'=2,'c'=2,'z'=8,'yh'=2,'yl'=2,'x'=2] {'h','c','yh','yl','x'}, dimensions={0} | all-to-all | bytes 1572864 | tf_op jit(solution)/shard_map/all_to_all | solution.py:39
  182.6 0.8 shard_map.109
  (49 shorter events, 0.5 us)
Async XLA Ops:
  3.4 29.5 %collective-permute-start.1 = (bf16[128,3072]{1,0:T(8,128)(2,1)}, bf16[128,3072]{1,0:T(8,128)(2,1)S(1)}, u32[]{:S(2)}, u32[]{:S(2)}) collective-permute-start(bf16[128,3072]{1,0:T(8,128)(2,1)} %shard_map.105), channel_id=1, source_target_pairs={{0,0},{1,64},{64,1},{65,65},{2,2},{3,66},{66,3},{67,67},{4,4},{5,6... | collective-permute-start | bytes 2359304 | tf_op jit(solution)/shard_map/ppermute | solution.py:51
  9.3 14.4 %all-to-all-start = ((bf16[16,32,128]{2,1,0:T(8,128)(2,1)}), bf16[16,32,128]{2,1,0:T(8,128)(2,1)S(1)}, u32[]{:S(2)}, u32[]{:S(2)}) async-start(bf16[16,32,128]{2,1,0:T(8,128)(2,1)} %shard_map.102), calls=%async_computation | async-start | bytes 262144 | tf_op jit(solution)/shard_map/all_to_all | solution.py:39
  18.6 14.5 %collective-permute-start = (bf16[128,3072]{1,0:T(8,128)(2,1)}, bf16[128,3072]{1,0:T(8,128)(2,1)S(1)}, u32[]{:S(2)}, u32[]{:S(2)}) collective-permute-start(bf16[128,3072]{1,0:T(8,128)(2,1)} %shard_map.104), channel_id=1, source_target_pairs={{0,0},{1,64},{64,1},{65,65},{2,2},{3,66},{66,3},{67,67},{4,4},{5,6... | collective-permute-start | bytes 2359304 | tf_op jit(solution)/shard_map/ppermute | solution.py:51
  23.8 9.1 %copy-start.11 = (bf16[16,32,128]{2,1,0:T(8,128)(2,1)}, bf16[16,32,128]{2,1,0:T(8,128)(2,1)S(1)}, u32[]{:S(2)}) copy-start(bf16[16,32,128]{2,1,0:T(8,128)(2,1)S(1)} %all-to-all-done) | copy-start | bytes 393220
  24.7 26.1 %all-to-all-start.1 = ((bf16[8,256,128]{2,1,0:T(8,128)(2,1)}), bf16[8,256,128]{2,1,0:T(8,128)(2,1)S(1)}, u32[]{:S(2)}, u32[]{:S(2)}) async-start(bf16[8,256,128]{2,1,0:T(8,128)(2,1)} %broadcast_select_fusion), calls=%async_computation.1 | async-start | bytes 1048576 | tf_op jit(solution)/shard_map/all_to_all | solution.py:39
  32.9 17.9 %copy-start = (bf16[128,3072]{1,0:T(8,128)(2,1)}, bf16[128,3072]{1,0:T(8,128)(2,1)S(1)}, u32[]{:S(2)}) copy-start(bf16[128,3072]{1,0:T(8,128)(2,1)S(1)} %collective-permute-done.1.refs_1_) | copy-start | bytes 2359300
  34.2 28.5 %collective-permute-start.2 = (bf16[256,2304]{1,0:T(8,128)(2,1)}, bf16[256,2304]{1,0:T(8,128)(2,1)}, u32[]{:S(2)}, u32[]{:S(2)}) collective-permute-start(bf16[256,2304]{1,0:T(8,128)(2,1)} %pad_maximum_fusion), channel_id=1, source_target_pairs={{0,2},{2,4},{4,6},{6,0},{1,3},{3,5},{5,7},{7,1},{8,10},{10,12},{12... | collective-permute-start | bytes 3538952 | tf_op jit(solution)/shard_map/ppermute | solution.py:31
  35.7 28.4 %collective-permute-start.4 = (bf16[256,2304]{1,0:T(8,128)(2,1)}, bf16[256,2304]{1,0:T(8,128)(2,1)}, u32[]{:S(2)}, u32[]{:S(2)}) collective-permute-start(bf16[256,2304]{1,0:T(8,128)(2,1)} %pad_maximum_fusion.1), channel_id=1, source_target_pairs={{0,6},{2,0},{4,2},{6,4},{1,7},{3,1},{5,3},{7,5},{8,14},{10,8},{12,... | collective-permute-start | bytes 3538952 | tf_op jit(solution)/shard_map/ppermute | solution.py:31
  50.9 1.8 slice-start
  50.9 1.8 slice-start.1
  50.9 5.0 %copy-start.2 = (f32[1,32,1024]{2,1,0:T(8,128)S(1)}, f32[1,32,1024]{2,1,0:T(8,128)}, u32[]{:S(2)}) copy-start(f32[1,32,1024]{2,1,0:T(8,128)} %first.3) | copy-start | bytes 393220
  50.9 5.0 %copy-start.3 = (f32[1,32,1024]{2,1,0:T(8,128)S(1)}, f32[1,32,1024]{2,1,0:T(8,128)}, u32[]{:S(2)}) copy-start(f32[1,32,1024]{2,1,0:T(8,128)} %second.3) | copy-start | bytes 393220
  51.0 5.0 %copy-start.6 = (s32[1,64]{1,0:T(1,128)S(1)}, s32[1,64]{1,0:T(1,128)}, u32[]{:S(2)}) copy-start(s32[1,64]{1,0:T(1,128)} %lengths.5) | copy-start | bytes 772
  51.0 20.2 %collective-permute-start.6 = (bf16[128,3072]{1,0:T(8,128)(2,1)S(1)}, bf16[128,3072]{1,0:T(8,128)(2,1)}, u32[]{:S(2)}, u32[]{:S(2)}) collective-permute-start(bf16[128,3072]{1,0:T(8,128)(2,1)S(1)} %collective-permute-done.refs_0_), channel_id=1, source_target_pairs={{0,64},{64,0},{1,65},{65,1},{2,66},{66,2},{3,67},{67,3},{4,68},{68... | collective-permute-start | bytes 2359304 | tf_op jit(solution)/shard_map/ppermute | solution.py:31
  52.4 17.0 %copy-start.1 = (bf16[128,3072]{1,0:T(8,128)(2,1)S(1)}, bf16[128,3072]{1,0:T(8,128)(2,1)}, u32[]{:S(2)}) copy-start(bf16[128,3072]{1,0:T(8,128)(2,1)} %copy-done) | copy-start | bytes 2359300
  52.4 17.0 %collective-permute-start.8 = (bf16[128,2304]{1,0:T(8,128)(2,1)}, bf16[128,2304]{1,0:T(8,128)(2,1)S(1)}, u32[]{:S(2)}, u32[]{:S(2)}) collective-permute-start(bf16[128,2304]{1,0:T(8,128)(2,1)} %pad_maximum_fusion.2), channel_id=1, source_target_pairs={{0,8},{8,16},{16,24},{24,32},{32,40},{40,48},{48,56},{56,0},{1,9},... | collective-permute-start | bytes 1769480 | tf_op jit(solution)/shard_map/ppermute | solution.py:31
  53.5 17.5 %collective-permute-start.9 = (bf16[128,2304]{1,0:T(8,128)(2,1)}, bf16[128,2304]{1,0:T(8,128)(2,1)S(1)}, u32[]{:S(2)}, u32[]{:S(2)}) collective-permute-start(bf16[128,2304]{1,0:T(8,128)(2,1)} %pad_maximum_fusion.3), channel_id=1, source_target_pairs={{0,56},{8,0},{16,8},{24,16},{32,24},{40,32},{48,40},{56,48},{1,57}... | collective-permute-start | bytes 1769480 | tf_op jit(solution)/shard_map/ppermute | solution.py:31
  57.6 11.8 %all-to-all-start.2 = ((bf16[16,80,128]{2,1,0:T(8,128)(2,1)}), bf16[16,80,128]{2,1,0:T(8,128)(2,1)}, u32[]{:S(2)}, u32[]{:S(2)}) async-start(bf16[16,80,128]{2,1,0:T(8,128)(2,1)} %shard_map.103), calls=%async_computation.2 | async-start | bytes 655360 | tf_op jit(solution)/shard_map/all_to_all | solution.py:39
  62.7 16.8 %collective-permute-start.3 = (bf16[256,2304]{1,0:T(8,128)(2,1)}, bf16[256,2304]{1,0:T(8,128)(2,1)}, u32[]{:S(2)}, u32[]{:S(2)}) collective-permute-start(bf16[256,2304]{1,0:T(8,128)(2,1)} %collective-permute-done.2.refs_0_.refs_8_), channel_id=1, source_target_pairs={{0,64},{64,0},{1,65},{65,1},{2,66},{66,2},{3,67},{67,3},{4,68},{68... | collective-permute-start | bytes 3538952 | tf_op jit(solution)/shard_map/ppermute | solution.py:31
  64.1 15.4 %collective-permute-start.5 = (bf16[256,2304]{1,0:T(8,128)(2,1)}, bf16[256,2304]{1,0:T(8,128)(2,1)}, u32[]{:S(2)}, u32[]{:S(2)}) collective-permute-start(bf16[256,2304]{1,0:T(8,128)(2,1)} %collective-permute-done.4.refs_2_.refs_10_), channel_id=1, source_target_pairs={{0,64},{64,0},{1,65},{65,1},{2,66},{66,2},{3,67},{67,3},{4,68},{68... | collective-permute-start | bytes 3538952 | tf_op jit(solution)/shard_map/ppermute | solution.py:31
  69.4 3.6 %collective-permute-start.7 = (bf16[128,3072]{1,0:T(8,128)(2,1)S(1)}, bf16[128,3072]{1,0:T(8,128)(2,1)}, u32[]{:S(2)}, u32[]{:S(2)}) collective-permute-start(bf16[128,3072]{1,0:T(8,128)(2,1)S(1)} %copy-done.1), channel_id=1, source_target_pairs={{0,64},{64,0},{1,65},{65,1},{2,66},{66,2},{3,67},{67,3},{4,68},{68... | collective-permute-start | bytes 2359304 | tf_op jit(solution)/shard_map/ppermute | solution.py:31
  71.0 2.9 %collective-permute-start.10 = (bf16[128,2304]{1,0:T(8,128)(2,1)S(1)}, bf16[128,2304]{1,0:T(8,128)(2,1)}, u32[]{:S(2)}, u32[]{:S(2)}) collective-permute-start(bf16[128,2304]{1,0:T(8,128)(2,1)S(1)} %collective-permute-done.8.refs_4_), channel_id=1, source_target_pairs={{0,64},{64,0},{1,65},{65,1},{2,66},{66,2},{3,67},{67,3},{4,68},{68... | collective-permute-start | bytes 1769480 | tf_op jit(solution)/shard_map/ppermute | solution.py:31
  71.1 3.6 %collective-permute-start.11 = (bf16[128,2304]{1,0:T(8,128)(2,1)S(1)}, bf16[128,2304]{1,0:T(8,128)(2,1)}, u32[]{:S(2)}, u32[]{:S(2)}) collective-permute-start(bf16[128,2304]{1,0:T(8,128)(2,1)S(1)} %collective-permute-done.9.refs_5_), channel_id=1, source_target_pairs={{0,64},{64,0},{1,65},{65,1},{2,66},{66,2},{3,67},{67,3},{4,68},{68... | collective-permute-start | bytes 1769480 | tf_op jit(solution)/shard_map/ppermute | solution.py:31
  85.3 22.6 %all-to-all-start.3 = ((bf16[8,256,128]{2,1,0:T(8,128)(2,1)}), bf16[8,256,128]{2,1,0:T(8,128)(2,1)S(1)}, u32[]{:S(2)}, u32[]{:S(2)}) async-start(bf16[8,256,128]{2,1,0:T(8,128)(2,1)} %shard_map.107), calls=%async_computation.3 | async-start | bytes 1048576 | tf_op jit(solution)/shard_map/all_to_all | solution.py:264
  108.0 1.2 copy-start.7
  131.3 14.2 %copy-start.8 = (f32[256,128]{1,0:T(8,128)S(1)}, f32[256,128]{1,0:T(8,128)}, u32[]{:S(2)}) copy-start(f32[256,128]{1,0:T(8,128)} %copy-done.7) | copy-start | bytes 393220
  141.1 19.7 %copy-start.9 = (f32[8,32,128]{2,1,0:T(8,128)S(1)}, f32[8,32,128]{2,1,0:T(8,128)}, u32[]{:S(2)}) copy-start(f32[8,32,128]{2,1,0:T(8,128)} %get-tuple-element.22) | copy-start | bytes 393220
  141.1 19.7 %copy-start.10 = (f32[8,32,128]{2,1,0:T(8,128)S(1)}, f32[8,32,128]{2,1,0:T(8,128)}, u32[]{:S(2)}) copy-start(f32[8,32,128]{2,1,0:T(8,128)} %get-tuple-element.23) | copy-start | bytes 393220
  141.1 19.7 %copy-start.12 = (bf16[16,32,128]{2,1,0:T(8,128)(2,1)S(1)}, bf16[16,32,128]{2,1,0:T(8,128)(2,1)}, u32[]{:S(2)}) copy-start(bf16[16,32,128]{2,1,0:T(8,128)(2,1)} %copy-done.11) | copy-start | bytes 393220
  141.2 19.6 %all-to-all-start.5 = ((bf16[8,256,128]{2,1,0:T(8,128)(2,1)}), bf16[8,256,128]{2,1,0:T(8,128)(2,1)S(1)}, u32[]{:S(2)}, u32[]{:S(2)}) async-start(bf16[8,256,128]{2,1,0:T(8,128)(2,1)} %shard_map.108), calls=%async_computation.5 | async-start | bytes 1048576 | tf_op jit(solution)/shard_map/all_to_all | solution.py:264
  161.1 21.5 %copy-start.4 = (f32[32,256]{1,0:T(8,128)S(1)}, f32[32,256]{1,0:T(8,128)}, u32[]{:S(2)}) copy-start(f32[32,256]{1,0:T(8,128)} %param.17) | copy-start | bytes 98308
  161.1 21.5 %copy-start.5 = (f32[32,256]{1,0:T(8,128)S(1)}, f32[32,256]{1,0:T(8,128)}, u32[]{:S(2)}) copy-start(f32[32,256]{1,0:T(8,128)} %mom.1) | copy-start | bytes 98308
